TPU v7x, 32 devices: a whole 2x2x4 slice. The times are simulated.
32 devices in a mesh: group: 2 (over x), tm: 4 (over y, core), tensor: 4 (over z).
Axes of the slice: x: 2, y: 2, z: 4, core: 2. Of those that a mesh axis runs over, the one named last changes fastest.
Arguments:
- states: bfloat16 [4, 1536, 5120], P('tm', 'group'), parts along dimension 1, may hold values from -60 to 60
- timesteps: int32 [4], P('tm'), may hold values from 0 to 999
- step_sizes: float32 [4], P('tm'), may hold values from 0.05 to 0.5
- mod_scale: float32 [5120], replicated, may hold values from -3 to 3
- mod_gate: float32 [5120], P('tensor'), may hold values from -3 to 3
- w_query: bfloat16 [5120, 3072], P('tm', 'tensor'), may hold values from -1 to 1
- w_key: bfloat16 [5120, 3072], P('tm', 'tensor'), may hold values from -1 to 1
- w_value: bfloat16 [5120, 3072], P('tm', 'tensor'), may hold values from -0.078125 to 0.078125
- query_gain: float32 [3072], P('tensor'), may hold values from 0.8 to 4.2
- key_gain: float32 [3072], P('tensor'), may hold values from 0.8 to 4.2
- w_out: bfloat16 [3072, 5120], P('tensor', 'tm'), may hold values from -0.109375 to 0.109375
Outputs:
- next_states: float32 [4, 1536, 5120], P('tm', 'group', 'tensor'), parts along dimension 1
- errors: float32 [2, 4], P('group', 'tm'), parts along dimension 0
There are 2 independent parts, one for each index of `group`. A program takes and returns all parts, laid end to end along the dimension named above; an argument that names none is the same for every part. Nothing has to cross between parts.
All inputs are finite; a program needn't handle non-finite values.
Results may differ from a plain program's by a relative error of at most 0.0015.
Values may be sent and summed in bfloat16 or wider, within the bound.
No kernel may reach another device: no remote copies, remote signals or barrier semaphores. Data moves between devices by JAX's collectives and lax.ppermute only.
A program may use at most 128 MiB of HBM per device.

v0:
```python
import math

import jax
import jax.numpy as jnp
from jax import lax
from jax.sharding import PartitionSpec as P

HD = 128


def spread(block, axis, holder):
    block = jnp.where(lax.axis_index(axis) == holder, block, jnp.zeros_like(block))
    return lax.psum(block, axis)


def from_behind(array, axis, by):
    devices = lax.axis_size(axis)
    pairs = [(i, i + by) for i in range(devices) if 0 <= i + by < devices]
    return lax.ppermute(array, axis, pairs)


def head_norm(values, gain):
    rows = values.shape[0]
    count = values.shape[1] // HD
    split = values.reshape(rows, count, HD)
    normed = split * lax.rsqrt(jnp.mean(split * split, axis=-1, keepdims=True) + 1e-06)
    return (normed * gain.reshape(count, HD)).astype(jnp.bfloat16)


def body(
    states,
    timesteps,
    step_sizes,
    mod_scale,
    mod_gate,
    w_query,
    w_key,
    w_value,
    query_gain,
    key_gain,
    w_out,
):
    latent = states[0]
    rows, width = latent.shape
    stamp = timesteps[0].astype(jnp.float32)
    omega = jnp.exp(-math.log(10000.0) * jnp.arange(width).astype(jnp.float32) / width)
    values = latent.astype(jnp.float32)
    normed = values * lax.rsqrt(jnp.mean(values * values, axis=-1, keepdims=True) + 1e-06)
    hidden = (normed * (1.0 + mod_scale * jnp.cos(stamp * omega))).astype(jnp.bfloat16)
    local_heads = w_query.shape[1]
    query = jnp.dot(
        hidden,
        lax.all_gather(w_query, "tm", axis=0, tiled=True),
        preferred_element_type=jnp.float32,
    )
    keys = jnp.dot(
        hidden, lax.all_gather(w_key, "tm", axis=0, tiled=True), preferred_element_type=jnp.float32
    )
    value = jnp.dot(
        hidden,
        lax.all_gather(w_value, "tm", axis=0, tiled=True),
        preferred_element_type=jnp.float32,
    )
    count = local_heads // HD
    q_norm = head_norm(query, query_gain)
    k_norm = head_norm(keys, key_gain)
    v_heads = value.astype(jnp.bfloat16).reshape(rows, count, HD)
    scores = jnp.einsum(
        "qhd,khd->hqk", q_norm, k_norm, preferred_element_type=jnp.float32
    ) / math.sqrt(HD)
    probs = jax.nn.softmax(scores, axis=-1).astype(jnp.bfloat16)
    attended = jnp.einsum("hqk,khd->qhd", probs, v_heads, preferred_element_type=jnp.float32)
    attended = attended.astype(jnp.bfloat16).reshape(rows, local_heads)
    share = mod_gate.shape[0]
    offset = lax.axis_index("tensor") * share
    partial_out = jnp.dot(
        attended,
        lax.all_gather(w_out, "tm", axis=1, tiled=True),
        preferred_element_type=jnp.float32,
    )
    projected = lax.psum_scatter(
        partial_out.astype(jnp.bfloat16), "tensor", scatter_dimension=1, tiled=True
    ).astype(jnp.float32)
    positions = (offset + jnp.arange(share)).astype(jnp.float32)
    omega_share = jnp.exp(-math.log(10000.0) * positions / width)
    gate = 1.0 + mod_gate * jnp.sin(stamp * omega_share)
    term = step_sizes[0] * gate * projected
    own_slice = lax.dynamic_slice_in_dim(latent, offset, share, 1)
    own_start = own_slice.astype(jnp.float32)
    base_state = spread(own_slice, "tm", 0).astype(jnp.float32)
    running = term
    for level in range(lax.axis_size("tm").bit_length() - 1):
        running = running + from_behind(running, "tm", 1 << level)
    before = running - term
    predicted = base_state + before
    next_share = predicted + term
    gap = predicted - own_start
    squared = lax.psum(jnp.sum(gap * gap), "tensor")
    errors = (squared / (rows * width)).reshape(1, 1)
    return (next_share[None], errors)


def solution(mesh):
    placed = (
        P("tm", "group", None),
        P("tm"),
        P("tm"),
        P(),
        P("tensor"),
        P("tm", "tensor"),
        P("tm", "tensor"),
        P("tm", "tensor"),
        P("tensor"),
        P("tensor"),
        P("tensor", "tm"),
    )
    return jax.shard_map(
        body,
        mesh=mesh,
        in_specs=placed,
        out_specs=(P("tm", "group", "tensor"), P("group", "tm")),
        check_vma=False,
    )
```

profile of v0, /device:TPU:12, one launch (start us, length us, event | category | flops | bytes accessed | tf_op | source)
XLA Modules:
  0.0 582.0 jit_solution(6055403932991183505)
XLA Ops:
  10.7 4.8 fusion.3
  15.6 49.5 %all-gather.7.cloned.1.call-done = bf16[5120,768]{1,0:T(8,128)(2,1)} async-done(((bf16[1280,768]{1,0:T(8,128)(2,1)}), bf16[5120,768]{1,0:T(8,128)(2,1)}) %all-gather.7.cloned.1.call-update) | async-done | bytes 7864336 | tf_op jit(solution)/shard_map/all_gather | solution.py:53
  65.1 10.6 %copy.13 = bf16[768,5120]{1,0:T(8,128)(2,1)} copy(bf16[768,5120]{0,1:T(8,128)(2,1)} %bitcast.51) | data formatting | bytes 15728640 | tf_op jit(solution)/shard_map/dot_general | solution.py:51
  75.7 46.3 %all-gather.9.cloned.1.call-done = bf16[5120,768]{1,0:T(8,128)(2,1)} async-done(((bf16[1280,768]{1,0:T(8,128)(2,1)}), bf16[5120,768]{1,0:T(8,128)(2,1)}) %all-gather.9.cloned.1.call-update) | async-done | bytes 7864336 | tf_op jit(solution)/shard_map/all_gather | solution.py:57
  122.0 10.4 %copy.14 = bf16[768,5120]{1,0:T(8,128)(2,1)} copy(bf16[768,5120]{0,1:T(8,128)(2,1)} %bitcast.52) | data formatting | bytes 15728640 | tf_op jit(solution)/shard_map/dot_general | solution.py:56
  132.4 13.2 %multiply_reduce_fusion.2 = (f32[768,6]{0,1:T(8,128)S(1)}, f32[768,6,128]{0,2,1:T(8,128)S(1)}) fusion(bf16[6,128,5120]{2,1,0:T(8,128)(2,1)} %bitcast.53, bf16[1,768,5120]{2,1,0:T(8,128)(2,1)} %param.11, f32[5120]{0:T(1024)S(1)} %multiply_add_fusion, f32[768]{0:T(1024)S(1)} %add_rsqrt_fusion.2), kind=kOutput, calls=%fused_computation.30 | convolution fusion | flops 6056701440 | bytes 18129920 | tf_op jit(solution)/shard_map/dot_general | solution.py:51
  145.7 11.1 %multiply_reduce_fusion.1 = (f32[768,6]{0,1:T(8,128)S(1)}, f32[768,6,128]{0,2,1:T(8,128)}) fusion(bf16[6,128,5120]{2,1,0:T(8,128)(2,1)S(1)} %bitcast.54, bf16[1,768,5120]{2,1,0:T(8,128)(2,1)} %param.11, f32[5120]{0:T(1024)S(1)} %multiply_add_fusion, f32[768]{0:T(1024)S(1)} %add_rsqrt_fusion.2), kind=kOutput, calls=%fused_computation.28 | convolution fusion | flops 6056701440 | bytes 18129920 | tf_op jit(solution)/shard_map/dot_general | solution.py:56
  156.8 11.1 %fusion.33 = (f32[6,768]{1,0:T(8,128)S(1)}, f32[6,768,768]{1,2,0:T(8,128)}) fusion(f32[768,6,128]{0,2,1:T(8,128)S(1)} %get-tuple-element.5, f32[6,128]{1,0:T(8,128)S(1)} %bitcast.55, f32[768,6]{0,1:T(8,128)S(1)} %get-tuple-element.11, f32[768,6,128]{0,2,1:T(8,128)} %get-tuple-element.7, f32[6,128]{1,0:T(8,128)S(1)} %bitcast.56, ...), kind=kOutput, calls=%fused_computation.45 | convolution fusion | flops 920126208 | bytes 18935808 | tf_op jit(solution)/shard_map/sub | solution.py:71
  167.9 11.0 %all-gather.5.cloned.1.call-done = bf16[5120,768]{1,0:T(8,128)(2,1)} async-done(((bf16[1280,768]{1,0:T(8,128)(2,1)}), bf16[5120,768]{1,0:T(8,128)(2,1)}) %all-gather.5.cloned.1.call-update) | async-done | bytes 7864336 | tf_op jit(solution)/shard_map/all_gather | solution.py:61
  178.9 11.3 %fusion.28 = bf16[768,768]{0,1:T(8,128)(2,1)S(1)} fusion(bf16[5120,768]{1,0:T(8,128)(2,1)} %all-gather.5.cloned.1.call-done, bf16[1,768,5120]{2,1,0:T(8,128)(2,1)} %param.11, f32[5120]{0:T(1024)S(1)} %multiply_add_fusion, f32[768]{0:T(1024)S(1)} %add_rsqrt_fusion.2), kind=kOutput, calls=%fused_computation.37 | convolution fusion | flops 6056116224 | bytes 16931840 | tf_op jit(solution)/shard_map/dot_general | solution.py:59
  190.3 7.6 %fusion.27 = bf16[6,128,768]{2,1,0:T(8,128)(2,1)S(1)} fusion(bf16[768,6,128]{0,2,1:T(8,128)(2,1)S(1)} %bitcast.58, f32[6,768,768]{1,2,0:T(8,128)} %get-tuple-element.9, f32[6,768]{1,0:T(8,128)S(1)} %get-tuple-element.8), kind=kOutput, calls=%fused_computation.36 | convolution fusion | flops 913637376 | bytes 16533504 | tf_op jit(solution)/shard_map/hqk,khd->qhd/dot_general | solution.py:72
  197.9 37.8 %all-gather.11.cloned.1.call-done = bf16[768,5120]{1,0:T(8,128)(2,1)} async-done(((bf16[768,1280]{1,0:T(8,128)(2,1)}), bf16[768,5120]{1,0:T(8,128)(2,1)}) %all-gather.11.cloned.1.call-update) | async-done | bytes 7864336 | tf_op jit(solution)/shard_map/all_gather | solution.py:78
  235.7 11.8 %convolution_convert_fusion = bf16[768,5120]{1,0:T(8,128)(2,1)} fusion(bf16[768,768]{0,1:T(8,128)(2,1)S(1)} %bitcast.57, bf16[768,5120]{1,0:T(8,128)(2,1)} %all-gather.11.cloned.1.call-done), kind=kOutput, calls=%fused_computation.14 | convolution fusion | flops 6043729920 | bytes 16908288 | tf_op jit(solution)/shard_map/dot_general | solution.py:76
  248.3 136.5 %reduce-scatter.2.cloned.1.call-done = bf16[768,1280]{1,0:T(8,128)(2,1)} async-done(((bf16[768,5120]{1,0:T(8,128)(2,1)}), bf16[768,1280]{1,0:T(8,128)(2,1)}) %reduce-scatter.2.cloned.1.call-update) | async-done | bytes 1966096 | tf_op jit(solution)/shard_map/reduce_scatter | solution.py:81
  384.8 1.9 convert_multiply_fusion.1
  386.7 1.9 collective-permute-start
  388.7 45.1 %collective-permute-done = f32[768,1280]{1,0:T(8,128)S(1)} collective-permute-done((f32[768,1280]{1,0:T(8,128)S(1)}, f32[768,1280]{1,0:T(8,128)S(1)}, u32[]{:S(2)}, u32[]{:S(2)}) %collective-permute-start) | collective-permute-done | bytes 3932192 | tf_op jit(solution)/shard_map/ppermute | solution.py:19
  433.8 2.7 fusion.24
  436.8 1.3 collective-permute-start.1
  438.1 3.1 select_bitcast_fusion
  441.3 83.9 %all-reduce.2.cloned.1.call-done = bf16[768,1280]{1,0:T(8,128)(2,1)} async-done(((bf16[768,1280]{1,0:T(8,128)(2,1)}), bf16[768,1280]{1,0:T(8,128)(2,1)}) %all-reduce.2.cloned.1.call-update) | async-done | bytes 1966096 | tf_op jit(solution)/shard_map/psum | solution.py:13
  525.3 29.6 %collective-permute-done.1 = f32[768,1280]{1,0:T(8,128)} collective-permute-done((f32[768,1280]{1,0:T(8,128)}, f32[768,1280]{1,0:T(8,128)}, u32[]{:S(2)}, u32[]{:S(2)}) %collective-permute-start.1) | collective-permute-done | bytes 3932192 | tf_op jit(solution)/shard_map/ppermute | solution.py:19
  554.8 8.5 %fusion.19 = (f32[]{:T(128)}, f32[1,768,1280]{2,1,0:T(8,128)}) fusion(bf16[1,768,5120]{2,1,0:T(8,128)(2,1)} %param.11, s32[]{:T(128)S(6)} %select_n.15, bf16[768,1280]{1,0:T(8,128)(2,1)S(1)} %copy-done, f32[1280]{0:T(1024)S(1)} %add_multiply_fusion, f32[768,1280]{1,0:T(8,128)} %collective-permute-done.1, bf16[768,1280]{1,0:T(8,128)(2,1)} %all-reduce.2.cloned.1.call-done, ...), kind=kLoop, calls=%fused_computation.23 | loop fusion | flops 11796479 | bytes 17699848 | tf_op jit(solution)/shard_map/reduce_sum | solution.py:98
  563.3 10.0 %psum.15 = f32[]{:T(128)} all-reduce(f32[]{:T(128)} %get-tuple-element.2), channel_id=1, replica_groups=mesh['group'=2,'tm'=4,'tensor'=4] {'tensor'}, use_global_device_ids=true, to_apply=%region_8.9 | all-reduce | flops 1 | bytes 8 | tf_op jit(solution)/shard_map/psum | solution.py:98
  (30 shorter events, 3.5 us)
Async XLA Ops:
  7.2 57.9 %all-gather.7.cloned.1.call-start = ((), (), s32[]{:S(2)}) async-start(), calls=%async_computation.3 | async-start | bytes 9830400 | tf_op jit(solution)/shard_map/all_gather | solution.py:53
  7.9 114.1 %all-gather.9.cloned.1.call-start = ((), (), s32[]{:S(2)}) async-start(), calls=%async_computation.4 | async-start | bytes 9830400 | tf_op jit(solution)/shard_map/all_gather | solution.py:57
  8.6 170.3 %all-gather.5.cloned.1.call-start = ((), (), s32[]{:S(2)}) async-start(), calls=%async_computation.2 | async-start | bytes 9830400 | tf_op jit(solution)/shard_map/all_gather | solution.py:61
  9.4 226.3 %all-gather.11.cloned.1.call-start = ((), (), s32[]{:S(2)}) async-start(), calls=%async_computation.5 | async-start | bytes 9830400 | tf_op jit(solution)/shard_map/all_gather | solution.py:78
  10.0 374.8 %reduce-scatter.2.cloned.1.call-start = ((), (), s32[]{:S(2)}) async-start(), calls=%async_computation.6 | async-start | bytes 9830400 | tf_op jit(solution)/shard_map/reduce_scatter | solution.py:81
  10.7 4.9 copy-start.3
  132.4 13.2 %copy-start.2 = (bf16[768,5120]{1,0:T(8,128)(2,1)S(1)}, bf16[768,5120]{1,0:T(8,128)(2,1)}, u32[]{:S(2)}) copy-start(bf16[768,5120]{1,0:T(8,128)(2,1)} %copy.14) | copy-start | bytes 23592964
  145.7 11.1 %copy-start.5 = (f32[768]{0:T(1024)S(1)}, f32[768]{0:T(1024)}, u32[]{:S(2)}) copy-start(f32[768]{0:T(1024)} %param.19) | copy-start | bytes 9220
  145.7 11.1 %copy-start.6 = (f32[768]{0:T(1024)S(1)}, f32[768]{0:T(1024)}, u32[]{:S(2)}) copy-start(f32[768]{0:T(1024)} %param.20) | copy-start | bytes 9220
  247.4 0.7 copy-start.4
  247.5 277.8 %all-reduce.2.cloned.1.call-start = ((), (), s32[]{:S(2)}) async-start(), calls=%async_computation.1 | async-start | bytes 3932160 | tf_op jit(solution)/shard_map/psum | solution.py:13
  384.8 49.0 %copy-start = (bf16[768,1280]{1,0:T(8,128)(2,1)S(1)}, bf16[768,1280]{1,0:T(8,128)(2,1)}, u32[]{:S(2)}) copy-start(bf16[768,1280]{1,0:T(8,128)(2,1)} %reduce-scatter.2.cloned.1.call-done) | copy-start | bytes 5898244
  386.7 47.0 %collective-permute-start = (f32[768,1280]{1,0:T(8,128)S(1)}, f32[768,1280]{1,0:T(8,128)S(1)}, u32[]{:S(2)}, u32[]{:S(2)}) collective-permute-start(f32[768,1280]{1,0:T(8,128)S(1)} %convert_multiply_fusion.1), channel_id=1, source_target_pairs={{0,4},{4,8},{8,12},{1,5},{5,9},{9,13},{2,6},{6,10},{10,14},{3,7},{... | collective-permute-start | bytes 11796488 | tf_op jit(solution)/shard_map/ppermute | solution.py:19
  433.8 3.1 copy-start.1
  436.8 118.0 %collective-permute-start.1 = (f32[768,1280]{1,0:T(8,128)}, f32[768,1280]{1,0:T(8,128)}, u32[]{:S(2)}, u32[]{:S(2)}) collective-permute-start(f32[768,1280]{1,0:T(8,128)} %fusion.24), channel_id=1, source_target_pairs={{0,8},{4,12},{1,9},{5,13},{2,10},{6,14},{3,11},{7,15},{16,24},{20,... | collective-permute-start | bytes 11796488 | tf_op jit(solution)/shard_map/ppermute | solution.py:19
Sparse Core Ops, SparseCore 0:
  9.6 55.4 all-gather.6
  66.7 55.3 all-gather.8
  123.6 55.3 all-gather.4
  180.3 55.3 all-gather.10
  247.6 137.1 reduce-scatter.1
  441.4 83.7 all-reduce.1
where the time goes:
time: 585 us; the launch traced here: 582 us
  waiting for transfers between devices  442 us (76%)
  matrix products  66.1 us (11%)
  local copies, waits for them, and re-layouts  21.5 us (4%)
  other arithmetic  21.3 us (4%)
  between operations  17.3 us (3%)
  blocking collectives  10 us (2%)
    reduce_scatter x1, waiting for transfers between devices, body(): lax.psum_scatter(partial_out.astype(jnp.bfloat16), 'tensor', scatter_dime...  137 us
    psum x1, waiting for transfers between devices, spread(): return lax.psum(block, axis)  83.9 us
    ppermute x2, waiting for transfers between devices, from_behind(): return lax.ppermute(array, axis, pairs)  74.6 us
    all_gather x1, waiting for transfers between devices, body(): lax.all_gather(w_query, 'tm', axis=0, tiled=True)  49.5 us
    all_gather x1, waiting for transfers between devices, body(): lax.all_gather(w_key, 'tm', axis=0, tiled=True)  46.3 us
    all_gather x1, waiting for transfers between devices, body(): lax.all_gather(w_out, 'tm', axis=1, tiled=True)  37.8 us
    dot_general x1, matrix products, body(): jnp.dot(hidden, lax.all_gather(w_query, 'tm', axis=0, tiled=True), prefer...  13.2 us
    dot_general x1, matrix products, body(): jnp.dot(attended, lax.all_gather(w_out, 'tm', axis=1, tiled=True), prefer...  11.8 us
  transfers between devices with their start and end apart: 8, of which 8 were waited for; matrix products, arithmetic and copies ran while one was open for 14% of the time, Pallas kernels for 0%

commit v1 on v0

v1 whole, which is shorter than its diff:
```python
import functools
import math

import jax
import jax.numpy as jnp
from jax import lax
from jax.experimental import pallas as pl
from jax.experimental.pallas import tpu as pltpu
from jax.sharding import PartitionSpec as P

HD = 128
CHUNK_HEADS = 2
VMEM_LIMIT = 56 * 2**20
ANY = pl.BlockSpec(memory_space=pl.ANY)
SMEM = pl.BlockSpec(memory_space=pltpu.SMEM)
VMEM = pl.BlockSpec(memory_space=pltpu.VMEM)


def spread(block, axis, holder):
    block = jnp.where(lax.axis_index(axis) == holder, block, jnp.zeros_like(block))
    return lax.psum(block, axis)


def from_behind(array, axis, by):
    devices = lax.axis_size(axis)
    pairs = [(i, i + by) for i in range(devices) if 0 <= i + by < devices]
    return lax.ppermute(array, axis, pairs)


def head_norm(values, gain):
    rows = values.shape[0]
    count = values.shape[1] // HD
    split = values.reshape(rows, count, HD)
    normed = split * lax.rsqrt(jnp.mean(split * split, axis=-1, keepdims=True) + 1e-06)
    return (normed * gain.reshape(count, HD)).astype(jnp.bfloat16)


def make_hidden(latent, stamp, mod_scale):
    width = latent.shape[1]
    omega = jnp.exp(-math.log(10000.0) * jnp.arange(width).astype(jnp.float32) / width)
    values = latent.astype(jnp.float32)
    normed = values * lax.rsqrt(jnp.mean(values * values, axis=-1, keepdims=True) + 1e-06)
    return (normed * (1.0 + mod_scale * jnp.cos(stamp * omega))).astype(jnp.bfloat16)


def make_gate(stamp, mod_gate, width):
    share = mod_gate.shape[0]
    offset = lax.axis_index("tensor") * share
    positions = (offset + jnp.arange(share)).astype(jnp.float32)
    omega_share = jnp.exp(-math.log(10000.0) * positions / width)
    return 1.0 + mod_gate * jnp.sin(stamp * omega_share)


def general_body(
    states, timesteps, step_sizes, mod_scale, mod_gate, w_query, w_key, w_value, query_gain, key_gain, w_out
):
    latent = states[0]
    rows, width = latent.shape
    stamp = timesteps[0].astype(jnp.float32)
    hidden = make_hidden(latent, stamp, mod_scale)
    local_heads = w_query.shape[1]

    def project(weight):
        whole = lax.all_gather(weight, "tm", axis=0, tiled=True)
        return jnp.dot(hidden, whole, preferred_element_type=jnp.float32)

    count = local_heads // HD
    q_norm = head_norm(project(w_query), query_gain)
    k_norm = head_norm(project(w_key), key_gain)
    v_heads = project(w_value).astype(jnp.bfloat16).reshape(rows, count, HD)
    scores = jnp.einsum("qhd,khd->hqk", q_norm, k_norm, preferred_element_type=jnp.float32) / math.sqrt(HD)
    probs = jax.nn.softmax(scores, axis=-1).astype(jnp.bfloat16)
    attended = jnp.einsum("hqk,khd->qhd", probs, v_heads, preferred_element_type=jnp.float32)
    attended = attended.astype(jnp.bfloat16).reshape(rows, local_heads)
    share = mod_gate.shape[0]
    offset = lax.axis_index("tensor") * share
    partial_out = jnp.dot(
        attended,
        lax.all_gather(w_out, "tm", axis=1, tiled=True),
        preferred_element_type=jnp.float32,
    )
    projected = lax.psum_scatter(
        partial_out.astype(jnp.bfloat16), "tensor", scatter_dimension=1, tiled=True
    ).astype(jnp.float32)
    term = step_sizes[0] * make_gate(stamp, mod_gate, width) * projected
    own_slice = lax.dynamic_slice_in_dim(latent, offset, share, 1)
    own_start = own_slice.astype(jnp.float32)
    base_state = spread(own_slice, "tm", 0).astype(jnp.float32)
    running = term
    for level in range((lax.axis_size("tm") - 1).bit_length()):
        running = running + from_behind(running, "tm", 1 << level)
    before = running - term
    predicted = base_state + before
    next_share = predicted + term
    gap = predicted - own_start
    squared = lax.psum(jnp.sum(gap * gap), "tensor")
    errors = (squared / (rows * width)).reshape(1, 1)
    return (next_share[None], errors)


def near_kernel(idx, h_own, h_par, wq, wk, wv, pq, pk, pv, acc):
    wide = wq.shape[1]
    for n, (own, par) in enumerate(((wq, pq), (wk, pk), (wv, pv))):
        acc[0, :, n * wide : (n + 1) * wide] = jnp.dot(
            h_own[...], own[...], preferred_element_type=jnp.float32
        ) + jnp.dot(h_par[...], par[...], preferred_element_type=jnp.float32)


def near_products(hidden, own, partner, tm):
    rows, _ = hidden.shape
    depth, cols = own[0].shape
    wide = CHUNK_HEADS * HD
    chunks = cols // wide
    weight = pl.BlockSpec((depth, wide), lambda j, idx: (0, j))
    return pl.pallas_call(
        near_kernel,
        grid_spec=pltpu.PrefetchScalarGridSpec(
            num_scalar_prefetch=1,
            grid=(chunks,),
            in_specs=[
                pl.BlockSpec((rows, depth), lambda j, idx: (0, idx[0])),
                pl.BlockSpec((rows, depth), lambda j, idx: (0, idx[1])),
            ]
            + [weight] * 6,
            out_specs=pl.BlockSpec((1, rows, 3 * wide), lambda j, idx: (j, 0, 0)),
        ),
        out_shape=jax.ShapeDtypeStruct((chunks, rows, 3 * wide), jnp.float32),
        compiler_params=pltpu.CompilerParams(vmem_limit_bytes=VMEM_LIMIT),
        cost_estimate=pl.CostEstimate(
            flops=12 * rows * depth * cols, bytes_accessed=6 * depth * cols * 2, transcendentals=0
        ),
        name="near_products",
    )(jnp.stack([tm, tm ^ 1]).astype(jnp.int32), hidden, hidden, *own, *partner)


def attend_kernel(chunk, idx, hid, acc, far, far_x, par, par_x, qg, kg, out, hbuf, wbuf, abuf, sems, asem):
    rows = hbuf.shape[0]
    half = far.shape[0]
    wide = CHUNK_HEADS * HD
    pieces = (far, par, far_x, par_x)
    copies = []
    for n, piece in enumerate(pieces):
        at = pl.multiple_of(idx[n], HD)
        copies.append(
            (
                pltpu.make_async_copy(
                    hid.at[:, pl.ds(at, half)], hbuf.at[:, n * half : (n + 1) * half], sems.at[2 * n]
                ),
                pltpu.make_async_copy(piece, wbuf.at[n * half : (n + 1) * half, :], sems.at[2 * n + 1]),
            )
        )
        for copy in copies[-1]:
            copy.start()
    first = pltpu.make_async_copy(acc.at[chunk], abuf, asem)
    first.start()
    for part in range(2):
        for pair in copies[2 * part : 2 * part + 2]:
            for copy in pair:
                copy.wait()
        if part == 0:
            first.wait()
        span = slice(2 * part * half, 2 * (part + 1) * half)
        for n in range(3):
            cols = slice(n * wide, (n + 1) * wide)
            abuf[:, cols] += jnp.dot(hbuf[:, span], wbuf[span, cols], preferred_element_type=jnp.float32)

    def normed(values, gain):
        scale = lax.rsqrt(jnp.mean(values * values, axis=-1, keepdims=True) + 1e-06)
        return (values * scale * gain).astype(jnp.bfloat16)

    block = rows // 3
    for head in range(CHUNK_HEADS):
        cols = slice(head * HD, (head + 1) * HD)
        qn = normed(abuf[:, cols], qg[:, cols])
        kn = normed(abuf[:, wide + head * HD : wide + (head + 1) * HD], kg[:, cols])
        vb = abuf[:, 2 * wide + head * HD : 2 * wide + (head + 1) * HD].astype(jnp.bfloat16)
        for r in range(3):
            scores = lax.dot_general(
                qn[r * block : (r + 1) * block],
                kn,
                (((1,), (1,)), ((), ())),
                preferred_element_type=jnp.float32,
            )
            top = jnp.max(scores, axis=-1, keepdims=True)
            grown = jnp.exp((scores - top) * (1.0 / math.sqrt(HD)))
            probs = grown * (1.0 / jnp.sum(grown, axis=-1, keepdims=True))
            out[r * block : (r + 1) * block, cols] = jnp.dot(
                probs.astype(jnp.bfloat16), vb, preferred_element_type=jnp.float32
            ).astype(jnp.bfloat16)


def attend(chunk, idx, hidden, acc, pieces, qg, kg):
    rows = hidden.shape[0]
    half = pieces[0].shape[0]
    wide = CHUNK_HEADS * HD
    gains = [g.reshape(1, -1)[:, chunk * wide : (chunk + 1) * wide] for g in (qg, kg)]
    return pl.pallas_call(
        functools.partial(attend_kernel, chunk),
        in_specs=[SMEM] + [ANY] * 6 + [VMEM] * 2,
        out_specs=VMEM,
        out_shape=jax.ShapeDtypeStruct((rows, wide), jnp.bfloat16),
        scratch_shapes=[
            pltpu.VMEM((rows, 4 * half), jnp.bfloat16),
            pltpu.VMEM((4 * half, 3 * wide), jnp.bfloat16),
            pltpu.VMEM((rows, 3 * wide), jnp.float32),
            pltpu.SemaphoreType.DMA((8,)),
            pltpu.SemaphoreType.DMA,
        ],
        compiler_params=pltpu.CompilerParams(vmem_limit_bytes=VMEM_LIMIT),
        cost_estimate=pl.CostEstimate(
            flops=2 * rows * 4 * half * 3 * wide * 2, bytes_accessed=12 * 2**20, transcendentals=CHUNK_HEADS * rows * rows
        ),
        name="attend",
    )(idx, hidden, acc, *pieces, *gains)


def out_kernel(devices, chunks, idx, gate, *refs):
    own, refs = refs[:chunks], refs[chunks:]
    right, refs = refs[: (devices - 1) * chunks], refs[(devices - 1) * chunks :]
    left, refs = refs[: (devices - 1) * chunks], refs[(devices - 1) * chunks :]
    held, refs = refs[:devices], refs[devices:]
    held_x, refs = refs[:devices], refs[devices:]
    given, refs = refs[:devices], refs[devices:]
    given_x, refs = refs[:devices], refs[devices:]
    out, att, w, asems, wsems = refs
    wide = own[0].shape[1]
    half = held[0].shape[0]
    z, source, g = idx[0], idx[1], idx[2]
    waits = []
    for d in range(devices):
        here = []
        for j in range(chunks):
            place = att.at[d, :, j * wide : (j + 1) * wide]
            if d == 0:
                pltpu.make_async_copy(own[j], place, asems.at[d * chunks + j]).start()
            else:
                behind = z + d >= devices

                @pl.when(behind)
                def _(d=d, j=j, place=place):
                    pltpu.make_async_copy(
                        right[(devices - d - 1) * chunks + j], place, asems.at[d * chunks + j]
                    ).start()

                @pl.when(jnp.logical_not(behind))
                def _(d=d, j=j, place=place):
                    pltpu.make_async_copy(left[(d - 1) * chunks + j], place, asems.at[d * chunks + j]).start()

            here.append(pltpu.make_async_copy(own[j], place, asems.at[d * chunks + j]))
        for n, (mine, other) in enumerate(((held, given), (held_x, given_x))):
            at = pl.multiple_of((g if n == 0 else 1 - g) * half, 16)
            place = w.at[d, pl.ds(at, half), :]

            @pl.when(source == 1)
            def _(d=d, n=n, place=place, mine=mine):
                pltpu.make_async_copy(mine[d], place, wsems.at[2 * d + n]).start()

            @pl.when(source == 0)
            def _(d=d, n=n, place=place, other=other):
                pltpu.make_async_copy(other[d], place, wsems.at[2 * d + n]).start()

            here.append(pltpu.make_async_copy(mine[d], place, wsems.at[2 * d + n]))
        waits.append(here)
    share = out.shape[1]
    block = 256 if share % 256 == 0 else share
    for d in range(devices):
        for copy in waits[d]:
            copy.wait()
        for n in range(share // block):
            cols = slice(n * block, (n + 1) * block)
            part = (
                jnp.dot(att[d], w[d, :, cols], preferred_element_type=jnp.float32)
                .astype(jnp.bfloat16)
                .astype(jnp.float32)
            )
            if d > 0:
                part = out[:, cols] + part
            if d == devices - 1:
                part = gate[:, cols] * part
            out[:, cols] = part


def out_projection(idx, gate, own, right, left, held, held_x, given, given_x):
    chunks = len(own)
    devices = len(held)
    rows, wide = own[0].shape
    half, share = held[0].shape
    operands = (*own, *right, *left, *held, *held_x, *given, *given_x)
    return pl.pallas_call(
        functools.partial(out_kernel, devices, chunks),
        in_specs=[SMEM, VMEM] + [ANY] * len(operands),
        out_specs=VMEM,
        out_shape=jax.ShapeDtypeStruct((rows, share), jnp.float32),
        scratch_shapes=[
            pltpu.VMEM((devices, rows, chunks * wide), jnp.bfloat16),
            pltpu.VMEM((devices, 2 * half, share), jnp.bfloat16),
            pltpu.SemaphoreType.DMA((devices * chunks,)),
            pltpu.SemaphoreType.DMA((2 * devices,)),
        ],
        compiler_params=pltpu.CompilerParams(vmem_limit_bytes=VMEM_LIMIT),
        cost_estimate=pl.CostEstimate(
            flops=2 * rows * devices * chunks * wide * share * 2, bytes_accessed=18 * 2**20, transcendentals=0
        ),
        name="out_projection",
    )(idx, gate, *operands)


def fast_body(
    states, timesteps, step_sizes, mod_scale, mod_gate, w_query, w_key, w_value, query_gain, key_gain, w_out
):
    latent = states[0]
    rows, width = latent.shape
    stamp = timesteps[0].astype(jnp.float32)
    g, t, z = lax.axis_index("group"), lax.axis_index("tm"), lax.axis_index("tensor")
    steps, devices = lax.axis_size("tm"), lax.axis_size("tensor")
    depth, cols = w_query.shape
    half = depth // 2
    wide = CHUNK_HEADS * HD
    chunks = cols // wide

    def over(array, axis, flip):
        return lax.ppermute(array, axis, [(i, i ^ flip) for i in range(lax.axis_size(axis))])

    def plane(array, pairs):
        flat = [(a[0] * devices + a[1], b[0] * devices + b[1]) for a, b in pairs]
        return lax.ppermute(array, ("tm", "tensor"), flat)

    sends = []
    for j in range(chunks):
        parts = [
            lax.dynamic_slice(w, (g * half, j * wide), (half, wide)) for w in (w_query, w_key, w_value)
        ]
        sends.append(jnp.concatenate(parts, axis=1))
    far = [over(s, "tm", 2) for s in sends]
    partner = [over(w, "tm", 1) for w in (w_query, w_key, w_value)]

    w_rows = w_out.shape[0] // 2
    own_half = lax.dynamic_slice_in_dim(w_out, g * w_rows, w_rows, 0)
    sent = [own_half] + [
        plane(own_half, [((s, (s + d) % devices), (s, s)) for s in range(steps)]) for d in range(1, devices)
    ]

    hidden = make_hidden(latent, stamp, mod_scale)
    acc = near_products(hidden, (w_query, w_key, w_value), partner, t)
    at_far, at_par = (t ^ 2) * depth, (t ^ 3) * depth
    idx = jnp.stack([at_far + g * half, at_par + g * half, at_far + (1 - g) * half, at_par + (1 - g) * half])
    idx = idx.astype(jnp.int32)

    far_x = [over(f, "group", 1) for f in far]
    par = [over(f, "tm", 1) for f in far]
    par_x = [over(f, "tm", 1) for f in far_x]

    own = []
    right = [[] for _ in range(devices - 1)]
    left = [[] for _ in range(devices - 1)]
    for j in range(chunks):
        att = attend(j, idx, hidden, acc, (far[j], far_x[j], par[j], par_x[j]), query_gain, key_gain)
        own.append(att)
        up = down = att
        for d in range(1, devices):
            up = lax.ppermute(up, "tensor", [(i, i + 1) for i in range(d - 1, devices - 1)])
            down = lax.ppermute(down, "tensor", [(i + 1, i) for i in range(0, devices - d)])
            right[d - 1].append(up)
            left[d - 1].append(down)

    across = [plane(s, [((s_, s_), (s_ ^ 2, s_)) for s_ in range(steps)]) for s in sent]
    held = [jnp.where(t == z, s, a) for s, a in zip(sent, across)]
    held_x = [over(h, "group", 1) for h in held]
    to_core = [((s, s), (s ^ 1, s)) for s in range(steps)] + [((s ^ 2, s), (s ^ 3, s)) for s in range(steps)]
    given = [plane(h, to_core) for h in held]
    given_x = [plane(h, to_core) for h in held_x]

    share = mod_gate.shape[0]
    gate = (step_sizes[0] * make_gate(stamp, mod_gate, width)).reshape(1, share)
    source = jnp.logical_or(t == z, t == (z ^ 2))
    out_idx = jnp.stack([z, source.astype(jnp.int32), g]).astype(jnp.int32)
    flat = lambda lists: [b for one in lists for b in one]
    term = out_projection(out_idx, gate, own, flat(right), flat(left), held, held_x, given, given_x)

    own_slice = lax.dynamic_slice_in_dim(latent, z * share, share, 1)
    start_core = lax.ppermute(own_slice, "tm", [(0, 1)])
    start_far = lax.ppermute(own_slice, "tm", [(0, 2)])
    start_last = lax.ppermute(start_far, "tm", [(2, 3)])
    start = jnp.where(t == 0, own_slice, jnp.where(t == 1, start_core, jnp.where(t == 2, start_far, start_last)))
    start = start.astype(jnp.float32)

    odd = t % 2 == 1
    before_core = lax.ppermute(term, "tm", [(0, 1), (2, 3)])
    chip_sum = before_core + term
    carry_last = lax.ppermute(chip_sum, "tm", [(1, 3)])
    carry_far = lax.ppermute(carry_last, "tm", [(3, 2)])
    before = jnp.where(odd, before_core, 0.0) + jnp.where(t == 2, carry_far, jnp.where(t == 3, carry_last, 0.0))
    predicted = start + before
    next_share = predicted + term
    gap = predicted - own_slice.astype(jnp.float32)
    squared = lax.psum(jnp.sum(gap * gap), "tensor")
    errors = (squared / (rows * width)).reshape(1, 1)
    return (next_share[None], errors)


def solution(mesh):
    placed = (
        P("tm", "group", None),
        P("tm"),
        P("tm"),
        P(),
        P("tensor"),
        P("tm", "tensor"),
        P("tm", "tensor"),
        P("tm", "tensor"),
        P("tensor"),
        P("tensor"),
        P("tensor", "tm"),
    )
    fast = mesh.shape["group"] == 2 and mesh.shape["tm"] == 4 and mesh.shape["tensor"] == 4
    return jax.shard_map(
        fast_body if fast else general_body,
        mesh=mesh,
        in_specs=placed,
        out_specs=(P("tm", "group", "tensor"), P("group", "tm")),
        check_vma=False,
    )
```

time: 585 us -> 480 us (0.82); the launches traced: 582 us -> 471 us
  waiting for transfers between devices: 442 us -> 192 us
  starting transfers between devices: 3.43 us -> 148 us
  Pallas kernels: 0 us -> 69.2 us
  matrix products: 66.1 us -> 0 us
  other arithmetic: 21.3 us -> 35.8 us
  between operations: 17.3 us -> 5.01 us
  local copies, waits for them, and re-layouts: 21.5 us -> 9.49 us
    ppermute x2 -> x58, starting transfers between devices: 3.2 us -> 148 us  [the longest x19 36.7 us: over(): lax.ppermute(array, axis, [(i, i ^ flip) for i in range(lax.axis_size(axi...]
    all_gather x4 -> x0, waiting for transfers between devices: 145 us -> none  [the longest x1 49.5 us: body(): lax.all_gather(w_query, 'tm', axis=0, tiled=True)]
    reduce_scatter x1 -> x0, waiting for transfers between devices: 137 us -> none  [body(): lax.psum_scatter(partial_out.astype(jnp.bfloat16), 'tensor', scatter_dime...]
    ppermute x2 -> x58, waiting for transfers between devices: 74.6 us -> 192 us  [the longest x19 108 us: over(): lax.ppermute(array, axis, [(i, i ^ flip) for i in range(lax.axis_size(axi...]
    psum x1 -> x0, waiting for transfers between devices: 83.9 us -> none  [spread(): return lax.psum(block, axis)]
    pallas_call x0 -> x5, Pallas kernels: none -> 69.2 us  [the longest x3 40.6 us: attend(): pl.pallas_call(functools.partial(attend_kernel, chunk), in_specs=[SMEM] +...]
    dot_general x5 -> x0, matrix products: 55 us -> none  [the longest x1 13.2 us: body(): jnp.dot(hidden, lax.all_gather(w_query, 'tm', axis=0, tiled=True), prefer...]
    dot_general x2 -> x0, local copies, waits for them, and re-layouts: 21 us -> none  [the longest x1 10.6 us: body(): jnp.dot(hidden, lax.all_gather(w_query, 'tm', axis=0, tiled=True), prefer...]
  transfers between devices with their start and end apart: 8 -> 58, of which waited for: 8 -> 20; matrix products, arithmetic and copies ran while one was open for 14% -> 5% of each run, Pallas kernels for 0% -> 12%
where the time goes in v1:
time: 480 us; the launch traced here: 471 us
  waiting for transfers between devices  192 us (40%)
  starting transfers between devices  148 us (31%)
  Pallas kernels  69.2 us (14%)
  other arithmetic  35.8 us (7%)
  blocking collectives  11.4 us (2%)
  local copies, waits for them, and re-layouts  9.49 us (2%)
  between operations  5.01 us (1%)
    ppermute x19, waiting for transfers between devices, over(): lax.ppermute(array, axis, [(i, i ^ flip) for i in range(lax.axis_size(axi...  108 us
    ppermute x1, waiting for transfers between devices, fast_body(): start_far = lax.ppermute(own_slice, 'tm', [(0, 2)])  43.2 us
    pallas_call x3, Pallas kernels, attend(): pl.pallas_call(functools.partial(attend_kernel, chunk), in_specs=[SMEM] +...  40.6 us
    ppermute x19, starting transfers between devices, over(): lax.ppermute(array, axis, [(i, i ^ flip) for i in range(lax.axis_size(axi...  36.7 us
    ppermute x9, starting transfers between devices, fast_body(): lax.ppermute(down, 'tensor', [(i + 1, i) for i in range(0, devices - d)])  34.1 us
    ppermute x9, waiting for transfers between devices, fast_body(): lax.ppermute(down, 'tensor', [(i + 1, i) for i in range(0, devices - d)])  31.8 us
    ppermute x9, starting transfers between devices, fast_body(): lax.ppermute(up, 'tensor', [(i, i + 1) for i in range(d - 1, devices - 1)])  25.9 us
    ppermute x1, starting transfers between devices, fast_body(): start_last = lax.ppermute(start_far, 'tm', [(2, 3)])  24.5 us
  transfers between devices with their start and end apart: 58, of which 20 were waited for; matrix products, arithmetic and copies ran while one was open for 5% of the time, Pallas kernels for 12%

profile of v1, /device:TPU:12, one launch (start us, length us, event | category | flops | bytes accessed | tf_op | source)
XLA Modules:
  0.0 470.8 jit_solution(15877330623951503689)
XLA Ops:
  27.0 7.2 %collective-permute-done.14.far = bf16[640,768]{1,0:T(8,128)(2,1)} collective-permute-done((bf16[640,768]{1,0:T(8,128)(2,1)}, bf16[640,768]{1,0:T(8,128)(2,1)}, u32[]{:S(2)}, u32[]{:S(2)}) %collective-permute-start.14) | collective-permute-done | bytes 983072 | tf_op jit(solution)/shard_map/ppermute | solution.py:322
  34.8 20.4 %collective-permute-done.10.far = bf16[640,768]{1,0:T(8,128)(2,1)} collective-permute-done((bf16[640,768]{1,0:T(8,128)(2,1)}, bf16[640,768]{1,0:T(8,128)(2,1)}, u32[]{:S(2)}, u32[]{:S(2)}) %collective-permute-start.10) | collective-permute-done | bytes 983072 | tf_op jit(solution)/shard_map/ppermute | solution.py:322
  58.6 17.2 %collective-permute-done.6.far = bf16[640,768]{1,0:T(8,128)(2,1)} collective-permute-done((bf16[640,768]{1,0:T(8,128)(2,1)}, bf16[640,768]{1,0:T(8,128)(2,1)}, u32[]{:S(2)}, u32[]{:S(2)}) %collective-permute-start.6) | collective-permute-done | bytes 983072 | tf_op jit(solution)/shard_map/ppermute | solution.py:322
  83.7 6.9 %collective-permute-start.5 = (bf16[1280,768]{1,0:T(8,128)(2,1)}, bf16[1280,768]{1,0:T(8,128)(2,1)}, u32[]{:S(2)}, u32[]{:S(2)}) collective-permute-start(bf16[1280,768]{1,0:T(8,128)(2,1)} %wv.1), channel_id=1, source_target_pairs={{0,4},{4,0},{8,12},{12,8},{1,5},{5,1},{9,13},{13,9},{2,6},{6,2},{1... | collective-permute-start | bytes 5898248 | tf_op jit(solution)/shard_map/ppermute | solution.py:322
  90.6 10.1 %collective-permute-done.15.far_x = bf16[640,768]{1,0:T(8,128)(2,1)S(1)} collective-permute-done((bf16[640,768]{1,0:T(8,128)(2,1)}, bf16[640,768]{1,0:T(8,128)(2,1)S(1)}, u32[]{:S(2)}, u32[]{:S(2)}) %collective-permute-start.15) | collective-permute-done | bytes 983072 | tf_op jit(solution)/shard_map/ppermute | solution.py:322
  104.1 9.7 %fusion.2.h_own.h_par.hid = bf16[768,5120]{1,0:T(8,128)(2,1)} fusion(bf16[1,768,5120]{2,1,0:T(8,128)(2,1)} %param.11, f32[5120]{0:T(1024)S(1)} %multiply_add_fusion, f32[768]{0:T(1024)S(1)} %add_rsqrt_fusion), kind=kLoop, calls=%fused_computation.4 | loop fusion | flops 15728640 | bytes 15752192 | tf_op jit(solution)/shard_map/convert_element_type | solution.py:43
  126.4 20.3 %collective-permute-done.7.far_x = bf16[640,768]{1,0:T(8,128)(2,1)} collective-permute-done((bf16[640,768]{1,0:T(8,128)(2,1)}, bf16[640,768]{1,0:T(8,128)(2,1)}, u32[]{:S(2)}, u32[]{:S(2)}) %collective-permute-start.7) | collective-permute-done | bytes 983072 | tf_op jit(solution)/shard_map/ppermute | solution.py:322
  147.5 15.6 %near_products.1.acc = f32[3,768,768]{2,1,0:T(8,128)} custom-call(s32[2]{0:T(128)} %pad_add_fusion.2.idx, bf16[768,5120]{1,0:T(8,128)(2,1)} %fusion.2.h_own.h_par.hid, bf16[768,5120]{1,0:T(8,128)(2,1)} %fusion.2.h_own.h_par.hid, bf16[1280,768]{1,0:T(8,128)(2,1)} %wq.1, bf16[1280,768]{1,0:T(8,128)(2,1)} %wk.1, bf16[1280,768]{1,0:T(8,128)(2,1)} %wv.1, ...), custom_call_target="tpu_custom_call" | custom-call | flops 9059696640 | bytes 11796480 | tf_op jit(solution)/shard_map/near_products/pallas_call | solution.py:115
  176.1 13.1 %collective-permute-done.44.refs_26_ = bf16[384,1280]{1,0:T(8,128)(2,1)S(1)} collective-permute-done((bf16[384,1280]{1,0:T(8,128)(2,1)S(1)}, bf16[384,1280]{1,0:T(8,128)(2,1)S(1)}, u32[]{:S(2)}, u32[]{:S(2)}) %collective-permute-start.44) | collective-permute-done | bytes 983072 | tf_op jit(solution)/shard_map/ppermute | solution.py:322
  190.7 13.5 %attend.5.refs_2_ = bf16[768,256]{1,0:T(8,128)(2,1)} custom-call(s32[4]{0:T(128)} %pad_add_fusion.1.idx, bf16[768,5120]{1,0:T(8,128)(2,1)} %fusion.2.h_own.h_par.hid, f32[3,768,768]{2,1,0:T(8,128)} %near_products.1.acc, bf16[640,768]{1,0:T(8,128)(2,1)} %collective-permute-done.14.far, bf16[640,768]{1,0:T(8,128)(2,1)} %copy-done.23, ...), custom_call_target="tpu_custom_call" | custom-call | flops 6039797760 | bytes 12582912 | tf_op jit(solution)/shard_map/attend/pallas_call | solution.py:197
  204.1 6.1 %collective-permute-done.45.refs_27_ = bf16[384,1280]{1,0:T(8,128)(2,1)S(1)} collective-permute-done((bf16[384,1280]{1,0:T(8,128)(2,1)S(1)}, bf16[384,1280]{1,0:T(8,128)(2,1)S(1)}, u32[]{:S(2)}, u32[]{:S(2)}) %collective-permute-start.45) | collective-permute-done | bytes 983072 | tf_op jit(solution)/shard_map/ppermute | solution.py:322
  211.5 13.6 %attend.4.refs_1_ = bf16[768,256]{1,0:T(8,128)(2,1)} custom-call(s32[4]{0:T(128)} %pad_add_fusion.1.idx, bf16[768,5120]{1,0:T(8,128)(2,1)} %fusion.2.h_own.h_par.hid, f32[3,768,768]{2,1,0:T(8,128)} %near_products.1.acc, bf16[640,768]{1,0:T(8,128)(2,1)} %collective-permute-done.10.far, bf16[640,768]{1,0:T(8,128)(2,1)} %collective-permute-done.11.far_x, ...), custom_call_target="tpu_custom_call" | custom-call | flops 6039797760 | bytes 12582912 | tf_op jit(solution)/shard_map/attend/pallas_call | solution.py:197
  225.1 6.3 %collective-permute-done.46.refs_28_ = bf16[384,1280]{1,0:T(8,128)(2,1)} collective-permute-done((bf16[384,1280]{1,0:T(8,128)(2,1)S(1)}, bf16[384,1280]{1,0:T(8,128)(2,1)}, u32[]{:S(2)}, u32[]{:S(2)}) %collective-permute-start.46) | collective-permute-done | bytes 983072 | tf_op jit(solution)/shard_map/ppermute | solution.py:322
  233.4 7.6 %collective-permute-start.29 = (bf16[768,256]{1,0:T(8,128)(2,1)S(1)}, bf16[768,256]{1,0:T(8,128)(2,1)S(1)}, u32[]{:S(2)}, u32[]{:S(2)}) collective-permute-start(bf16[768,256]{1,0:T(8,128)(2,1)S(1)} %copy-done.31), channel_id=1, source_target_pairs={{1,0},{2,1},{3,2},{5,4},{6,5},{7,6},{9,8},{10,9},{11,10},{13,12},{... | collective-permute-start | bytes 1179656 | tf_op jit(solution)/shard_map/ppermute | solution.py:362
  244.4 6.1 %collective-permute-start.28 = (bf16[768,256]{1,0:T(8,128)(2,1)}, bf16[768,256]{1,0:T(8,128)(2,1)S(1)}, u32[]{:S(2)}, u32[]{:S(2)}) collective-permute-start(bf16[768,256]{1,0:T(8,128)(2,1)} %attend.4.refs_1_), channel_id=1, source_target_pairs={{1,0},{2,1},{3,2},{5,4},{6,5},{7,6},{9,8},{10,9},{11,10},{13,12},{... | collective-permute-start | bytes 1179656 | tf_op jit(solution)/shard_map/ppermute | solution.py:362
  250.5 13.6 %attend.3.refs_0_ = bf16[768,256]{1,0:T(8,128)(2,1)} custom-call(s32[4]{0:T(128)} %pad_add_fusion.1.idx, bf16[768,5120]{1,0:T(8,128)(2,1)} %fusion.2.h_own.h_par.hid, f32[3,768,768]{2,1,0:T(8,128)} %near_products.1.acc, bf16[640,768]{1,0:T(8,128)(2,1)} %collective-permute-done.6.far, bf16[640,768]{1,0:T(8,128)(2,1)} %collective-permute-done.7.far_x, ...), custom_call_target="tpu_custom_call" | custom-call | flops 6039797760 | bytes 12582912 | tf_op jit(solution)/shard_map/attend/pallas_call | solution.py:197
  267.5 6.1 %collective-permute-start.27 = (bf16[768,256]{1,0:T(8,128)(2,1)}, bf16[768,256]{1,0:T(8,128)(2,1)S(1)}, u32[]{:S(2)}, u32[]{:S(2)}) collective-permute-start(bf16[768,256]{1,0:T(8,128)(2,1)} %attend.3.refs_0_), channel_id=1, source_target_pairs={{1,0},{2,1},{3,2},{5,4},{6,5},{7,6},{9,8},{10,9},{11,10},{13,12},{... | collective-permute-start | bytes 1179656 | tf_op jit(solution)/shard_map/ppermute | solution.py:362
  309.3 8.6 %collective-permute-done.30.refs_15_ = bf16[768,256]{1,0:T(8,128)(2,1)} collective-permute-done((bf16[768,256]{1,0:T(8,128)(2,1)S(1)}, bf16[768,256]{1,0:T(8,128)(2,1)}, u32[]{:S(2)}, u32[]{:S(2)}) %collective-permute-start.30) | collective-permute-done | bytes 393248 | tf_op jit(solution)/shard_map/ppermute | solution.py:362
  331.0 7.6 %collective-permute-done.34.refs_19_ = bf16[768,256]{1,0:T(8,128)(2,1)} collective-permute-done((bf16[768,256]{1,0:T(8,128)(2,1)}, bf16[768,256]{1,0:T(8,128)(2,1)}, u32[]{:S(2)}, u32[]{:S(2)}) %collective-permute-start.34) | collective-permute-done | bytes 393248 | tf_op jit(solution)/shard_map/ppermute | solution.py:362
  343.8 12.9 %out_projection.1 = f32[768,1280]{1,0:T(8,128)} custom-call(s32[3]{0:T(128)} %pad_add_fusion.idx, f32[1,1280]{1,0:T(1,128)} %reshape.33.gate, bf16[768,256]{1,0:T(8,128)(2,1)} %attend.3.refs_0_, bf16[768,256]{1,0:T(8,128)(2,1)} %attend.4.refs_1_, bf16[768,256]{1,0:T(8,128)(2,1)} %attend.5.refs_2_, bf16[768,256]{1,0:T(8,128)(2,1)} %copy-done.35, ...), custom_call_target="tpu_custom_call" | custom-call | flops 12079595520 | bytes 18874368 | tf_op jit(solution)/shard_map/out_projection/pallas_call | solution.py:289
  358.3 6.4 %collective-permute-done.55 = f32[768,1280]{1,0:T(8,128)S(1)} collective-permute-done((f32[768,1280]{1,0:T(8,128)}, f32[768,1280]{1,0:T(8,128)S(1)}, u32[]{:S(2)}, u32[]{:S(2)}) %collective-permute-start.55) | collective-permute-done | bytes 3932192 | tf_op jit(solution)/shard_map/ppermute | solution.py:388
  379.4 43.2 %collective-permute-done.1 = bf16[768,1280]{1,0:T(8,128)(2,1)} collective-permute-done((bf16[768,1280]{1,0:T(8,128)(2,1)S(1)}, bf16[768,1280]{1,0:T(8,128)(2,1)}, u32[]{:S(2)}, u32[]{:S(2)}) %collective-permute-start.1) | collective-permute-done | bytes 1966112 | tf_op jit(solution)/shard_map/ppermute | solution.py:382
  422.6 24.5 %collective-permute-start.2 = (bf16[768,1280]{1,0:T(8,128)(2,1)}, bf16[768,1280]{1,0:T(8,128)(2,1)}, u32[]{:S(2)}, u32[]{:S(2)}) collective-permute-start(bf16[768,1280]{1,0:T(8,128)(2,1)} %collective-permute-done.1), channel_id=1, source_target_pairs={{8,12},{9,13},{10,14},{11,15},{24,28},{25,29},{26,30},{27,31}} | collective-permute-start | bytes 5898248 | tf_op jit(solution)/shard_map/ppermute | solution.py:383
  457.2 11.4 %psum.7 = f32[]{:T(128)} all-reduce(f32[]{:T(128)} %get-tuple-element.2), channel_id=1, replica_groups=mesh['group'=2,'tm'=4,'tensor'=4] {'tensor'}, use_global_device_ids=true, to_apply=%region_2.3 | all-reduce | flops 1 | bytes 8 | tf_op jit(solution)/shard_map/psum | solution.py:396
  (203 shorter events, 157.9 us)
Async XLA Ops:
  11.8 43.5 %collective-permute-start.10 = (bf16[640,768]{1,0:T(8,128)(2,1)}, bf16[640,768]{1,0:T(8,128)(2,1)}, u32[]{:S(2)}, u32[]{:S(2)}) collective-permute-start(bf16[640,768]{1,0:T(8,128)(2,1)} %pad_maximum_fusion.1), channel_id=1, source_target_pairs={{0,8},{4,12},{8,0},{12,4},{1,9},{5,13},{9,1},{13,5},{2,10},{6,14},... | collective-permute-start | bytes 2949128 | tf_op jit(solution)/shard_map/ppermute | solution.py:322
  18.5 57.3 %collective-permute-start.6 = (bf16[640,768]{1,0:T(8,128)(2,1)}, bf16[640,768]{1,0:T(8,128)(2,1)}, u32[]{:S(2)}, u32[]{:S(2)}) collective-permute-start(bf16[640,768]{1,0:T(8,128)(2,1)} %pad_maximum_fusion), channel_id=1, source_target_pairs={{0,8},{4,12},{8,0},{12,4},{1,9},{5,13},{9,1},{13,5},{2,10},{6,14},... | collective-permute-start | bytes 2949128 | tf_op jit(solution)/shard_map/ppermute | solution.py:322
  25.5 51.0 %collective-permute-start.37 = (bf16[384,1280]{1,0:T(8,128)(2,1)S(1)}, bf16[384,1280]{1,0:T(8,128)(2,1)S(1)}, u32[]{:S(2)}, u32[]{:S(2)}) collective-permute-start(bf16[384,1280]{1,0:T(8,128)(2,1)S(1)} %constant_dynamic-slice_fusion), channel_id=1, source_target_pairs={{1,0},{6,5},{11,10},{12,15},{17,16},{22,21},{27,26},{28,31}} | collective-permute-start | bytes 2949128 | tf_op jit(solution)/shard_map/ppermute | solution.py:326
  26.2 51.9 %collective-permute-start.39 = (bf16[384,1280]{1,0:T(8,128)(2,1)S(1)}, bf16[384,1280]{1,0:T(8,128)(2,1)S(1)}, u32[]{:S(2)}, u32[]{:S(2)}) collective-permute-start(bf16[384,1280]{1,0:T(8,128)(2,1)S(1)} %constant_dynamic-slice_fusion), channel_id=1, source_target_pairs={{2,0},{7,5},{8,10},{13,15},{18,16},{23,21},{24,26},{29,31}} | collective-permute-start | bytes 2949128 | tf_op jit(solution)/shard_map/ppermute | solution.py:326
  34.1 68.0 %collective-permute-start.3 = (bf16[1280,768]{1,0:T(8,128)(2,1)S(1)}, bf16[1280,768]{1,0:T(8,128)(2,1)S(1)}, u32[]{:S(2)}, u32[]{:S(2)}) collective-permute-start(bf16[1280,768]{1,0:T(8,128)(2,1)S(1)} %copy-done.2), channel_id=1, source_target_pairs={{0,4},{4,0},{8,12},{12,8},{1,5},{5,1},{9,13},{13,9},{2,6},{6,2},{1... | collective-permute-start | bytes 5898248 | tf_op jit(solution)/shard_map/ppermute | solution.py:322
  103.5 43.2 %collective-permute-start.7 = (bf16[640,768]{1,0:T(8,128)(2,1)}, bf16[640,768]{1,0:T(8,128)(2,1)}, u32[]{:S(2)}, u32[]{:S(2)}) collective-permute-start(bf16[640,768]{1,0:T(8,128)(2,1)} %collective-permute-done.6.far), channel_id=1, source_target_pairs={{0,16},{16,0},{1,17},{17,1},{2,18},{18,2},{3,19},{19,3},{4,20},{20... | collective-permute-start | bytes 2949128 | tf_op jit(solution)/shard_map/ppermute | solution.py:322
  115.7 47.4 %collective-permute-start.38 = (bf16[384,1280]{1,0:T(8,128)(2,1)}, bf16[384,1280]{1,0:T(8,128)(2,1)S(1)}, u32[]{:S(2)}, u32[]{:S(2)}) collective-permute-start(bf16[384,1280]{1,0:T(8,128)(2,1)} %copy-done.10), channel_id=1, source_target_pairs={{0,8},{5,13},{10,2},{15,7},{16,24},{21,29},{26,18},{31,23}} | collective-permute-start | bytes 2949128 | tf_op jit(solution)/shard_map/ppermute | solution.py:326
  118.8 48.4 %collective-permute-start.43 = (bf16[384,1280]{1,0:T(8,128)(2,1)}, bf16[384,1280]{1,0:T(8,128)(2,1)}, u32[]{:S(2)}, u32[]{:S(2)}) collective-permute-start(bf16[384,1280]{1,0:T(8,128)(2,1)} %broadcast_select_fusion.3.refs_21_), channel_id=1, source_target_pairs={{0,16},{16,0},{1,17},{17,1},{2,18},{18,2},{3,19},{19,3},{4,20},{20... | collective-permute-start | bytes 2949128 | tf_op jit(solution)/shard_map/ppermute | solution.py:322
  125.7 39.0 %collective-permute-start.8 = (bf16[640,768]{1,0:T(8,128)(2,1)}, bf16[640,768]{1,0:T(8,128)(2,1)}, u32[]{:S(2)}, u32[]{:S(2)}) collective-permute-start(bf16[640,768]{1,0:T(8,128)(2,1)} %collective-permute-done.6.far), channel_id=1, source_target_pairs={{0,4},{4,0},{8,12},{12,8},{1,5},{5,1},{9,13},{13,9},{2,6},{6,2},{1... | collective-permute-start | bytes 2949128 | tf_op jit(solution)/shard_map/ppermute | solution.py:322
  125.7 40.5 %collective-permute-start.40 = (bf16[384,1280]{1,0:T(8,128)(2,1)S(1)}, bf16[384,1280]{1,0:T(8,128)(2,1)S(1)}, u32[]{:S(2)}, u32[]{:S(2)}) collective-permute-start(bf16[384,1280]{1,0:T(8,128)(2,1)S(1)} %collective-permute-done.39), channel_id=1, source_target_pairs={{0,8},{5,13},{10,2},{15,7},{16,24},{21,29},{26,18},{31,23}} | collective-permute-start | bytes 2949128 | tf_op jit(solution)/shard_map/ppermute | solution.py:326
  167.9 42.3 %collective-permute-start.45 = (bf16[384,1280]{1,0:T(8,128)(2,1)S(1)}, bf16[384,1280]{1,0:T(8,128)(2,1)S(1)}, u32[]{:S(2)}, u32[]{:S(2)}) collective-permute-start(bf16[384,1280]{1,0:T(8,128)(2,1)S(1)} %broadcast_select_fusion.1.refs_23_), channel_id=1, source_target_pairs={{0,16},{16,0},{1,17},{17,1},{2,18},{18,2},{3,19},{19,3},{4,20},{20... | collective-permute-start | bytes 2949128 | tf_op jit(solution)/shard_map/ppermute | solution.py:322
  169.9 63.4 %collective-permute-start.48 = (bf16[384,1280]{1,0:T(8,128)(2,1)S(1)}, bf16[384,1280]{1,0:T(8,128)(2,1)S(1)}, u32[]{:S(2)}, u32[]{:S(2)}) collective-permute-start(bf16[384,1280]{1,0:T(8,128)(2,1)S(1)} %broadcast_select_fusion.2.refs_22_), channel_id=1, source_target_pairs={{0,4},{5,1},{10,14},{15,11},{8,12},{13,9},{2,6},{7,3},{16,20},{21,... | collective-permute-start | bytes 2949128 | tf_op jit(solution)/shard_map/ppermute | solution.py:326
  172.3 68.6 %collective-permute-start.49 = (bf16[384,1280]{1,0:T(8,128)(2,1)S(1)}, bf16[384,1280]{1,0:T(8,128)(2,1)S(1)}, u32[]{:S(2)}, u32[]{:S(2)}) collective-permute-start(bf16[384,1280]{1,0:T(8,128)(2,1)S(1)} %broadcast_select_fusion.1.refs_23_), channel_id=1, source_target_pairs={{0,4},{5,1},{10,14},{15,11},{8,12},{13,9},{2,6},{7,3},{16,20},{21,... | collective-permute-start | bytes 2949128 | tf_op jit(solution)/shard_map/ppermute | solution.py:326
  173.7 57.8 %collective-permute-start.46 = (bf16[384,1280]{1,0:T(8,128)(2,1)S(1)}, bf16[384,1280]{1,0:T(8,128)(2,1)}, u32[]{:S(2)}, u32[]{:S(2)}) collective-permute-start(bf16[384,1280]{1,0:T(8,128)(2,1)S(1)} %broadcast_select_fusion.refs_24_), channel_id=1, source_target_pairs={{0,16},{16,0},{1,17},{17,1},{2,18},{18,2},{3,19},{19,3},{4,20},{20... | collective-permute-start | bytes 2949128 | tf_op jit(solution)/shard_map/ppermute | solution.py:322
  189.2 55.2 %collective-permute-start.50 = (bf16[384,1280]{1,0:T(8,128)(2,1)S(1)}, bf16[384,1280]{1,0:T(8,128)(2,1)}, u32[]{:S(2)}, u32[]{:S(2)}) collective-permute-start(bf16[384,1280]{1,0:T(8,128)(2,1)S(1)} %broadcast_select_fusion.refs_24_), channel_id=1, source_target_pairs={{0,4},{5,1},{10,14},{15,11},{8,12},{13,9},{2,6},{7,3},{16,20},{21,... | collective-permute-start | bytes 2949128 | tf_op jit(solution)/shard_map/ppermute | solution.py:326
  210.2 53.8 %collective-permute-start.51 = (bf16[384,1280]{1,0:T(8,128)(2,1)}, bf16[384,1280]{1,0:T(8,128)(2,1)}, u32[]{:S(2)}, u32[]{:S(2)}) collective-permute-start(bf16[384,1280]{1,0:T(8,128)(2,1)} %collective-permute-done.43.refs_25_), channel_id=1, source_target_pairs={{0,4},{5,1},{10,14},{15,11},{8,12},{13,9},{2,6},{7,3},{16,20},{21,... | collective-permute-start | bytes 2949128 | tf_op jit(solution)/shard_map/ppermute | solution.py:326
  233.4 40.3 %collective-permute-start.29 = (bf16[768,256]{1,0:T(8,128)(2,1)S(1)}, bf16[768,256]{1,0:T(8,128)(2,1)S(1)}, u32[]{:S(2)}, u32[]{:S(2)}) collective-permute-start(bf16[768,256]{1,0:T(8,128)(2,1)S(1)} %copy-done.31), channel_id=1, source_target_pairs={{1,0},{2,1},{3,2},{5,4},{6,5},{7,6},{9,8},{10,9},{11,10},{13,12},{... | collective-permute-start | bytes 1179656 | tf_op jit(solution)/shard_map/ppermute | solution.py:362
  240.9 36.1 %collective-permute-start.19 = (bf16[768,256]{1,0:T(8,128)(2,1)}, bf16[768,256]{1,0:T(8,128)(2,1)}, u32[]{:S(2)}, u32[]{:S(2)}) collective-permute-start(bf16[768,256]{1,0:T(8,128)(2,1)} %attend.4.refs_1_), channel_id=1, source_target_pairs={{0,1},{1,2},{2,3},{4,5},{5,6},{6,7},{8,9},{9,10},{10,11},{12,13},{... | collective-permute-start | bytes 1179656 | tf_op jit(solution)/shard_map/ppermute | solution.py:361
  284.4 36.6 %collective-permute-start.52 = (bf16[384,1280]{1,0:T(8,128)(2,1)S(1)}, bf16[384,1280]{1,0:T(8,128)(2,1)S(1)}, u32[]{:S(2)}, u32[]{:S(2)}) collective-permute-start(bf16[384,1280]{1,0:T(8,128)(2,1)S(1)} %collective-permute-done.44.refs_26_), channel_id=1, source_target_pairs={{0,4},{5,1},{10,14},{15,11},{8,12},{13,9},{2,6},{7,3},{16,20},{21,... | collective-permute-start | bytes 2949128 | tf_op jit(solution)/shard_map/ppermute | solution.py:326
  285.8 36.7 %collective-permute-start.53 = (bf16[384,1280]{1,0:T(8,128)(2,1)S(1)}, bf16[384,1280]{1,0:T(8,128)(2,1)S(1)}, u32[]{:S(2)}, u32[]{:S(2)}) collective-permute-start(bf16[384,1280]{1,0:T(8,128)(2,1)S(1)} %collective-permute-done.45.refs_27_), channel_id=1, source_target_pairs={{0,4},{5,1},{10,14},{15,11},{8,12},{13,9},{2,6},{7,3},{16,20},{21,... | collective-permute-start | bytes 2949128 | tf_op jit(solution)/shard_map/ppermute | solution.py:326
  287.1 37.5 %collective-permute-start.54 = (bf16[384,1280]{1,0:T(8,128)(2,1)}, bf16[384,1280]{1,0:T(8,128)(2,1)S(1)}, u32[]{:S(2)}, u32[]{:S(2)}) collective-permute-start(bf16[384,1280]{1,0:T(8,128)(2,1)} %collective-permute-done.46.refs_28_), channel_id=1, source_target_pairs={{0,4},{5,1},{10,14},{15,11},{8,12},{13,9},{2,6},{7,3},{16,20},{21,... | collective-permute-start | bytes 2949128 | tf_op jit(solution)/shard_map/ppermute | solution.py:326
  374.9 47.8 %collective-permute-start.1 = (bf16[768,1280]{1,0:T(8,128)(2,1)S(1)}, bf16[768,1280]{1,0:T(8,128)(2,1)}, u32[]{:S(2)}, u32[]{:S(2)}) collective-permute-start(bf16[768,1280]{1,0:T(8,128)(2,1)S(1)} %dynamic-slice_bitcast_fusion), channel_id=1, source_target_pairs={{0,8},{1,9},{2,10},{3,11},{16,24},{17,25},{18,26},{19,27}} | collective-permute-start | bytes 5898248 | tf_op jit(solution)/shard_map/ppermute | solution.py:382
  376.2 73.6 %collective-permute-start.57 = (f32[768,1280]{1,0:T(8,128)}, f32[768,1280]{1,0:T(8,128)}, u32[]{:S(2)}, u32[]{:S(2)}) collective-permute-start(f32[768,1280]{1,0:T(8,128)} %collective-permute-done.56), channel_id=1, source_target_pairs={{12,8},{13,9},{14,10},{15,11},{28,24},{29,25},{30,26},{31,27}} | collective-permute-start | bytes 11796488 | tf_op jit(solution)/shard_map/ppermute | solution.py:391
  377.5 69.7 %collective-permute-start = (bf16[768,1280]{1,0:T(8,128)(2,1)S(1)}, bf16[768,1280]{1,0:T(8,128)(2,1)}, u32[]{:S(2)}, u32[]{:S(2)}) collective-permute-start(bf16[768,1280]{1,0:T(8,128)(2,1)S(1)} %dynamic-slice_bitcast_fusion), channel_id=1, source_target_pairs={{0,4},{1,5},{2,6},{3,7},{16,20},{17,21},{18,22},{19,23}} | collective-permute-start | bytes 5898248 | tf_op jit(solution)/shard_map/ppermute | solution.py:381
  (73 other events, 1644.8 us)

commit v2 on v1

--- a/solution.py
+++ b/solution.py
@@ -10,6 +10,9 @@
 
 HD = 128
 CHUNK_HEADS = 2
+PARTS = 2
+CARRY = jnp.bfloat16
+COST = 1e6
 VMEM_LIMIT = 56 * 2**20
 ANY = pl.BlockSpec(memory_space=pl.ANY)
 SMEM = pl.BlockSpec(memory_space=pltpu.SMEM)
@@ -98,6 +101,69 @@
     return (next_share[None], errors)
 
 
+def after(value, *others):
+    return lax.optimization_barrier((value, *others))[0]
+
+
+def hidden_kernel(latent, scale, out):
+    values = latent[0].astype(jnp.float32)
+    normed = values * lax.rsqrt(jnp.mean(values * values, axis=-1, keepdims=True) + 1e-06)
+    out[...] = (normed * scale[...]).astype(jnp.bfloat16)
+
+
+def fast_hidden(states, stamp, mod_scale):
+    _, rows, width = states.shape
+    omega = jnp.exp(-math.log(10000.0) * jnp.arange(width).astype(jnp.float32) / width)
+    scale = (1.0 + mod_scale * jnp.cos(stamp * omega)).reshape(1, width)
+    block = 96 if rows % 96 == 0 else rows
+    return pl.pallas_call(
+        hidden_kernel,
+        grid=(rows // block,),
+        in_specs=[
+            pl.BlockSpec((1, block, width), lambda i: (0, i, 0)),
+            pl.BlockSpec((1, width), lambda i: (0, 0)),
+        ],
+        out_specs=pl.BlockSpec((block, width), lambda i: (i, 0)),
+        out_shape=jax.ShapeDtypeStruct((rows, width), jnp.bfloat16),
+        compiler_params=pltpu.CompilerParams(vmem_limit_bytes=VMEM_LIMIT),
+        cost_estimate=cost(5),
+        name="hidden",
+    )(states, scale)
+
+
+def phase(*values):
+    return lax.optimization_barrier(values)
+
+
+def cost(micros):
+    return pl.CostEstimate(flops=int(micros * 1e3 * COST), bytes_accessed=1024, transcendentals=0)
+
+
+def pack_kernel(idx, wq, wk, wv, out):
+    wide = wq.shape[1]
+    for n, w in enumerate((wq, wk, wv)):
+        out[:, n * wide : (n + 1) * wide] = w[...]
+
+
+def pack(chunk, group, weights):
+    depth = weights[0].shape[0]
+    wide = CHUNK_HEADS * HD
+    blocks = 2
+    tall = depth // 2 // blocks
+    return pl.pallas_call(
+        pack_kernel,
+        grid_spec=pltpu.PrefetchScalarGridSpec(
+            num_scalar_prefetch=1,
+            grid=(blocks,),
+            in_specs=[pl.BlockSpec((tall, wide), lambda i, idx: (idx[0] * blocks + i, chunk))] * 3,
+            out_specs=pl.BlockSpec((tall, 3 * wide), lambda i, idx: (i, 0)),
+        ),
+        out_shape=jax.ShapeDtypeStruct((depth // 2, 3 * wide), jnp.bfloat16),
+        cost_estimate=cost(1),
+        name="pack",
+    )(group.astype(jnp.int32).reshape(1), *weights)
+
+
 def near_kernel(idx, h_own, h_par, wq, wk, wv, pq, pk, pv, acc):
     wide = wq.shape[1]
     for n, (own, par) in enumerate(((wq, pq), (wk, pk), (wv, pv))):
@@ -126,9 +192,7 @@
         ),
         out_shape=jax.ShapeDtypeStruct((chunks, rows, 3 * wide), jnp.float32),
         compiler_params=pltpu.CompilerParams(vmem_limit_bytes=VMEM_LIMIT),
-        cost_estimate=pl.CostEstimate(
-            flops=12 * rows * depth * cols, bytes_accessed=6 * depth * cols * 2, transcendentals=0
-        ),
+        cost_estimate=cost(15),
         name="near_products",
     )(jnp.stack([tm, tm ^ 1]).astype(jnp.int32), hidden, hidden, *own, *partner)
 
@@ -207,65 +271,45 @@
             pltpu.SemaphoreType.DMA,
         ],
         compiler_params=pltpu.CompilerParams(vmem_limit_bytes=VMEM_LIMIT),
-        cost_estimate=pl.CostEstimate(
-            flops=2 * rows * 4 * half * 3 * wide * 2, bytes_accessed=12 * 2**20, transcendentals=CHUNK_HEADS * rows * rows
-        ),
+        cost_estimate=cost(12),
         name="attend",
     )(idx, hidden, acc, *pieces, *gains)
 
 
-def out_kernel(devices, chunks, idx, gate, *refs):
-    own, refs = refs[:chunks], refs[chunks:]
-    right, refs = refs[: (devices - 1) * chunks], refs[(devices - 1) * chunks :]
-    left, refs = refs[: (devices - 1) * chunks], refs[(devices - 1) * chunks :]
-    held, refs = refs[:devices], refs[devices:]
-    held_x, refs = refs[:devices], refs[devices:]
-    given, refs = refs[:devices], refs[devices:]
-    given_x, refs = refs[:devices], refs[devices:]
-    out, att, w, asems, wsems = refs
-    wide = own[0].shape[1]
-    half = held[0].shape[0]
-    z, source, g = idx[0], idx[1], idx[2]
+def out_kernel(devices, chunks, top, idx, gate, *refs):
+    gathered, pieces, (out, att, w, asems, wsems) = refs[:chunks], refs[chunks : chunks + 8], refs[chunks + 8 :]
+    rows = out.shape[0]
+    wide = gathered[0].shape[2]
+    half = pieces[0].shape[0]
+    core, g = idx[0], idx[1]
     waits = []
     for d in range(devices):
         here = []
         for j in range(chunks):
-            place = att.at[d, :, j * wide : (j + 1) * wide]
-            if d == 0:
-                pltpu.make_async_copy(own[j], place, asems.at[d * chunks + j]).start()
-            else:
-                behind = z + d >= devices
-
-                @pl.when(behind)
-                def _(d=d, j=j, place=place):
-                    pltpu.make_async_copy(
-                        right[(devices - d - 1) * chunks + j], place, asems.at[d * chunks + j]
-                    ).start()
-
-                @pl.when(jnp.logical_not(behind))
-                def _(d=d, j=j, place=place):
-                    pltpu.make_async_copy(left[(d - 1) * chunks + j], place, asems.at[d * chunks + j]).start()
-
-            here.append(pltpu.make_async_copy(own[j], place, asems.at[d * chunks + j]))
-        for n, (mine, other) in enumerate(((held, given), (held_x, given_x))):
-            at = pl.multiple_of((g if n == 0 else 1 - g) * half, 16)
-            place = w.at[d, pl.ds(at, half), :]
-
-            @pl.when(source == 1)
-            def _(d=d, n=n, place=place, mine=mine):
-                pltpu.make_async_copy(mine[d], place, wsems.at[2 * d + n]).start()
-
-            @pl.when(source == 0)
-            def _(d=d, n=n, place=place, other=other):
-                pltpu.make_async_copy(other[d], place, wsems.at[2 * d + n]).start()
-
-            here.append(pltpu.make_async_copy(mine[d], place, wsems.at[2 * d + n]))
+            here.append(
+                pltpu.make_async_copy(
+                    gathered[j].at[d, top : top + rows],
+                    att.at[d, :, j * wide : (j + 1) * wide],
+                    asems.at[d * chunks + j],
+                )
+            )
+            here[-1].start()
         waits.append(here)
+    wcopies = []
+    for n, piece in enumerate(pieces):
+        lower, other, swap = n // 4, (n // 2) % 2, n % 2
+        block = 2 * (core if other == 0 else 1 - core) + (g if swap == 0 else 1 - g)
+        place = w.at[block, lower * half : (lower + 1) * half, :]
+        wcopies.append(pltpu.make_async_copy(piece, place, wsems.at[n]))
+        wcopies[-1].start()
     share = out.shape[1]
     block = 256 if share % 256 == 0 else share
     for d in range(devices):
         for copy in waits[d]:
             copy.wait()
+        if d == 0:
+            for copy in wcopies:
+                copy.wait()
         for n in range(share // block):
             cols = slice(n * block, (n + 1) * block)
             part = (
@@ -280,29 +324,25 @@
             out[:, cols] = part
 
 
-def out_projection(idx, gate, own, right, left, held, held_x, given, given_x):
-    chunks = len(own)
-    devices = len(held)
-    rows, wide = own[0].shape
-    half, share = held[0].shape
-    operands = (*own, *right, *left, *held, *held_x, *given, *given_x)
+def out_projection(top, count, idx, gate, gathered, pieces):
+    chunks = len(gathered)
+    devices, rows, wide = gathered[0].shape
+    half, share = pieces[0].shape
     return pl.pallas_call(
-        functools.partial(out_kernel, devices, chunks),
-        in_specs=[SMEM, VMEM] + [ANY] * len(operands),
+        functools.partial(out_kernel, devices, chunks, top),
+        in_specs=[SMEM, VMEM] + [ANY] * (chunks + 8),
         out_specs=VMEM,
-        out_shape=jax.ShapeDtypeStruct((rows, share), jnp.float32),
+        out_shape=jax.ShapeDtypeStruct((count, share), jnp.float32),
         scratch_shapes=[
-            pltpu.VMEM((devices, rows, chunks * wide), jnp.bfloat16),
+            pltpu.VMEM((devices, count, chunks * wide), jnp.bfloat16),
             pltpu.VMEM((devices, 2 * half, share), jnp.bfloat16),
             pltpu.SemaphoreType.DMA((devices * chunks,)),
-            pltpu.SemaphoreType.DMA((2 * devices,)),
+            pltpu.SemaphoreType.DMA((8,)),
         ],
         compiler_params=pltpu.CompilerParams(vmem_limit_bytes=VMEM_LIMIT),
-        cost_estimate=pl.CostEstimate(
-            flops=2 * rows * devices * chunks * wide * share * 2, bytes_accessed=18 * 2**20, transcendentals=0
-        ),
+        cost_estimate=cost(7),
         name="out_projection",
-    )(idx, gate, *operands)
+    )(idx, gate, *gathered, *pieces)
 
 
 def fast_body(
@@ -312,86 +352,109 @@
     rows, width = latent.shape
     stamp = timesteps[0].astype(jnp.float32)
     g, t, z = lax.axis_index("group"), lax.axis_index("tm"), lax.axis_index("tensor")
-    steps, devices = lax.axis_size("tm"), lax.axis_size("tensor")
+    devices = 4
     depth, cols = w_query.shape
     half = depth // 2
-    wide = CHUNK_HEADS * HD
-    chunks = cols // wide
+    chunks = cols // (CHUNK_HEADS * HD)
 
     def over(array, axis, flip):
         return lax.ppermute(array, axis, [(i, i ^ flip) for i in range(lax.axis_size(axis))])
 
-    def plane(array, pairs):
-        flat = [(a[0] * devices + a[1], b[0] * devices + b[1]) for a, b in pairs]
-        return lax.ppermute(array, ("tm", "tensor"), flat)
-
-    sends = []
-    for j in range(chunks):
-        parts = [
-            lax.dynamic_slice(w, (g * half, j * wide), (half, wide)) for w in (w_query, w_key, w_value)
-        ]
-        sends.append(jnp.concatenate(parts, axis=1))
-    far = [over(s, "tm", 2) for s in sends]
-    partner = [over(w, "tm", 1) for w in (w_query, w_key, w_value)]
-
-    w_rows = w_out.shape[0] // 2
-    own_half = lax.dynamic_slice_in_dim(w_out, g * w_rows, w_rows, 0)
-    sent = [own_half] + [
-        plane(own_half, [((s, (s + d) % devices), (s, s)) for s in range(steps)]) for d in range(1, devices)
-    ]
-
-    hidden = make_hidden(latent, stamp, mod_scale)
-    acc = near_products(hidden, (w_query, w_key, w_value), partner, t)
+    weights = (w_query, w_key, w_value)
+    sends = [pack(0, g, weights)]
+    for j in range(1, chunks):
+        sends.append(pack(j, g, (after(weights[0], sends[-1]), *weights[1:])))
     at_far, at_par = (t ^ 2) * depth, (t ^ 3) * depth
     idx = jnp.stack([at_far + g * half, at_par + g * half, at_far + (1 - g) * half, at_par + (1 - g) * half])
     idx = idx.astype(jnp.int32)
-
-    far_x = [over(f, "group", 1) for f in far]
-    par = [over(f, "tm", 1) for f in far]
-    par_x = [over(f, "tm", 1) for f in far_x]
-
-    own = []
-    right = [[] for _ in range(devices - 1)]
-    left = [[] for _ in range(devices - 1)]
-    for j in range(chunks):
-        att = attend(j, idx, hidden, acc, (far[j], far_x[j], par[j], par_x[j]), query_gain, key_gain)
-        own.append(att)
-        up = down = att
-        for d in range(1, devices):
-            up = lax.ppermute(up, "tensor", [(i, i + 1) for i in range(d - 1, devices - 1)])
-            down = lax.ppermute(down, "tensor", [(i + 1, i) for i in range(0, devices - d)])
-            right[d - 1].append(up)
-            left[d - 1].append(down)
-
-    across = [plane(s, [((s_, s_), (s_ ^ 2, s_)) for s_ in range(steps)]) for s in sent]
-    held = [jnp.where(t == z, s, a) for s, a in zip(sent, across)]
-    held_x = [over(h, "group", 1) for h in held]
-    to_core = [((s, s), (s ^ 1, s)) for s in range(steps)] + [((s ^ 2, s), (s ^ 3, s)) for s in range(steps)]
-    given = [plane(h, to_core) for h in held]
-    given_x = [plane(h, to_core) for h in held_x]
-
     share = mod_gate.shape[0]
+    steps = range(4)
+
+    def place(group, step, tensor):
+        return (group * 4 + step) * devices + tensor
+
+    def far(array):
+        return over(array, "tm", 2)
+
+    def swap(array):
+        return over(array, "group", 1)
+
+    def partner(array):
+        return over(array, "tm", 1)
+
+    def attended(j, acc, pieces):
+        return attend(j, idx, hidden, acc, pieces, query_gain, key_gain)
+
+    y0 = far(sends[0])
+    to_plane = [
+        (place(b % 2, a, b), place(b % 2, 2 * (a // 2) + b // 2, a)) for a in steps for b in range(devices)
+    ]
+    sent = lax.ppermute(w_out, ("group", "tm", "tensor"), to_plane)
+    pq, pk, pv = (partner(w) for w in weights)
+    hidden = fast_hidden(after(states, *sends), stamp, mod_scale)
+    y0, pq, pk, pv, hidden, s1, s2 = phase(y0, pq, pk, pv, hidden, sends[1], sends[2])
+
+    y1, x0, c0 = far(s1), swap(y0), partner(y0)
+    acc = near_products(hidden, weights, (pq, pk, pv), t)
+    y1, x0, c0, acc, s2, sent = phase(y1, x0, c0, acc, s2, sent)
+
+    y2, x1, c1 = far(s2), swap(y1), partner(y1)
+    att0 = attended(0, acc, (y0, x0, c0, partner(x0)))
+    y2, x1, c1, att0, sent = phase(y2, x1, c1, att0, sent)
+
+    w_rows = w_out.shape[0] // 2
+    home = (t // 2) == (z // 2)
+    upper, lower = sent[:w_rows], sent[w_rows:]
+    crossing = [(a * devices + b, (a ^ 2) * devices + b) for a in steps for b in range(devices) if a // 2 == b // 2]
+
+    def cross(array):
+        return lax.ppermute(array, ("tm", "tensor"), crossing)
+
+    g0 = lax.all_gather(att0, "tensor")
+    u, x2, c2 = cross(upper), swap(y2), partner(y2)
+    att1 = attended(1, acc, (y1, x1, c1, partner(x1)))
+    u, x2, c2, att1, sent = phase(u, x2, c2, att1, sent)
+
+    g1 = lax.all_gather(att1, "tensor")
+    upper, lower = sent[:w_rows], sent[w_rows:]
+    v = jnp.where(home, upper, u)
+    w, xv, cv = cross(lower), swap(v), partner(v)
+    att2 = attended(2, acc, (y2, x2, c2, partner(x2)))
+    w, xv, cv, att2, v, sent = phase(w, xv, cv, att2, v, sent)
+
+    g2 = lax.all_gather(att2, "tensor")
+    lower = sent[w_rows:]
+    w = jnp.where(home, lower, w)
+    own_slice = lax.dynamic_slice_in_dim(latent, z * share, share, 1)
+    xw, cw, cxv = swap(w), partner(w), partner(xv)
+    start_far = lax.ppermute(own_slice, "tm", [(0, 2)])
+    start_core = lax.ppermute(own_slice, "tm", [(0, 1)])
+    xw, cw, cxv, start_far, start_core = phase(xw, cw, cxv, start_far, start_core)
+    start_last = lax.ppermute(start_far, "tm", [(2, 3)])
+    pieces = [v, xv, cv, cxv, w, xw, cw, partner(xw)]
+    gathered = [g0, g1, g2]
+
     gate = (step_sizes[0] * make_gate(stamp, mod_gate, width)).reshape(1, share)
-    source = jnp.logical_or(t == z, t == (z ^ 2))
-    out_idx = jnp.stack([z, source.astype(jnp.int32), g]).astype(jnp.int32)
-    flat = lambda lists: [b for one in lists for b in one]
-    term = out_projection(out_idx, gate, own, flat(right), flat(left), held, held_x, given, given_x)
-
-    own_slice = lax.dynamic_slice_in_dim(latent, z * share, share, 1)
-    start_core = lax.ppermute(own_slice, "tm", [(0, 1)])
-    start_far = lax.ppermute(own_slice, "tm", [(0, 2)])
-    start_last = lax.ppermute(start_far, "tm", [(2, 3)])
+    gate = after(gate, start_core, start_last)
+    out_idx = jnp.stack([t % 2, g]).astype(jnp.int32)
+    odd = t % 2 == 1
+    count = rows // PARTS
+    terms, befores = [], []
+    last = None
+    for r in range(PARTS):
+        feed = gate if last is None else after(gate, last)
+        term = out_projection(r * count, count, out_idx, feed, gathered, pieces)
+        last = term
+        before_core = lax.ppermute(term, "tm", [(0, 1), (2, 3)])
+        chip_sum = (before_core + term).astype(CARRY)
+        carry_last = lax.ppermute(chip_sum, "tm", [(1, 3)])
+        carry_far = lax.ppermute(carry_last, "tm", [(3, 2)])
+        carry = jnp.where(t == 2, carry_far, jnp.where(t == 3, carry_last, jnp.zeros_like(carry_last)))
+        terms.append(term)
+        befores.append(jnp.where(odd, before_core, 0.0) + carry.astype(jnp.float32))
     start = jnp.where(t == 0, own_slice, jnp.where(t == 1, start_core, jnp.where(t == 2, start_far, start_last)))
-    start = start.astype(jnp.float32)
-
-    odd = t % 2 == 1
-    before_core = lax.ppermute(term, "tm", [(0, 1), (2, 3)])
-    chip_sum = before_core + term
-    carry_last = lax.ppermute(chip_sum, "tm", [(1, 3)])
-    carry_far = lax.ppermute(carry_last, "tm", [(3, 2)])
-    before = jnp.where(odd, before_core, 0.0) + jnp.where(t == 2, carry_far, jnp.where(t == 3, carry_last, 0.0))
-    predicted = start + before
-    next_share = predicted + term
+    predicted = start.astype(jnp.float32) + jnp.concatenate(befores)
+    next_share = predicted + jnp.concatenate(terms)
     gap = predicted - own_slice.astype(jnp.float32)
     squared = lax.psum(jnp.sum(gap * gap), "tensor")
     errors = (squared / (rows * width)).reshape(1, 1)

time: 480 us -> 293 us (0.61); the launches traced: 471 us -> 291 us
  starting transfers between devices: 148 us -> 25 us
  waiting for transfers between devices: 192 us -> 116 us
  Pallas kernels: 69.2 us -> 94.2 us
  other arithmetic: 35.8 us -> 18.8 us
  between operations: 5.01 us -> 17.3 us
    ppermute x33 -> x3, starting transfers between devices: 78.3 us -> 3.52 us  [the longest x2 2.74 us: cross(): return lax.ppermute(array, ('tm', 'tensor'), crossing)]
    ppermute x19 -> x21, waiting for transfers between devices: 108 us -> 39.2 us  [over(): lax.ppermute(array, axis, [(i, i ^ flip) for i in range(lax.axis_size(axi...]
    ppermute x1, waiting for transfers between devices: 43.2 us -> 0.01 us  [fast_body(): start_far = lax.ppermute(own_slice, 'tm', [(0, 2)])]
    ppermute x19 -> x21, starting transfers between devices: 36.7 us -> 8.61 us  [over(): lax.ppermute(array, axis, [(i, i ^ flip) for i in range(lax.axis_size(axi...]
    pallas_call x1 -> x6, Pallas kernels: 12.9 us -> 38.1 us  [the longest x2 21.2 us: out_projection(): pl.pallas_call(functools.partial(out_kernel, devices, chunks, top), in_sp...]
    ppermute x1, starting transfers between devices: 24.5 us -> 1.62 us  [fast_body(): start_last = lax.ppermute(start_far, 'tm', [(2, 3)])]
    ppermute x1 -> x2, waiting for transfers between devices: 0.01 us -> 21.7 us  [fast_body(): carry_far = lax.ppermute(carry_last, 'tm', [(3, 2)])]
    all_gather x0 -> x3, waiting for transfers between devices: none -> 13.7 us  [the longest x1 13.7 us: fast_body(): g2 = lax.all_gather(att2, 'tensor')]
  transfers between devices with their start and end apart: 58 -> 36, of which waited for: 20 -> 13; matrix products, arithmetic and copies ran while one was open for 5% -> 6% of each run, Pallas kernels for 12% -> 25%
where the time goes in v2:
time: 293 us; the launch traced here: 291 us
  waiting for transfers between devices  116 us (40%)
  Pallas kernels  94.2 us (32%)
  starting transfers between devices  25 us (9%)
  other arithmetic  18.8 us (6%)
  between operations  17.3 us (6%)
  blocking collectives  10.6 us (4%)
  local copies, waits for them, and re-layouts  9.51 us (3%)
    pallas_call x3, Pallas kernels, attend(): pl.pallas_call(functools.partial(attend_kernel, chunk), in_specs=[SMEM] +...  40.5 us
    ppermute x21, waiting for transfers between devices, over(): lax.ppermute(array, axis, [(i, i ^ flip) for i in range(lax.axis_size(axi...  39.2 us
    ppermute x2, waiting for transfers between devices, cross(): return lax.ppermute(array, ('tm', 'tensor'), crossing)  37.2 us
    ppermute x2, waiting for transfers between devices, fast_body(): carry_far = lax.ppermute(carry_last, 'tm', [(3, 2)])  21.7 us
    pallas_call x2, Pallas kernels, out_projection(): pl.pallas_call(functools.partial(out_kernel, devices, chunks, top), in_sp...  21.2 us
    pallas_call x1, Pallas kernels, near_products(): pl.pallas_call(near_kernel, grid_spec=pltpu.PrefetchScalarGridSpec(num_sc...  15.6 us
    all_gather x1, waiting for transfers between devices, fast_body(): g2 = lax.all_gather(att2, 'tensor')  13.7 us
    psum x1, blocking collectives, fast_body(): squared = lax.psum(jnp.sum(gap * gap), 'tensor')  10.6 us
  transfers between devices with their start and end apart: 36, of which 13 were waited for; matrix products, arithmetic and copies ran while one was open for 6% of the time, Pallas kernels for 25%

profile of v2, /device:TPU:12, one launch (start us, length us, event | category | flops | bytes accessed | tf_op | source)
XLA Modules:
  0.0 290.9 jit_solution(1489207783685427070)
XLA Ops:
  11.9 2.2 pack.4
  17.6 10.4 %hidden.1.h_own.h_par.hid = bf16[768,5120]{1,0:T(8,128)(2,1)} custom-call(bf16[1,768,5120]{2,1,0:T(8,128)(2,1)} %latent, f32[1,5120]{1,0:T(1,128)} %bitcast.22), custom_call_target="tpu_custom_call" | custom-call | flops 5000000000 | bytes 1024 | tf_op jit(solution)/shard_map/hidden/pallas_call | solution.py:119
  28.0 6.4 %collective-permute-done.far = bf16[640,768]{1,0:T(8,128)(2,1)} collective-permute-done((bf16[640,768]{1,0:T(8,128)(2,1)}, bf16[640,768]{1,0:T(8,128)(2,1)}, u32[]{:S(2)}, u32[]{:S(2)}) %collective-permute-start) | collective-permute-done | bytes 983072 | tf_op jit(solution)/shard_map/ppermute | solution.py:361
  36.5 15.6 %near_products.1.acc = f32[3,768,768]{2,1,0:T(8,128)} custom-call(s32[2]{0:T(128)} %pad_add_fusion.idx, bf16[768,5120]{1,0:T(8,128)(2,1)} %hidden.1.h_own.h_par.hid, bf16[768,5120]{1,0:T(8,128)(2,1)} %hidden.1.h_own.h_par.hid, bf16[1280,768]{1,0:T(8,128)(2,1)} %wq.5, bf16[1280,768]{1,0:T(8,128)(2,1)} %wk.7, bf16[1280,768]{1,0:T(8,128)(2,1)} %wv.7, ...), custom_call_target="tpu_custom_call" | custom-call | flops 15000000512 | bytes 1024 | tf_op jit(solution)/shard_map/near_products/pallas_call | solution.py:181
  52.1 8.1 %collective-permute-done.4.far = bf16[640,768]{1,0:T(8,128)(2,1)S(1)} collective-permute-done((bf16[640,768]{1,0:T(8,128)(2,1)S(1)}, bf16[640,768]{1,0:T(8,128)(2,1)S(1)}, u32[]{:S(2)}, u32[]{:S(2)}) %collective-permute-start.4) | collective-permute-done | bytes 983072 | tf_op jit(solution)/shard_map/ppermute | solution.py:361
  64.0 13.5 %attend.3 = bf16[768,256]{1,0:T(8,128)(2,1)} custom-call(s32[4]{0:T(128)} %pad_add_fusion.1.idx, bf16[768,5120]{1,0:T(8,128)(2,1)} %hidden.1.h_own.h_par.hid, f32[3,768,768]{2,1,0:T(8,128)} %near_products.1.acc, bf16[640,768]{1,0:T(8,128)(2,1)} %collective-permute-done.far, bf16[640,768]{1,0:T(8,128)(2,1)} %collective-permute-done.5.far_x, ...), custom_call_target="tpu_custom_call" | custom-call | flops 12000000000 | bytes 1024 | tf_op jit(solution)/shard_map/attend/pallas_call | solution.py:261
  77.5 9.7 %collective-permute-done.8.far = bf16[640,768]{1,0:T(8,128)(2,1)} collective-permute-done((bf16[640,768]{1,0:T(8,128)(2,1)S(1)}, bf16[640,768]{1,0:T(8,128)(2,1)}, u32[]{:S(2)}, u32[]{:S(2)}) %collective-permute-start.8) | collective-permute-done | bytes 983072 | tf_op jit(solution)/shard_map/ppermute | solution.py:361
  91.6 13.6 %attend.4 = bf16[768,256]{1,0:T(8,128)(2,1)} custom-call(s32[4]{0:T(128)} %pad_add_fusion.1.idx, bf16[768,5120]{1,0:T(8,128)(2,1)} %hidden.1.h_own.h_par.hid, f32[3,768,768]{2,1,0:T(8,128)} %near_products.1.acc, bf16[640,768]{1,0:T(8,128)(2,1)} %copy-done.16, bf16[640,768]{1,0:T(8,128)(2,1)} %collective-permute-done.9.far_x, ...), custom_call_target="tpu_custom_call" | custom-call | flops 12000000000 | bytes 1024 | tf_op jit(solution)/shard_map/attend/pallas_call | solution.py:261
  105.2 10.9 %collective-permute-done.12 = bf16[384,1280]{1,0:T(8,128)(2,1)S(1)} collective-permute-done((bf16[384,1280]{1,0:T(8,128)(2,1)}, bf16[384,1280]{1,0:T(8,128)(2,1)S(1)}, u32[]{:S(2)}, u32[]{:S(2)}) %collective-permute-start.12) | collective-permute-done | bytes 983072 | tf_op jit(solution)/shard_map/ppermute | solution.py:411
  116.2 3.2 %dynamic-slice_bitcast_fusion = bf16[768,1280]{1,0:T(8,128)(2,1)} fusion(bf16[1,768,5120]{2,1,0:T(8,128)(2,1)} %latent, s32[]{:T(128)S(6)} %select_n.84), kind=kLoop, calls=%fused_computation.9 | loop fusion | bytes 3932164 | tf_op jit(solution)/shard_map/dynamic_slice | solution.py:428
  122.7 2.4 slice_select_fusion.1
  127.6 13.5 %attend.5 = bf16[768,256]{1,0:T(8,128)(2,1)} custom-call(s32[4]{0:T(128)} %pad_add_fusion.1.idx, bf16[768,5120]{1,0:T(8,128)(2,1)} %hidden.1.h_own.h_par.hid, f32[3,768,768]{2,1,0:T(8,128)} %near_products.1.acc, bf16[640,768]{1,0:T(8,128)(2,1)} %collective-permute-done.8.far, bf16[640,768]{1,0:T(8,128)(2,1)} %collective-permute-done.13.far_x, ...), custom_call_target="tpu_custom_call" | custom-call | flops 12000000000 | bytes 1024 | tf_op jit(solution)/shard_map/attend/pallas_call | solution.py:261
  141.1 26.3 %collective-permute-done.16 = bf16[384,1280]{1,0:T(8,128)(2,1)} collective-permute-done((bf16[384,1280]{1,0:T(8,128)(2,1)}, bf16[384,1280]{1,0:T(8,128)(2,1)}, u32[]{:S(2)}, u32[]{:S(2)}) %collective-permute-start.16) | collective-permute-done | bytes 983072 | tf_op jit(solution)/shard_map/ppermute | solution.py:411
  169.8 13.0 %collective-permute-done.20.refs_8_ = bf16[384,1280]{1,0:T(8,128)(2,1)S(1)} collective-permute-done((bf16[384,1280]{1,0:T(8,128)(2,1)S(1)}, bf16[384,1280]{1,0:T(8,128)(2,1)S(1)}, u32[]{:S(2)}, u32[]{:S(2)}) %collective-permute-start.20) | collective-permute-done | bytes 983072 | tf_op jit(solution)/shard_map/ppermute | solution.py:361
  191.5 13.7 %all-gather.11.cloned.1.call-done = bf16[3072,256]{1,0:T(8,128)(2,1)} async-done(((bf16[768,256]{1,0:T(8,128)(2,1)}), bf16[3072,256]{1,0:T(8,128)(2,1)}) %all-gather.11.cloned.1.call-update) | async-done | bytes 1572880 | tf_op jit(solution)/shard_map/all_gather | solution.py:425
  205.1 10.6 %out_projection.2 = f32[384,1280]{1,0:T(8,128)} custom-call(s32[2]{0:T(128)} %pad_add_fusion.2.idx, f32[1,1280]{1,0:T(1,128)} %reshape.34.gate, bf16[4,768,256]{2,1,0:T(8,128)(2,1)} %bitcast.23, bf16[4,768,256]{2,1,0:T(8,128)(2,1)} %bitcast.25, bf16[4,768,256]{2,1,0:T(8,128)(2,1)} %bitcast.27, bf16[384,1280]{1,0:T(8,128)(2,1)} %copy-done.7, ...), custom_call_target="tpu_custom_call" | custom-call | flops 7000000000 | bytes 1024 | tf_op jit(solution)/shard_map/out_projection/pallas_call | solution.py:331
  215.7 10.7 %out_projection.3 = f32[384,1280]{1,0:T(8,128)} custom-call(s32[2]{0:T(128)} %pad_add_fusion.2.idx, f32[1,1280]{1,0:T(1,128)} %reshape.34.gate, bf16[4,768,256]{2,1,0:T(8,128)(2,1)} %bitcast.24, bf16[4,768,256]{2,1,0:T(8,128)(2,1)} %bitcast.26, bf16[4,768,256]{2,1,0:T(8,128)(2,1)} %bitcast.28, bf16[384,1280]{1,0:T(8,128)(2,1)} %copy-done.7, ...), custom_call_target="tpu_custom_call" | custom-call | flops 7000000000 | bytes 1024 | tf_op jit(solution)/shard_map/out_projection/pallas_call | solution.py:331
  229.5 2.2 collective-permute-done.30
  231.7 2.5 add_convert_fusion
  240.5 12.4 %collective-permute-done.32 = bf16[384,1280]{1,0:T(8,128)(2,1)} collective-permute-done((bf16[384,1280]{1,0:T(8,128)(2,1)S(1)}, bf16[384,1280]{1,0:T(8,128)(2,1)}, u32[]{:S(2)}, u32[]{:S(2)}) %collective-permute-start.32) | collective-permute-done | bytes 983072 | tf_op jit(solution)/shard_map/ppermute | solution.py:451
  254.5 9.2 %collective-permute-done.29 = bf16[384,1280]{1,0:T(8,128)(2,1)} collective-permute-done((bf16[384,1280]{1,0:T(8,128)(2,1)}, bf16[384,1280]{1,0:T(8,128)(2,1)}, u32[]{:S(2)}, u32[]{:S(2)}) %collective-permute-start.29) | collective-permute-done | bytes 983072 | tf_op jit(solution)/shard_map/ppermute | solution.py:451
  265.5 3.9 %multiply_reduce_fusion = (f32[]{:T(128)}, bf16[768,1280]{1,0:T(8,128)(2,1)S(1)}) fusion(f32[384,1280]{1,0:T(8,128)S(1)} %convert_add_fusion, f32[384,1280]{1,0:T(8,128)S(1)} %convert_add_fusion.1, bf16[768,1280]{1,0:T(8,128)(2,1)} %collective-permute-done.24, bf16[768,1280]{1,0:T(8,128)(2,1)} %collective-permute-done.23, bf16[768,1280]{1,0:T(8,128)(2,1)S(1)} %copy-done.6, ...), kind=kLoop, calls=%fused_computation.3 | loop fusion | flops 9830399 | bytes 13762571 | tf_op jit(solution)/shard_map/reduce_sum | solution.py:459
  269.4 2.7 fusion
  272.0 10.6 %psum.7 = f32[]{:T(128)} all-reduce(f32[]{:T(128)} %get-tuple-element.80), channel_id=1, replica_groups=mesh['group'=2,'tm'=4,'tensor'=4] {'tensor'}, use_global_device_ids=true, to_apply=%region_1.2 | all-reduce | flops 1 | bytes 8 | tf_op jit(solution)/shard_map/psum | solution.py:459
  (119 shorter events, 46.4 us)
Async XLA Ops:
  7.2 182.8 %all-gather.7.cloned.1.call-start = ((), (), s32[]{:S(2)}) async-start(), calls=%async_computation | async-start | bytes 1966080 | tf_op jit(solution)/shard_map/all_gather | solution.py:413
  7.2 27.2 %collective-permute-start.1 = (bf16[1280,768]{1,0:T(8,128)(2,1)}, bf16[1280,768]{1,0:T(8,128)(2,1)}, u32[]{:S(2)}, u32[]{:S(2)}) collective-permute-start(bf16[1280,768]{1,0:T(8,128)(2,1)} %wq.5), channel_id=1, source_target_pairs={{0,4},{4,0},{8,12},{12,8},{1,5},{5,1},{9,13},{13,9},{2,6},{6,2},{1... | collective-permute-start | bytes 5898248 | tf_op jit(solution)/shard_map/ppermute | solution.py:361
  7.3 27.1 %collective-permute-start.2 = (bf16[1280,768]{1,0:T(8,128)(2,1)}, bf16[1280,768]{1,0:T(8,128)(2,1)}, u32[]{:S(2)}, u32[]{:S(2)}) collective-permute-start(bf16[1280,768]{1,0:T(8,128)(2,1)} %wk.7), channel_id=1, source_target_pairs={{0,4},{4,0},{8,12},{12,8},{1,5},{5,1},{9,13},{13,9},{2,6},{6,2},{1... | collective-permute-start | bytes 5898248 | tf_op jit(solution)/shard_map/ppermute | solution.py:361
  7.8 26.6 %collective-permute-start.3 = (bf16[1280,768]{1,0:T(8,128)(2,1)}, bf16[1280,768]{1,0:T(8,128)(2,1)}, u32[]{:S(2)}, u32[]{:S(2)}) collective-permute-start(bf16[1280,768]{1,0:T(8,128)(2,1)} %wv.7), channel_id=1, source_target_pairs={{0,4},{4,0},{8,12},{12,8},{1,5},{5,1},{9,13},{13,9},{2,6},{6,2},{1... | collective-permute-start | bytes 5898248 | tf_op jit(solution)/shard_map/ppermute | solution.py:361
  10.0 24.4 %collective-permute-start = (bf16[640,768]{1,0:T(8,128)(2,1)}, bf16[640,768]{1,0:T(8,128)(2,1)}, u32[]{:S(2)}, u32[]{:S(2)}) collective-permute-start(bf16[640,768]{1,0:T(8,128)(2,1)} %pack.3), channel_id=1, source_target_pairs={{0,8},{4,12},{8,0},{12,4},{1,9},{5,13},{9,1},{13,5},{2,10},{6,14},... | collective-permute-start | bytes 2949128 | tf_op jit(solution)/shard_map/ppermute | solution.py:361
  10.5 41.6 %collective-permute-start.7 = (bf16[768,1280]{1,0:T(8,128)(2,1)}, bf16[768,1280]{1,0:T(8,128)(2,1)S(1)}, u32[]{:S(2)}, u32[]{:S(2)}) collective-permute-start(bf16[768,1280]{1,0:T(8,128)(2,1)} %param.21), channel_id=1, source_target_pairs={{0,0},{17,16},{2,4},{19,20},{4,1},{21,17},{6,5},{23,21},{8,10},{25... | collective-permute-start | bytes 5898248 | tf_op jit(solution)/shard_map/ppermute | solution.py:392
  34.4 26.7 %collective-permute-start.5 = (bf16[640,768]{1,0:T(8,128)(2,1)}, bf16[640,768]{1,0:T(8,128)(2,1)}, u32[]{:S(2)}, u32[]{:S(2)}) collective-permute-start(bf16[640,768]{1,0:T(8,128)(2,1)} %collective-permute-done.far), channel_id=1, source_target_pairs={{0,16},{16,0},{1,17},{17,1},{2,18},{18,2},{3,19},{19,3},{4,20},{20... | collective-permute-start | bytes 2949128 | tf_op jit(solution)/shard_map/ppermute | solution.py:361
  36.0 25.1 %collective-permute-start.6 = (bf16[640,768]{1,0:T(8,128)(2,1)}, bf16[640,768]{1,0:T(8,128)(2,1)}, u32[]{:S(2)}, u32[]{:S(2)}) collective-permute-start(bf16[640,768]{1,0:T(8,128)(2,1)} %collective-permute-done.far), channel_id=1, source_target_pairs={{0,4},{4,0},{8,12},{12,8},{1,5},{5,1},{9,13},{13,9},{2,6},{6,2},{1... | collective-permute-start | bytes 2949128 | tf_op jit(solution)/shard_map/ppermute | solution.py:361
  36.0 24.2 %collective-permute-start.4 = (bf16[640,768]{1,0:T(8,128)(2,1)S(1)}, bf16[640,768]{1,0:T(8,128)(2,1)S(1)}, u32[]{:S(2)}, u32[]{:S(2)}) collective-permute-start(bf16[640,768]{1,0:T(8,128)(2,1)S(1)} %copy-done.11), channel_id=1, source_target_pairs={{0,8},{4,12},{8,0},{12,4},{1,9},{5,13},{9,1},{13,5},{2,10},{6,14},... | collective-permute-start | bytes 2949128 | tf_op jit(solution)/shard_map/ppermute | solution.py:361
  62.4 24.8 %collective-permute-start.9 = (bf16[640,768]{1,0:T(8,128)(2,1)}, bf16[640,768]{1,0:T(8,128)(2,1)}, u32[]{:S(2)}, u32[]{:S(2)}) collective-permute-start(bf16[640,768]{1,0:T(8,128)(2,1)} %copy-done.16), channel_id=1, source_target_pairs={{0,16},{16,0},{1,17},{17,1},{2,18},{18,2},{3,19},{19,3},{4,20},{20... | collective-permute-start | bytes 2949128 | tf_op jit(solution)/shard_map/ppermute | solution.py:361
  62.9 24.3 %collective-permute-start.10 = (bf16[640,768]{1,0:T(8,128)(2,1)}, bf16[640,768]{1,0:T(8,128)(2,1)}, u32[]{:S(2)}, u32[]{:S(2)}) collective-permute-start(bf16[640,768]{1,0:T(8,128)(2,1)} %copy-done.16), channel_id=1, source_target_pairs={{0,4},{4,0},{8,12},{12,8},{1,5},{5,1},{9,13},{13,9},{2,6},{6,2},{1... | collective-permute-start | bytes 2949128 | tf_op jit(solution)/shard_map/ppermute | solution.py:361
  63.1 24.1 %collective-permute-start.8 = (bf16[640,768]{1,0:T(8,128)(2,1)S(1)}, bf16[640,768]{1,0:T(8,128)(2,1)}, u32[]{:S(2)}, u32[]{:S(2)}) collective-permute-start(bf16[640,768]{1,0:T(8,128)(2,1)S(1)} %copy-done.9), channel_id=1, source_target_pairs={{0,8},{4,12},{8,0},{12,4},{1,9},{5,13},{9,1},{13,5},{2,10},{6,14},... | collective-permute-start | bytes 2949128 | tf_op jit(solution)/shard_map/ppermute | solution.py:361
  87.2 102.7 %all-gather.9.cloned.1.call-start = ((), (), s32[]{:S(2)}) async-start(), calls=%async_computation.1 | async-start | bytes 1966080 | tf_op jit(solution)/shard_map/all_gather | solution.py:418
  87.3 28.9 %collective-permute-start.13 = (bf16[640,768]{1,0:T(8,128)(2,1)}, bf16[640,768]{1,0:T(8,128)(2,1)}, u32[]{:S(2)}, u32[]{:S(2)}) collective-permute-start(bf16[640,768]{1,0:T(8,128)(2,1)} %collective-permute-done.8.far), channel_id=1, source_target_pairs={{0,16},{16,0},{1,17},{17,1},{2,18},{18,2},{3,19},{19,3},{4,20},{20... | collective-permute-start | bytes 2949128 | tf_op jit(solution)/shard_map/ppermute | solution.py:361
  88.8 27.3 %collective-permute-start.14 = (bf16[640,768]{1,0:T(8,128)(2,1)}, bf16[640,768]{1,0:T(8,128)(2,1)}, u32[]{:S(2)}, u32[]{:S(2)}) collective-permute-start(bf16[640,768]{1,0:T(8,128)(2,1)} %collective-permute-done.8.far), channel_id=1, source_target_pairs={{0,4},{4,0},{8,12},{12,8},{1,5},{5,1},{9,13},{13,9},{2,6},{6,2},{1... | collective-permute-start | bytes 2949128 | tf_op jit(solution)/shard_map/ppermute | solution.py:361
  90.1 26.0 %collective-permute-start.12 = (bf16[384,1280]{1,0:T(8,128)(2,1)}, bf16[384,1280]{1,0:T(8,128)(2,1)S(1)}, u32[]{:S(2)}, u32[]{:S(2)}) collective-permute-start(bf16[384,1280]{1,0:T(8,128)(2,1)} %slice.32), channel_id=1, source_target_pairs={{0,8},{1,9},{4,12},{5,13},{10,2},{11,3},{14,6},{15,7},{16,24},{17,... | collective-permute-start | bytes 2949128 | tf_op jit(solution)/shard_map/ppermute | solution.py:411
  119.5 50.3 %collective-permute-start.23 = (bf16[768,1280]{1,0:T(8,128)(2,1)}, bf16[768,1280]{1,0:T(8,128)(2,1)}, u32[]{:S(2)}, u32[]{:S(2)}) collective-permute-start(bf16[768,1280]{1,0:T(8,128)(2,1)} %dynamic-slice_bitcast_fusion), channel_id=1, source_target_pairs={{0,8},{1,9},{2,10},{3,11},{16,24},{17,25},{18,26},{19,27}} | collective-permute-start | bytes 5898248 | tf_op jit(solution)/shard_map/ppermute | solution.py:430
  120.7 49.1 %collective-permute-start.24 = (bf16[768,1280]{1,0:T(8,128)(2,1)}, bf16[768,1280]{1,0:T(8,128)(2,1)}, u32[]{:S(2)}, u32[]{:S(2)}) collective-permute-start(bf16[768,1280]{1,0:T(8,128)(2,1)} %dynamic-slice_bitcast_fusion), channel_id=1, source_target_pairs={{0,4},{1,5},{2,6},{3,7},{16,20},{17,21},{18,22},{19,23}} | collective-permute-start | bytes 5898248 | tf_op jit(solution)/shard_map/ppermute | solution.py:431
  122.7 82.4 %all-gather.11.cloned.1.call-start = ((), (), s32[]{:S(2)}) async-start(), calls=%async_computation.2 | async-start | bytes 1966080 | tf_op jit(solution)/shard_map/all_gather | solution.py:425
  125.1 42.2 %collective-permute-start.17 = (bf16[384,1280]{1,0:T(8,128)(2,1)S(1)}, bf16[384,1280]{1,0:T(8,128)(2,1)}, u32[]{:S(2)}, u32[]{:S(2)}) collective-permute-start(bf16[384,1280]{1,0:T(8,128)(2,1)S(1)} %get-tuple-element.74.refs_3_), channel_id=1, source_target_pairs={{0,16},{16,0},{1,17},{17,1},{2,18},{18,2},{3,19},{19,3},{4,20},{20... | collective-permute-start | bytes 2949128 | tf_op jit(solution)/shard_map/ppermute | solution.py:361
  125.7 41.7 %collective-permute-start.18 = (bf16[384,1280]{1,0:T(8,128)(2,1)S(1)}, bf16[384,1280]{1,0:T(8,128)(2,1)}, u32[]{:S(2)}, u32[]{:S(2)}) collective-permute-start(bf16[384,1280]{1,0:T(8,128)(2,1)S(1)} %get-tuple-element.74.refs_3_), channel_id=1, source_target_pairs={{0,4},{4,0},{8,12},{12,8},{1,5},{5,1},{9,13},{13,9},{2,6},{6,2},{1... | collective-permute-start | bytes 2949128 | tf_op jit(solution)/shard_map/ppermute | solution.py:361
  126.3 41.1 %collective-permute-start.16 = (bf16[384,1280]{1,0:T(8,128)(2,1)}, bf16[384,1280]{1,0:T(8,128)(2,1)}, u32[]{:S(2)}, u32[]{:S(2)}) collective-permute-start(bf16[384,1280]{1,0:T(8,128)(2,1)} %get-tuple-element.83), channel_id=1, source_target_pairs={{0,8},{1,9},{4,12},{5,13},{10,2},{11,3},{14,6},{15,7},{16,24},{17,... | collective-permute-start | bytes 2949128 | tf_op jit(solution)/shard_map/ppermute | solution.py:411
  169.3 15.6 %collective-permute-start.22 = (bf16[384,1280]{1,0:T(8,128)(2,1)}, bf16[384,1280]{1,0:T(8,128)(2,1)}, u32[]{:S(2)}, u32[]{:S(2)}) collective-permute-start(bf16[384,1280]{1,0:T(8,128)(2,1)} %collective-permute-done.17.refs_4_), channel_id=1, source_target_pairs={{0,4},{4,0},{8,12},{12,8},{1,5},{5,1},{9,13},{13,9},{2,6},{6,2},{1... | collective-permute-start | bytes 2949128 | tf_op jit(solution)/shard_map/ppermute | solution.py:361
  239.2 24.6 %collective-permute-start.29 = (bf16[384,1280]{1,0:T(8,128)(2,1)}, bf16[384,1280]{1,0:T(8,128)(2,1)}, u32[]{:S(2)}, u32[]{:S(2)}) collective-permute-start(bf16[384,1280]{1,0:T(8,128)(2,1)} %collective-permute-done.28), channel_id=1, source_target_pairs={{12,8},{13,9},{14,10},{15,11},{28,24},{29,25},{30,26},{31,27}} | collective-permute-start | bytes 2949128 | tf_op jit(solution)/shard_map/ppermute | solution.py:451
  (31 other events, 385.4 us)
Sparse Core Ops, SparseCore 0:
  87.3 37.3 all-gather.6
  126.3 35.9 all-gather.8
  169.9 35.1 all-gather.10

commit v3 on v0

v3 whole, which is shorter than its diff:
```python
import functools
import math

import jax
import jax.numpy as jnp
from jax import lax
from jax.experimental import pallas as pl
from jax.experimental.pallas import tpu as pltpu
from jax.sharding import PartitionSpec as P

HD = 128
CARRY = jnp.bfloat16
COST = 1e6
VMEM_LIMIT = 56 * 2**20
ANY = pl.BlockSpec(memory_space=pltpu.HBM)
SMEM = pl.BlockSpec(memory_space=pltpu.SMEM)
VMEM = pl.BlockSpec(memory_space=pltpu.VMEM)


def spread(block, axis, holder):
    block = jnp.where(lax.axis_index(axis) == holder, block, jnp.zeros_like(block))
    return lax.psum(block, axis)


def from_behind(array, axis, by):
    devices = lax.axis_size(axis)
    pairs = [(i, i + by) for i in range(devices) if 0 <= i + by < devices]
    return lax.ppermute(array, axis, pairs)


def head_norm(values, gain):
    rows = values.shape[0]
    count = values.shape[1] // HD
    split = values.reshape(rows, count, HD)
    normed = split * lax.rsqrt(jnp.mean(split * split, axis=-1, keepdims=True) + 1e-06)
    return (normed * gain.reshape(count, HD)).astype(jnp.bfloat16)


def make_hidden(latent, stamp, mod_scale):
    width = latent.shape[1]
    omega = jnp.exp(-math.log(10000.0) * jnp.arange(width).astype(jnp.float32) / width)
    values = latent.astype(jnp.float32)
    normed = values * lax.rsqrt(jnp.mean(values * values, axis=-1, keepdims=True) + 1e-06)
    return (normed * (1.0 + mod_scale * jnp.cos(stamp * omega))).astype(jnp.bfloat16)


def make_gate(stamp, mod_gate, width):
    share = mod_gate.shape[0]
    offset = lax.axis_index("tensor") * share
    positions = (offset + jnp.arange(share)).astype(jnp.float32)
    omega_share = jnp.exp(-math.log(10000.0) * positions / width)
    return 1.0 + mod_gate * jnp.sin(stamp * omega_share)


def general_body(
    states, timesteps, step_sizes, mod_scale, mod_gate, w_query, w_key, w_value, query_gain, key_gain, w_out
):
    latent = states[0]
    rows, width = latent.shape
    stamp = timesteps[0].astype(jnp.float32)
    hidden = make_hidden(latent, stamp, mod_scale)
    local_heads = w_query.shape[1]

    def project(weight):
        whole = lax.all_gather(weight, "tm", axis=0, tiled=True)
        return jnp.dot(hidden, whole, preferred_element_type=jnp.float32)

    count = local_heads // HD
    q_norm = head_norm(project(w_query), query_gain)
    k_norm = head_norm(project(w_key), key_gain)
    v_heads = project(w_value).astype(jnp.bfloat16).reshape(rows, count, HD)
    scores = jnp.einsum("qhd,khd->hqk", q_norm, k_norm, preferred_element_type=jnp.float32) / math.sqrt(HD)
    probs = jax.nn.softmax(scores, axis=-1).astype(jnp.bfloat16)
    attended = jnp.einsum("hqk,khd->qhd", probs, v_heads, preferred_element_type=jnp.float32)
    attended = attended.astype(jnp.bfloat16).reshape(rows, local_heads)
    share = mod_gate.shape[0]
    offset = lax.axis_index("tensor") * share
    partial_out = jnp.dot(
        attended,
        lax.all_gather(w_out, "tm", axis=1, tiled=True),
        preferred_element_type=jnp.float32,
    )
    projected = lax.psum_scatter(
        partial_out.astype(jnp.bfloat16), "tensor", scatter_dimension=1, tiled=True
    ).astype(jnp.float32)
    term = step_sizes[0] * make_gate(stamp, mod_gate, width) * projected
    own_slice = lax.dynamic_slice_in_dim(latent, offset, share, 1)
    own_start = own_slice.astype(jnp.float32)
    base_state = spread(own_slice, "tm", 0).astype(jnp.float32)
    running = term
    for level in range((lax.axis_size("tm") - 1).bit_length()):
        running = running + from_behind(running, "tm", 1 << level)
    before = running - term
    predicted = base_state + before
    next_share = predicted + term
    gap = predicted - own_start
    squared = lax.psum(jnp.sum(gap * gap), "tensor")
    errors = (squared / (rows * width)).reshape(1, 1)
    return (next_share[None], errors)


def after(value, *others):
    return lax.optimization_barrier((value, *others))[0]


def hidden_kernel(latent, scale, out):
    values = latent[0].astype(jnp.float32)
    normed = values * lax.rsqrt(jnp.mean(values * values, axis=-1, keepdims=True) + 1e-06)
    out[...] = (normed * scale[...]).astype(jnp.bfloat16)


def make_scale(stamp, mod_scale):
    width = mod_scale.shape[0]
    omega = jnp.exp(-math.log(10000.0) * jnp.arange(width).astype(jnp.float32) / width)
    return (1.0 + mod_scale * jnp.cos(stamp * omega)).reshape(1, width)


def fast_hidden(states, scale):
    _, rows, width = states.shape
    block = 192 if rows % 192 == 0 else rows
    return pl.pallas_call(
        hidden_kernel,
        grid=(rows // block,),
        in_specs=[
            pl.BlockSpec((1, block, width), lambda i: (0, i, 0)),
            pl.BlockSpec((1, width), lambda i: (0, 0)),
        ],
        out_specs=pl.BlockSpec((block, width), lambda i: (i, 0)),
        out_shape=jax.ShapeDtypeStruct((rows, width), jnp.bfloat16),
        compiler_params=pltpu.CompilerParams(vmem_limit_bytes=VMEM_LIMIT),
        cost_estimate=cost(5),
        name="hidden",
    )(states, scale)


def phase(*values):
    return lax.optimization_barrier(values)


def cost(micros):
    return pl.CostEstimate(flops=int(micros * 1e3 * COST), bytes_accessed=1024, transcendentals=0)


def here():
    t = lax.axis_index("tm")
    return lax.axis_index("group"), t, lax.axis_index("tensor"), t % 2


def move(sources, place, sems):
    copies = [pltpu.make_async_copy(src, dst, sems.at[n]) for n, (src, dst) in enumerate(zip(sources, place))]
    for copy in copies:
        copy.start()
    return copies


def params():
    return pltpu.CompilerParams(vmem_limit_bytes=VMEM_LIMIT)


def first_kernel(wq, wk, wv, mine, theirs, a, b, sems):
    g, _, _, core = here()
    half = a.shape[0]
    row = pl.multiple_of(g * half, 16)
    chunks = wq.shape[1] // (2 * HD)
    waits = []
    for m, (buf, out, who) in enumerate(((a, mine, core), (b, theirs, 1 - core))):
        col = pl.multiple_of(who * (chunks * HD), HD)
        src = [w.at[pl.ds(row, half), pl.ds(col, HD)] for w in (wq, wk, wv)]
        dst = [buf.at[:, n * HD : (n + 1) * HD] for n in range(3)]
        waits.append(move(src, dst, sems.at[pl.ds(4 * m, 3)]))
    for m, (buf, out) in enumerate(((a, mine), (b, theirs))):
        for copy in waits[m]:
            copy.wait()
        pltpu.make_async_copy(buf, out, sems.at[4 * m + 3]).start()
    for m, (buf, out) in enumerate(((a, mine), (b, theirs))):
        pltpu.make_async_copy(buf, out, sems.at[4 * m + 3]).wait()


def first_packs(weights):
    half = weights[0].shape[0] // 2
    shape = (half, 3 * HD)
    return pl.pallas_call(
        first_kernel,
        in_specs=[ANY] * 3,
        out_specs=[ANY] * 2,
        out_shape=[jax.ShapeDtypeStruct(shape, jnp.bfloat16)] * 2,
        scratch_shapes=[pltpu.VMEM(shape, jnp.bfloat16)] * 2 + [pltpu.SemaphoreType.DMA((8,))],
        compiler_params=params(),
        cost_estimate=cost(1),
        name="first_packs",
    )(*weights)


def packs_kernel(wq, wk, wv, pq, pk, pv, w_out, *refs):
    chunks = wq.shape[1] // (2 * HD)
    outs, bufs, (sems,) = refs[: chunks + 1], refs[chunks + 1 : 2 * (chunks + 1)], refs[2 * (chunks + 1) :]
    g, _, z, core = here()
    half = wq.shape[0] // 2
    share = w_out.shape[1] // 2
    row = pl.multiple_of(g * half, 16)
    waits = []
    for j in range(1, chunks):
        col = pl.multiple_of(core * (chunks * HD) + j * HD, HD)
        src = [w.at[pl.ds(row, half), pl.ds(col, HD)] for w in (wq, wk, wv, pq, pk, pv)]
        dst = [
            bufs[j - 1].at[(n // 3) * half : (n // 3 + 1) * half, (n % 3) * HD : (n % 3 + 1) * HD] for n in range(6)
        ]
        waits.append(move(src, dst, sems.at[pl.ds(6 * (j - 1), 6)]))
    base = 6 * (chunks - 1)
    for k in range(2):
        at = pl.multiple_of((k ^ (z // 2)) * share, HD)
        waits.append(move([w_out.at[:, pl.ds(at, share)]], [bufs[chunks - 1 + k]], sems.at[pl.ds(base + k, 1)]))
    for n, copies in enumerate(waits):
        for copy in copies:
            copy.wait()
        pltpu.make_async_copy(bufs[n], outs[n], sems.at[base + 2 + n]).start()
    for n in range(chunks + 1):
        pltpu.make_async_copy(bufs[n], outs[n], sems.at[base + 2 + n]).wait()


def packs(own, partner, w_out):
    depth, cols = own[0].shape
    chunks = cols // (2 * HD)
    shapes = [(depth, 3 * HD)] * (chunks - 1) + [(w_out.shape[0], w_out.shape[1] // 2)] * 2
    return pl.pallas_call(
        packs_kernel,
        in_specs=[ANY] * 7,
        out_specs=[ANY] * len(shapes),
        out_shape=[jax.ShapeDtypeStruct(shape, jnp.bfloat16) for shape in shapes],
        scratch_shapes=[pltpu.VMEM(shape, jnp.bfloat16) for shape in shapes]
        + [pltpu.SemaphoreType.DMA((6 * (chunks - 1) + 2 + len(shapes),))],
        compiler_params=params(),
        cost_estimate=cost(1),
        name="packs",
    )(*own, *partner, w_out)


def near_kernel(h_own, h_par, wq, wk, wv, pq, pk, pv, out, hbuf, wbuf, obuf, hsems, wsems, osems):
    _, t, _, core = here()
    depth = wq.shape[0]
    chunks = wq.shape[1] // (2 * HD)
    wide = chunks * HD
    head = pl.multiple_of(core * wide, HD)
    spans = [slice(m * depth, (m + 1) * depth) for m in range(2)]
    at = [pl.multiple_of(owner * depth, HD) for owner in (t, t ^ 1)]

    def hidden_part(i, h):
        src = [h.at[:, pl.ds(at[m], depth)] for m in range(2)]
        return move(src, [hbuf.at[i, :, spans[m]] for m in range(2)], hsems.at[pl.ds(2 * i, 2)])

    hcopies = [hidden_part(0, h_own)]
    wcopies = []
    for n, pair in enumerate(((wq, pq), (wk, pk), (wv, pv))):
        src = [w.at[:, pl.ds(head, wide)] for w in pair]
        dst = [wbuf.at[spans[m], n * wide : (n + 1) * wide] for m in range(2)]
        wcopies.append(move(src, dst, wsems.at[pl.ds(2 * n, 2)]))
    hcopies.append(hidden_part(1, h_par))
    cols = 3 * wide
    last = []
    for i in range(2):
        for copy in hcopies[i]:
            copy.wait()
        ready = 0
        for low in range(0, cols, 256):
            tile = slice(low, min(low + 256, cols))
            while i == 0 and ready * wide < tile.stop:
                for copy in wcopies[ready]:
                    copy.wait()
                ready += 1
            obuf[i, :, tile] = jnp.dot(hbuf[i], wbuf[:, tile], preferred_element_type=jnp.float32)
        src = [obuf.at[i, :, n * wide + j * HD : n * wide + (j + 1) * HD] for j in range(chunks) for n in range(3)]
        dst = [out.at[j, i, :, n * HD : (n + 1) * HD] for j in range(chunks) for n in range(3)]
        last += move(src, dst, osems.at[pl.ds(i * 3 * chunks, 3 * chunks)])
    for copy in last:
        copy.wait()


def near(hidden, beside, weights):
    rows, _ = hidden.shape
    depth, cols = weights[0].shape
    chunks = cols // (2 * HD)
    return pl.pallas_call(
        near_kernel,
        in_specs=[ANY] * 8,
        out_specs=ANY,
        out_shape=jax.ShapeDtypeStruct((chunks, 2, rows, 3 * HD), jnp.float32),
        scratch_shapes=[
            pltpu.VMEM((2, rows, 2 * depth), jnp.bfloat16),
            pltpu.VMEM((2 * depth, 3 * HD * chunks), jnp.bfloat16),
            pltpu.VMEM((2, rows, 3 * HD * chunks), jnp.float32),
            pltpu.SemaphoreType.DMA((4,)),
            pltpu.SemaphoreType.DMA((6,)),
            pltpu.SemaphoreType.DMA((6 * chunks,)),
        ],
        compiler_params=params(),
        cost_estimate=cost(10),
        name="near",
    )(hidden, beside, *weights)


def attend_kernel(chunk, row, parts, h_own, h_par, acc, qg, kg, *refs):
    pieces, (out, hbuf, wbuf, abuf, hsems, wsems, asems) = refs[:parts], refs[parts:]
    g, t, _, core = here()
    rows = hbuf.shape[1]
    half = hbuf.shape[2] // 4
    tall = 4 * half // parts
    chunks = qg.shape[1] // (2 * HD)
    starts = [(t ^ (2 + n % 2)) * (2 * half) + (g if n < 2 else 1 - g) * half for n in range(4)]
    wcopies, hcopies, acopies = [], [[], []], []
    for part in range(2):
        some = range(part * parts // 2, (part + 1) * parts // 2)
        dst = [wbuf.at[n * tall : (n + 1) * tall, :] for n in some]
        wcopies.append(move([pieces[n] for n in some], dst, wsems.at[pl.ds(part * parts // 2, parts // 2)]))
        for i, h in enumerate((h_own, h_par)):
            src = [h.at[:, pl.ds(pl.multiple_of(starts[n], HD), half)] for n in (2 * part, 2 * part + 1)]
            dst = [hbuf.at[i, :, n * half : (n + 1) * half] for n in (2 * part, 2 * part + 1)]
            hcopies[i].append(move(src, dst, hsems.at[pl.ds(4 * i + 2 * part, 2)]))
            if part == 0:
                acopies += move([acc.at[row, i]], [abuf.at[i]], asems.at[pl.ds(i, 1)])
    head = pl.multiple_of(core * (chunks * HD) + chunk * HD, HD)

    def normed(values, gain):
        scale = lax.rsqrt(jnp.mean(values * values, axis=-1, keepdims=True) + 1e-06)
        return (values * scale * gain).astype(jnp.bfloat16)

    block = rows // 2
    for i in range(2):
        for part in range(2):
            if i == 0:
                for copy in wcopies[part]:
                    copy.wait()
            for copy in hcopies[i][part]:
                copy.wait()
            if part == 0:
                acopies[i].wait()
            span = slice(2 * part * half, 2 * (part + 1) * half)
            abuf[i] += jnp.dot(hbuf[i, :, span], wbuf[span, :], preferred_element_type=jnp.float32)
        qn = normed(abuf[i, :, :HD], qg[:, pl.ds(head, HD)])
        kn = normed(abuf[i, :, HD : 2 * HD], kg[:, pl.ds(head, HD)])
        vb = abuf[i, :, 2 * HD :].astype(jnp.bfloat16)
        for r in range(2):
            scores = lax.dot_general(
                qn[r * block : (r + 1) * block],
                kn,
                (((1,), (1,)), ((), ())),
                preferred_element_type=jnp.float32,
            )
            top = jnp.max(scores, axis=-1, keepdims=True)
            grown = jnp.exp2((scores - top) * (math.log2(math.e) / math.sqrt(HD)))
            probs = grown * (1.0 / jnp.sum(grown, axis=-1, keepdims=True))
            out[i, r * block : (r + 1) * block, :] = jnp.dot(
                probs.astype(jnp.bfloat16), vb, preferred_element_type=jnp.float32
            ).astype(jnp.bfloat16)


def attend(chunk, hidden, beside, acc, row, pieces, qg, kg):
    rows = hidden.shape[0]
    parts = len(pieces)
    depth = sum(p.shape[0] for p in pieces)
    return pl.pallas_call(
        functools.partial(attend_kernel, chunk, row, parts),
        in_specs=[ANY] * 3 + [VMEM] * 2 + [ANY] * parts,
        out_specs=VMEM,
        out_shape=jax.ShapeDtypeStruct((2, rows, HD), jnp.bfloat16),
        scratch_shapes=[
            pltpu.VMEM((2, rows, depth), jnp.bfloat16),
            pltpu.VMEM((depth, 3 * HD), jnp.bfloat16),
            pltpu.VMEM((2, rows, 3 * HD), jnp.float32),
            pltpu.SemaphoreType.DMA((8,)),
            pltpu.SemaphoreType.DMA((parts,)),
            pltpu.SemaphoreType.DMA((2,)),
        ],
        compiler_params=params(),
        cost_estimate=cost(12),
        name="attend",
    )(hidden, beside, acc, qg.reshape(1, -1), kg.reshape(1, -1), *pieces)


def bundle_kernel(*refs):
    pieces, (out, buf, sems) = refs[:4], refs[4:]
    copies = move(pieces, [buf.at[d] for d in range(4)], sems.at[pl.ds(0, 4)])
    for d, copy in enumerate(copies):
        copy.wait()
        pltpu.make_async_copy(buf.at[d], out.at[d], sems.at[4 + d]).start()
    for d in range(4):
        pltpu.make_async_copy(buf.at[d], out.at[d], sems.at[4 + d]).wait()


def bundle(*pieces):
    shape = (4, *pieces[0].shape)
    return pl.pallas_call(
        bundle_kernel,
        in_specs=[ANY] * 4,
        out_specs=ANY,
        out_shape=jax.ShapeDtypeStruct(shape, pieces[0].dtype),
        scratch_shapes=[pltpu.VMEM(shape, pieces[0].dtype), pltpu.SemaphoreType.DMA((8,))],
        compiler_params=params(),
        cost_estimate=cost(1),
        name="bundle",
    )(*pieces)


def out_kernel(chunks, top, gate_own, gate_par, *refs):
    mine, theirs, pieces = refs[:chunks], refs[chunks : 2 * chunks], refs[2 * chunks : 2 * chunks + 4]
    terms, total, att, w, asems, wsems = refs[2 * chunks + 4 :]
    devices, _, rows, _ = att.shape
    group, _, plane, core = here()
    span = slice(top, top + rows)
    waits = []
    for d in range(devices):
        pairs = []
        for j in range(chunks):
            at = pl.multiple_of(core * (chunks * HD) + j * HD, HD)
            pairs.append((mine[j].at[d, :, span, :], att.at[d, :, :, pl.ds(at, HD)]))
            at = pl.multiple_of((1 - core) * (chunks * HD) + j * HD, HD)
            for i in range(2):
                pairs.append((theirs[j].at[d, 1 - i, span, :], att.at[d, i, :, pl.ds(at, HD)]))
        waits.append([pltpu.make_async_copy(a, b, asems.at[3 * chunks * d + n]) for n, (a, b) in enumerate(pairs)])
    wcopies = []
    for d in range(devices):
        block = plane ^ d
        slot = (block // 2) ^ core
        swap = (block % 2) ^ group
        which = 2 * slot + swap
        for n, piece in enumerate(pieces):
            copy = pltpu.make_async_copy(piece, w.at[d], wsems.at[d])
            pl.when(which == n)(copy.start)
        wcopies.append(pltpu.make_async_copy(pieces[0], w.at[d], wsems.at[d]))
        for copy in waits[d]:
            copy.start()
    for d in range(devices):
        wcopies[d].wait()
        for copy in waits[d]:
            copy.wait()
        for i, gate in enumerate((gate_own, gate_par)):
            place = core if i == 0 else 1 - core
            part = (
                jnp.dot(att[d, i], w[d], preferred_element_type=jnp.float32).astype(jnp.bfloat16).astype(jnp.float32)
            )
            if d > 0:
                part = terms[place] + part
            if d == devices - 1:
                part = gate[...] * part
            terms[place] = part
    total[...] = (terms[0] + terms[1]).astype(total.dtype)


def out_projection(top, count, gate_own, gate_par, mine, theirs, pieces):
    chunks = len(mine)
    devices = mine[0].shape[0]
    deep, share = pieces[0].shape
    return pl.pallas_call(
        functools.partial(out_kernel, chunks, top),
        in_specs=[VMEM, VMEM] + [ANY] * (2 * chunks + 4),
        out_specs=[VMEM, VMEM],
        out_shape=[
            jax.ShapeDtypeStruct((2, count, share), jnp.float32),
            jax.ShapeDtypeStruct((count, share), CARRY),
        ],
        scratch_shapes=[
            pltpu.VMEM((devices, 2, count, deep), jnp.bfloat16),
            pltpu.VMEM((devices, deep, share), jnp.bfloat16),
            pltpu.SemaphoreType.DMA((devices * 3 * chunks,)),
            pltpu.SemaphoreType.DMA((devices,)),
        ],
        compiler_params=params(),
        cost_estimate=cost(12),
        name="out_projection",
    )(gate_own, gate_par, *mine, *theirs, *pieces)


def close_kernel(terms, carry, start, own, par, mine, send, squares):
    _, _, _, core = here()
    first = core == 0
    low = jnp.where(first, own[...], par[...]).astype(jnp.float32)
    high = jnp.where(first, par[...], own[...]).astype(jnp.float32)
    at_low = start[...].astype(jnp.float32) + carry[...].astype(jnp.float32)
    at_high = at_low + terms[0]
    end = at_high + terms[1]
    mine[...] = jnp.where(first, at_high, end)
    send[...] = jnp.where(first, end, at_high)
    for n, gap in enumerate((at_low - low, at_high - high)):
        part = jnp.sum(gap * gap, axis=0, keepdims=True)

        @pl.when(pl.program_id(0) == 0)
        def _(n=n, part=part):
            squares[n : n + 1, :] = part

        @pl.when(pl.program_id(0) > 0)
        def _(n=n, part=part):
            squares[n : n + 1, :] += part


def close(top, terms, carry, start, own, par):
    _, count, share = terms.shape
    block = 192 if count % 192 == 0 and top % 192 == 0 else count
    skip = top // block
    whole = pl.BlockSpec((block, share), lambda i: (skip + i, 0))
    part = pl.BlockSpec((block, share), lambda i: (i, 0))
    return pl.pallas_call(
        close_kernel,
        grid=(count // block,),
        in_specs=[pl.BlockSpec((2, block, share), lambda i: (0, i, 0)), part, whole, whole, whole],
        out_specs=[part, part, pl.BlockSpec((2, share), lambda i: (0, 0))],
        out_shape=[
            jax.ShapeDtypeStruct((count, share), jnp.float32),
            jax.ShapeDtypeStruct((count, share), jnp.float32),
            jax.ShapeDtypeStruct((2, share), jnp.float32),
        ],
        compiler_params=params(),
        cost_estimate=cost(8),
        name="close",
    )(terms, carry, start, own, par)


def join_kernel(parts, *refs):
    mine, given, (out, buf, sems) = refs[:parts], refs[parts : 2 * parts], refs[2 * parts :]
    count, share = mine[0].shape
    _, _, _, core = here()
    copies = []
    for n, piece in enumerate((*mine, *given)):
        rows = slice((n % parts) * count, (n % parts + 1) * count)
        at = pl.multiple_of((core if n < parts else 1 - core) * share, HD)
        copies.append(
            (
                pltpu.make_async_copy(piece, buf.at[n], sems.at[2 * n]),
                pltpu.make_async_copy(buf.at[n], out.at[0, rows, pl.ds(at, share)], sems.at[2 * n + 1]),
            )
        )
    for come, _ in copies:
        come.start()
    for come, go in copies:
        come.wait()
        go.start()
    for _, go in copies:
        go.wait()


def join(mine, given):
    parts = len(mine)
    count, share = mine[0].shape
    return pl.pallas_call(
        functools.partial(join_kernel, parts),
        in_specs=[ANY] * (2 * parts),
        out_specs=ANY,
        out_shape=jax.ShapeDtypeStruct((1, parts * count, 2 * share), jnp.float32),
        scratch_shapes=[
            pltpu.VMEM((2 * parts, count, share), jnp.float32),
            pltpu.SemaphoreType.DMA((4 * parts,)),
        ],
        compiler_params=params(),
        cost_estimate=cost(8),
        name="join",
    )(*mine, *given)


def fast_body(
    states, timesteps, step_sizes, mod_scale, mod_gate, w_query, w_key, w_value, query_gain, key_gain, w_out
):
    latent = states[0]
    rows, width = latent.shape
    stamp = timesteps[0].astype(jnp.float32)
    t, z = lax.axis_index("tm"), lax.axis_index("tensor")
    core, chip = t % 2, t // 2
    devices = 4
    steps = range(4)
    share = mod_gate.shape[0] // 2
    chunks = w_query.shape[1] // (2 * HD)

    def over(array, axis, flip):
        return lax.ppermute(array, axis, [(i, i ^ flip) for i in range(lax.axis_size(axis))])

    def far(array):
        return over(array, "tm", 2)

    def swap(array):
        return over(array, "group", 1)

    def partner(array):
        return over(array, "tm", 1)

    def along(array, flip):
        return over(array, "tensor", flip)

    def place(group, step, tensor):
        return (group * 4 + step) * devices + tensor

    def cross(array):
        pairs = [(a * devices + b, (a ^ 2) * devices + b) for a in steps for b in range(devices) if a // 2 == b // 2]
        return lax.ppermute(array, ("tm", "tensor"), pairs)

    def to_plane(k, piece):
        pairs = [
            (place(b % 2, a, b), place(b % 2, 2 * (a // 2) + (k ^ (b // 2)), a))
            for a in steps
            for b in range(devices)
        ]
        return lax.ppermute(piece, ("group", "tm", "tensor"), pairs)

    weights = (w_query, w_key, w_value)
    others = [partner(w) for w in weights]
    own_step = jnp.stack([stamp, step_sizes[0]])
    par_step = partner(own_step)
    p0, r0 = first_packs(weights)
    p0, r0, w_out, states = phase(p0, r0, w_out, states)

    y0 = far(p0)
    z0 = over(r0, "tm", 3)
    hidden = fast_hidden(states, make_scale(stamp, mod_scale))
    s1, s2, o0, o1 = packs(weights, others, w_out)
    y0, z0, hidden, s1, s2, o0, o1, states, own_step, par_step = phase(
        y0, z0, hidden, s1, s2, o0, o1, states, own_step, par_step
    )

    beside = partner(hidden)
    y1, x0, xz0, sent0 = far(s1), swap(y0), swap(z0), to_plane(0, o0)
    acc = near(hidden, beside, (*weights, *others))
    y1, x0, xz0, acc, beside, s2, o1, sent0, states = phase(y1, x0, xz0, acc, beside, s2, o1, sent0, states)

    x1, y2, sent1 = swap(y1), far(s2), to_plane(1, o1)
    att0 = attend(0, hidden, beside, acc, 0, (y0, z0, x0, xz0), query_gain, key_gain)
    att0, states = phase(att0, states)
    two0, one0 = along(att0, 2), along(att0, 1)
    base = z * (2 * share)
    lat_own = lax.dynamic_slice_in_dim(states[0], base + core * share, share, 1)
    lat_give = lax.dynamic_slice_in_dim(states[0], base + (1 - core) * share, share, 1)
    y2, x1, sent1, acc, lat_own, lat_give = phase(y2, x1, sent1, acc, lat_own, lat_give)

    x2, u0, three0 = swap(y2), cross(sent0), along(att0, 3)
    lat_par = partner(lat_give)
    att1 = attend(1, hidden, beside, acc, 1, (y1, x1), query_gain, key_gain)
    u0, x2, sent1, att1, two0, one0, three0, lat_own, lat_par = phase(
        u0, x2, sent1, att1, two0, one0, three0, lat_own, lat_par
    )

    home = chip == z // 2
    v0 = jnp.where(home, sent0, u0)
    xv0, u1 = swap(v0), cross(sent1)
    two1, one1, three1 = along(att1, 2), along(att1, 1), along(att1, 3)
    att2 = attend(2, hidden, beside, acc, 2, (y2, x2), query_gain, key_gain)
    u1, xv0, v0, att2, two1, one1, three1, lat_own, lat_par = phase(
        u1, xv0, v0, att2, two1, one1, three1, lat_own, lat_par
    )

    two2, one2, three2 = along(att2, 2), along(att2, 1), along(att2, 3)
    v1 = jnp.where(home, sent1, u1)
    xv1 = swap(v1)
    start_near = jnp.where(core == 0, lat_own, lat_par)
    start_far = lax.ppermute(start_near, "tm", [(0, 2), (1, 3)])
    g0 = bundle(att0, one0, two0, three0)
    g1 = bundle(att1, one1, two1, three1)
    gates = []
    for pair in (own_step, par_step):
        gate = pair[1] * make_gate(pair[0], mod_gate, width)
        gates.append(lax.dynamic_slice_in_dim(gate, core * share, share, 0).reshape(1, share))
    two2, one2, three2, v1, xv1, start_far, start_near, g0, g1, *gates = phase(
        two2, one2, three2, v1, xv1, start_far, start_near, g0, g1, *gates
    )
    gate_own, gate_par = gates

    q0, q1 = partner(g0), partner(g1)
    g2 = bundle(att2, one2, two2, three2)
    start = jnp.where(chip == 0, start_near, start_far)
    q0, q1, g2, start = phase(q0, q1, g2, start)
    q2 = partner(g2)
    pieces = [v0, xv0, v1, xv1]

    count = rows // 2

    def project(top, gate_own):
        return out_projection(top, count, gate_own, gate_par, [g0, g1, g2], [q0, q1, q2], pieces)

    def ahead(total):
        return lax.ppermute(total, "tm", [(0, 2), (1, 3)])

    terms0, total0 = project(0, gate_own)
    terms0, total0, gate_own = phase(terms0, total0, gate_own)
    carry0 = ahead(total0)
    terms1, total1 = project(count, gate_own)
    terms1, total1, carry0, start = phase(terms1, total1, carry0, start)
    carry1 = ahead(total1)
    own0, send0, squares0 = close(0, terms0, carry0, start, lat_own, lat_par)
    carry1, own0, send0, squares0, start = phase(carry1, own0, send0, squares0, start)
    given0 = partner(send0)
    own1, send1, squares1 = close(count, terms1, carry1, start, lat_own, lat_par)
    given0, own1, send1, squares = phase(given0, own1, send1, squares0 + squares1)
    given1, squares_par = partner(send1), partner(squares)
    given1, squares = phase(given1, squares + squares_par)
    sums = jnp.sum(squares, axis=1)
    next_share = join([own0, own1], [given0, given1])
    sums, next_share = phase(sums, next_share)
    sums = sums + along(sums, 1) + along(sums, 2) + along(sums, 3)
    errors = (lax.dynamic_slice_in_dim(sums, core, 1, 0) / (rows * width)).reshape(1, 1)
    return (next_share, errors)


def solution(mesh):
    placed = (
        P("tm", "group", None),
        P("tm"),
        P("tm"),
        P(),
        P("tensor"),
        P("tm", "tensor"),
        P("tm", "tensor"),
        P("tm", "tensor"),
        P("tensor"),
        P("tensor"),
        P("tensor", "tm"),
    )
    fast = mesh.shape["group"] == 2 and mesh.shape["tm"] == 4 and mesh.shape["tensor"] == 4
    return jax.shard_map(
        fast_body if fast else general_body,
        mesh=mesh,
        in_specs=placed,
        out_specs=(P("tm", "group", "tensor"), P("group", "tm")),
        check_vma=False,
    )
```

time: 585 us -> 269 us (0.46)
  waiting for transfers between devices: 442 us -> 89.8 us
  Pallas kernels: 0 us -> 104 us
  matrix products: 66.1 us -> 0 us
  starting transfers between devices: 3.43 us -> 49.4 us
  other arithmetic: 21.3 us -> 5.69 us
  between operations: 17.3 us -> 4.32 us
  blocking collectives: 10 us -> 0 us
  local copies, waits for them, and re-layouts: 21.5 us -> 12.7 us
    all_gather x4 -> x0, waiting for transfers between devices: 145 us -> none  [the longest x1 49.5 us: body(): lax.all_gather(w_query, 'tm', axis=0, tiled=True)]
    reduce_scatter x1 -> x0, waiting for transfers between devices: 137 us -> none  [body(): lax.psum_scatter(partial_out.astype(jnp.bfloat16), 'tensor', scatter_dime...]
    pallas_call x0 -> x15, Pallas kernels: none -> 104 us  [the longest x3 36.7 us: attend(): pl.pallas_call(functools.partial(attend_kernel, chunk, row, parts), in_sp...]
    psum x1 -> x0, waiting for transfers between devices: 83.9 us -> none  [spread(): return lax.psum(block, axis)]
    dot_general x5 -> x0, matrix products: 55 us -> none  [the longest x1 13.2 us: body(): jnp.dot(hidden, lax.all_gather(w_query, 'tm', axis=0, tiled=True), prefer...]
    ppermute x2 -> x41, starting transfers between devices: 3.2 us -> 49.4 us  [the longest x34 40.8 us: over(): lax.ppermute(array, axis, [(i, i ^ flip) for i in range(lax.axis_size(axi...]
    dot_general x2 -> x0, local copies, waits for them, and re-layouts: 21 us -> none  [the longest x1 10.6 us: body(): jnp.dot(hidden, lax.all_gather(w_query, 'tm', axis=0, tiled=True), prefer...]
    ppermute x2 -> x41, waiting for transfers between devices: 74.6 us -> 89.8 us  [the longest x34 75.1 us: over(): lax.ppermute(array, axis, [(i, i ^ flip) for i in range(lax.axis_size(axi...]
  transfers between devices with their start and end apart: 8 -> 41, of which waited for: 8 -> 19; matrix products, arithmetic and copies ran while one was open for 14% -> 4% of each run, Pallas kernels for 0% -> 35%
where the time goes in v3:
time: 269 us; the launch traced here: 266 us
  Pallas kernels  104 us (39%)
  waiting for transfers between devices  89.8 us (33%)
  starting transfers between devices  49.4 us (18%)
  local copies, waits for them, and re-layouts  12.7 us (5%)
  other arithmetic  5.69 us (2%)
  between operations  4.32 us (2%)
    ppermute x34, waiting for transfers between devices, over(): lax.ppermute(array, axis, [(i, i ^ flip) for i in range(lax.axis_size(axi...  75.1 us
    ppermute x34, starting transfers between devices, over(): lax.ppermute(array, axis, [(i, i ^ flip) for i in range(lax.axis_size(axi...  40.8 us
    pallas_call x3, Pallas kernels, attend(): pl.pallas_call(functools.partial(attend_kernel, chunk, row, parts), in_sp...  36.7 us
    pallas_call x2, Pallas kernels, out_projection(): pl.pallas_call(functools.partial(out_kernel, chunks, top), in_specs=[VMEM...  17.9 us
    pallas_call x1, Pallas kernels, near(): pl.pallas_call(near_kernel, in_specs=[ANY] * 8, out_specs=ANY, out_shape=...  17.9 us
    ppermute x2, waiting for transfers between devices, ahead(): return lax.ppermute(total, 'tm', [(0, 2), (1, 3)])  14.6 us
    pallas_call x1, Pallas kernels, fast_hidden(): pl.pallas_call(hidden_kernel, grid=(rows // block,), in_specs=[pl.BlockSp...  8.92 us
    unnamed x70, local copies, waits for them, and re-layouts  7.43 us
  transfers between devices with their start and end apart: 41, of which 19 were waited for; matrix products, arithmetic and copies ran while one was open for 4% of the time, Pallas kernels for 35%

profile of v3, /device:TPU:12, one launch (start us, length us, event | category | flops | bytes accessed | tf_op | source)
XLA Modules:
  0.0 265.6 jit_solution(6217442961372907636)
XLA Ops:
  7.4 8.9 %hidden.1.h_own = bf16[768,5120]{1,0:T(8,128)(2,1)} custom-call(bf16[1,768,5120]{2,1,0:T(8,128)(2,1)} %latent, f32[1,5120]{1,0:T(1,128)} %bitcast.11), custom_call_target="tpu_custom_call" | custom-call | flops 5000000000 | bytes 1024 | tf_op jit(solution)/shard_map/hidden/pallas_call | solution.py:121
  19.6 3.5 %packs.1 = (bf16[1280,384]{1,0:T(8,128)(2,1)}, bf16[1280,384]{1,0:T(8,128)(2,1)}, bf16[768,640]{1,0:T(8,128)(2,1)}, bf16[768,640]{1,0:T(8,128)(2,1)}) custom-call(bf16[1280,768]{1,0:T(8,128)(2,1)} %wq.5, bf16[1280,768]{1,0:T(8,128)(2,1)} %wk.5, bf16[1280,768]{1,0:T(8,128)(2,1)} %wv.5, bf16[1280,768]{1,0:T(8,128)(2,1)} %copy-done.1, ...), custom_call_target="tpu_custom_call" | custom-call | flops 1000000000 | bytes 1024 | tf_op jit(solution)/shard_map/packs/pallas_call | solution.py:225
  23.2 4.2 %collective-permute-done.1.refs_1_ = bf16[640,384]{1,0:T(8,128)(2,1)S(1)} collective-permute-done((bf16[640,384]{1,0:T(8,128)(2,1)}, bf16[640,384]{1,0:T(8,128)(2,1)S(1)}, u32[]{:S(2)}, u32[]{:S(2)}) %collective-permute-start.1) | collective-permute-done | bytes 491552 | tf_op jit(solution)/shard_map/ppermute | solution.py:571
  34.0 6.2 %collective-permute-done.9.h_par = bf16[768,5120]{1,0:T(8,128)(2,1)} collective-permute-done((bf16[768,5120]{1,0:T(8,128)(2,1)}, bf16[768,5120]{1,0:T(8,128)(2,1)}, u32[]{:S(2)}, u32[]{:S(2)}) %collective-permute-start.9) | collective-permute-done | bytes 7864352 | tf_op jit(solution)/shard_map/ppermute | solution.py:571
  40.2 17.9 %near.1.acc = f32[3,2,768,384]{3,2,1,0:T(8,128)} custom-call(bf16[768,5120]{1,0:T(8,128)(2,1)} %hidden.1.h_own, bf16[768,5120]{1,0:T(8,128)(2,1)} %collective-permute-done.9.h_par, bf16[1280,768]{1,0:T(8,128)(2,1)} %wq.5, bf16[1280,768]{1,0:T(8,128)(2,1)} %wk.5, bf16[1280,768]{1,0:T(8,128)(2,1)} %wv.5, bf16[1280,768]{1,0:T(8,128)(2,1)} %copy-done.1, ...), custom_call_target="tpu_custom_call" | custom-call | flops 10000000000 | bytes 1024 | tf_op jit(solution)/shard_map/near/pallas_call | solution.py:282
  61.5 12.3 %attend.3.refs_0_ = bf16[2,768,128]{2,1,0:T(8,128)(2,1)} custom-call(bf16[768,5120]{1,0:T(8,128)(2,1)} %hidden.1.h_own, bf16[768,5120]{1,0:T(8,128)(2,1)} %collective-permute-done.9.h_par, f32[3,2,768,384]{3,2,1,0:T(8,128)} %near.1.acc, f32[1,768]{1,0:T(1,128)} %reshape.31.qg, f32[1,768]{1,0:T(1,128)} %reshape.32.kg, bf16[640,384]{1,0:T(8,128)(2,1)} %copy-done.21, ...), custom_call_target="tpu_custom_call" | custom-call | flops 12000000000 | bytes 1024 | tf_op jit(solution)/shard_map/attend/pallas_call | solution.py:360
  85.2 9.5 %collective-permute-start.15 = (bf16[1280,384]{1,0:T(8,128)(2,1)}, bf16[1280,384]{1,0:T(8,128)(2,1)}, u32[]{:S(2)}, u32[]{:S(2)}) collective-permute-start(bf16[1280,384]{1,0:T(8,128)(2,1)} %copy-done.17), channel_id=1, source_target_pairs={{0,16},{16,0},{1,17},{17,1},{2,18},{18,2},{3,19},{19,3},{4,20},{20... | collective-permute-start | bytes 2949128 | tf_op jit(solution)/shard_map/ppermute | solution.py:571
  94.8 8.6 %collective-permute-done.16.refs_2_ = bf16[2,768,128]{2,1,0:T(8,128)(2,1)} collective-permute-done((bf16[2,768,128]{2,1,0:T(8,128)(2,1)}, bf16[2,768,128]{2,1,0:T(8,128)(2,1)}, u32[]{:S(2)}, u32[]{:S(2)}) %collective-permute-start.16) | collective-permute-done | bytes 393248 | tf_op jit(solution)/shard_map/ppermute | solution.py:571
  103.4 12.3 %attend.4.refs_0_ = bf16[2,768,128]{2,1,0:T(8,128)(2,1)} custom-call(bf16[768,5120]{1,0:T(8,128)(2,1)} %hidden.1.h_own, bf16[768,5120]{1,0:T(8,128)(2,1)} %collective-permute-done.9.h_par, f32[3,2,768,384]{3,2,1,0:T(8,128)} %near.1.acc, f32[1,768]{1,0:T(1,128)} %reshape.31.qg, f32[1,768]{1,0:T(1,128)} %reshape.32.kg, ...), custom_call_target="tpu_custom_call" | custom-call | flops 12000000000 | bytes 1024 | tf_op jit(solution)/shard_map/attend/pallas_call | solution.py:360
  115.7 4.3 %collective-permute-done.18.refs_3_ = bf16[2,768,128]{2,1,0:T(8,128)(2,1)S(1)} collective-permute-done((bf16[2,768,128]{2,1,0:T(8,128)(2,1)S(1)}, bf16[2,768,128]{2,1,0:T(8,128)(2,1)S(1)}, u32[]{:S(2)}, u32[]{:S(2)}) %collective-permute-start.18) | collective-permute-done | bytes 393248 | tf_op jit(solution)/shard_map/ppermute | solution.py:571
  120.0 3.9 %collective-permute-start.23 = (bf16[2,768,128]{2,1,0:T(8,128)(2,1)}, bf16[2,768,128]{2,1,0:T(8,128)(2,1)}, u32[]{:S(2)}, u32[]{:S(2)}) collective-permute-start(bf16[2,768,128]{2,1,0:T(8,128)(2,1)} %attend.4.refs_0_), channel_id=1, source_target_pairs={{0,1},{1,0},{2,3},{3,2},{4,5},{5,4},{6,7},{7,6},{8,9},{9,8},{10,11... | collective-permute-start | bytes 1179656 | tf_op jit(solution)/shard_map/ppermute | solution.py:571
  124.1 4.0 %collective-permute-start.21 = (bf16[768,640]{1,0:T(8,128)(2,1)S(1)}, bf16[768,640]{1,0:T(8,128)(2,1)S(1)}, u32[]{:S(2)}, u32[]{:S(2)}) collective-permute-start(bf16[768,640]{1,0:T(8,128)(2,1)S(1)} %broadcast_select_fusion.3.refs_6_), channel_id=1, source_target_pairs={{0,16},{16,0},{1,17},{17,1},{2,18},{18,2},{3,19},{19,3},{4,20},{20... | collective-permute-start | bytes 2949128 | tf_op jit(solution)/shard_map/ppermute | solution.py:571
  129.6 12.2 %attend.5.refs_0_ = bf16[2,768,128]{2,1,0:T(8,128)(2,1)} custom-call(bf16[768,5120]{1,0:T(8,128)(2,1)} %hidden.1.h_own, bf16[768,5120]{1,0:T(8,128)(2,1)} %collective-permute-done.9.h_par, f32[3,2,768,384]{3,2,1,0:T(8,128)} %near.1.acc, f32[1,768]{1,0:T(1,128)} %reshape.31.qg, f32[1,768]{1,0:T(1,128)} %reshape.32.kg, bf16[1280,384]{1,0:T(8,128)(2,1)} %copy-done.17, ...), custom_call_target="tpu_custom_call" | custom-call | flops 12000000000 | bytes 1024 | tf_op jit(solution)/shard_map/attend/pallas_call | solution.py:360
  141.8 7.3 %collective-permute-done.23.refs_1_ = bf16[2,768,128]{2,1,0:T(8,128)(2,1)} collective-permute-done((bf16[2,768,128]{2,1,0:T(8,128)(2,1)}, bf16[2,768,128]{2,1,0:T(8,128)(2,1)}, u32[]{:S(2)}, u32[]{:S(2)}) %collective-permute-start.23) | collective-permute-done | bytes 393248 | tf_op jit(solution)/shard_map/ppermute | solution.py:571
  149.2 8.3 %collective-permute-done.24.refs_3_ = bf16[2,768,128]{2,1,0:T(8,128)(2,1)} collective-permute-done((bf16[2,768,128]{2,1,0:T(8,128)(2,1)}, bf16[2,768,128]{2,1,0:T(8,128)(2,1)}, u32[]{:S(2)}, u32[]{:S(2)}) %collective-permute-start.24) | collective-permute-done | bytes 393248 | tf_op jit(solution)/shard_map/ppermute | solution.py:571
  160.4 3.5 %collective-permute-start.26 = (bf16[2,768,128]{2,1,0:T(8,128)(2,1)S(1)}, bf16[2,768,128]{2,1,0:T(8,128)(2,1)S(1)}, u32[]{:S(2)}, u32[]{:S(2)}) collective-permute-start(bf16[2,768,128]{2,1,0:T(8,128)(2,1)S(1)} %copy-done.30), channel_id=1, source_target_pairs={{0,1},{1,0},{2,3},{3,2},{4,5},{5,4},{6,7},{7,6},{8,9},{9,8},{10,11... | collective-permute-start | bytes 1179656 | tf_op jit(solution)/shard_map/ppermute | solution.py:571
  172.9 5.4 %collective-permute-done.25.refs_2_ = bf16[2,768,128]{2,1,0:T(8,128)(2,1)S(1)} collective-permute-done((bf16[2,768,128]{2,1,0:T(8,128)(2,1)S(1)}, bf16[2,768,128]{2,1,0:T(8,128)(2,1)S(1)}, u32[]{:S(2)}, u32[]{:S(2)}) %collective-permute-start.25) | collective-permute-done | bytes 393248 | tf_op jit(solution)/shard_map/ppermute | solution.py:571
  178.3 4.0 %collective-permute-done.26.refs_1_ = bf16[2,768,128]{2,1,0:T(8,128)(2,1)S(1)} collective-permute-done((bf16[2,768,128]{2,1,0:T(8,128)(2,1)S(1)}, bf16[2,768,128]{2,1,0:T(8,128)(2,1)S(1)}, u32[]{:S(2)}, u32[]{:S(2)}) %collective-permute-start.26) | collective-permute-done | bytes 393248 | tf_op jit(solution)/shard_map/ppermute | solution.py:571
  182.3 14.5 %collective-permute-done.27.refs_3_ = bf16[2,768,128]{2,1,0:T(8,128)(2,1)S(1)} collective-permute-done((bf16[2,768,128]{2,1,0:T(8,128)(2,1)S(1)}, bf16[2,768,128]{2,1,0:T(8,128)(2,1)S(1)}, u32[]{:S(2)}, u32[]{:S(2)}) %collective-permute-start.27) | collective-permute-done | bytes 393248 | tf_op jit(solution)/shard_map/ppermute | solution.py:571
  207.4 8.8 %out_projection.2 = (f32[2,384,640]{2,1,0:T(8,128)}, bf16[384,640]{1,0:T(8,128)(2,1)}) custom-call(f32[1,640]{1,0:T(1,128)} %reshape.33.gate_own, f32[1,640]{1,0:T(1,128)} %reshape.34.gate_par, bf16[4,2,768,128]{3,2,1,0:T(8,128)(2,1)} %bundle.3.refs_0_, bf16[4,2,768,128]{3,2,1,0:T(8,128)(2,1)} %bundle.4.refs_1_, bf16[4,2,768,128]{3,2,1,0:T(8,128)(2,1)} %bundle.5.refs_2_, ...), custom_call_target="tpu_custom_call" | custom-call | flops 12000000000 | bytes 1024 | tf_op jit(solution)/shard_map/out_projection/pallas_call | solution.py:452
  217.8 9.1 %out_projection.3 = (f32[2,384,640]{2,1,0:T(8,128)}, bf16[384,640]{1,0:T(8,128)(2,1)}) custom-call(f32[1,640]{1,0:T(1,128)} %reshape.33.gate_own, f32[1,640]{1,0:T(1,128)} %reshape.34.gate_par, bf16[4,2,768,128]{3,2,1,0:T(8,128)(2,1)} %bundle.3.refs_0_, bf16[4,2,768,128]{3,2,1,0:T(8,128)(2,1)} %bundle.4.refs_1_, bf16[4,2,768,128]{3,2,1,0:T(8,128)(2,1)} %bundle.5.refs_2_, ...), custom_call_target="tpu_custom_call" | custom-call | flops 12000000000 | bytes 1024 | tf_op jit(solution)/shard_map/out_projection/pallas_call | solution.py:452
  226.9 4.7 %collective-permute-done.33.carry = bf16[384,640]{1,0:T(8,128)(2,1)S(1)} collective-permute-done((bf16[384,640]{1,0:T(8,128)(2,1)}, bf16[384,640]{1,0:T(8,128)(2,1)S(1)}, u32[]{:S(2)}, u32[]{:S(2)}) %collective-permute-start.33) | collective-permute-done | bytes 491552 | tf_op jit(solution)/shard_map/ppermute | solution.py:674
  233.0 3.4 %close.2 = (f32[384,640]{1,0:T(8,128)}, f32[384,640]{1,0:T(8,128)}, f32[2,640]{1,0:T(2,128)}) custom-call(f32[2,384,640]{2,1,0:T(8,128)} %get-tuple-element.179.terms, bf16[384,640]{1,0:T(8,128)(2,1)} %copy-done.25, bf16[768,640]{1,0:T(8,128)(2,1)} %broadcast_select_fusion.start, bf16[768,640]{1,0:T(8,128)(2,1)} %copy-done, bf16[768,640]{1,0:T(8,128)(2,1)} %copy-done.4), custom_call_target="tpu_custom_call" | custom-call | flops 8000000000 | bytes 1024 | tf_op jit(solution)/shard_map/close/pallas_call | solution.py:500
  236.4 9.9 %collective-permute-done.34.carry = bf16[384,640]{1,0:T(8,128)(2,1)S(1)} collective-permute-done((bf16[384,640]{1,0:T(8,128)(2,1)}, bf16[384,640]{1,0:T(8,128)(2,1)S(1)}, u32[]{:S(2)}, u32[]{:S(2)}) %collective-permute-start.34) | collective-permute-done | bytes 491552 | tf_op jit(solution)/shard_map/ppermute | solution.py:674
  (162 shorter events, 74.6 us)
Async XLA Ops:
  3.5 19.7 %collective-permute-start = (bf16[640,384]{1,0:T(8,128)(2,1)}, bf16[640,384]{1,0:T(8,128)(2,1)S(1)}, u32[]{:S(2)}, u32[]{:S(2)}) collective-permute-start(bf16[640,384]{1,0:T(8,128)(2,1)} %get-tuple-element.104), channel_id=1, source_target_pairs={{0,8},{4,12},{8,0},{12,4},{1,9},{5,13},{9,1},{13,5},{2,10},{6,14},... | collective-permute-start | bytes 1474568 | tf_op jit(solution)/shard_map/ppermute | solution.py:571
  4.0 23.4 %collective-permute-start.1 = (bf16[640,384]{1,0:T(8,128)(2,1)}, bf16[640,384]{1,0:T(8,128)(2,1)S(1)}, u32[]{:S(2)}, u32[]{:S(2)}) collective-permute-start(bf16[640,384]{1,0:T(8,128)(2,1)} %get-tuple-element.105), channel_id=1, source_target_pairs={{0,12},{4,8},{8,4},{12,0},{1,13},{5,9},{9,5},{13,1},{2,14},{6,10},... | collective-permute-start | bytes 1474568 | tf_op jit(solution)/shard_map/ppermute | solution.py:571
  27.7 30.4 %collective-permute-start.10 = (bf16[768,640]{1,0:T(8,128)(2,1)}, bf16[768,640]{1,0:T(8,128)(2,1)S(1)}, u32[]{:S(2)}, u32[]{:S(2)}) collective-permute-start(bf16[768,640]{1,0:T(8,128)(2,1)} %get-tuple-element.118), channel_id=1, source_target_pairs={{0,0},{17,16},{2,4},{19,20},{4,1},{21,17},{6,5},{23,21},{8,10},{25... | collective-permute-start | bytes 2949128 | tf_op jit(solution)/shard_map/ppermute | solution.py:598
  28.4 29.7 %collective-permute-start.6 = (bf16[1280,384]{1,0:T(8,128)(2,1)}, bf16[1280,384]{1,0:T(8,128)(2,1)}, u32[]{:S(2)}, u32[]{:S(2)}) collective-permute-start(bf16[1280,384]{1,0:T(8,128)(2,1)} %get-tuple-element.112), channel_id=1, source_target_pairs={{0,8},{4,12},{8,0},{12,4},{1,9},{5,13},{9,1},{13,5},{2,10},{6,14},... | collective-permute-start | bytes 2949128 | tf_op jit(solution)/shard_map/ppermute | solution.py:571
  30.7 27.4 %collective-permute-start.7 = (bf16[640,384]{1,0:T(8,128)(2,1)S(1)}, bf16[640,384]{1,0:T(8,128)(2,1)S(1)}, u32[]{:S(2)}, u32[]{:S(2)}) collective-permute-start(bf16[640,384]{1,0:T(8,128)(2,1)S(1)} %collective-permute-done.refs_0_), channel_id=1, source_target_pairs={{0,16},{16,0},{1,17},{17,1},{2,18},{18,2},{3,19},{19,3},{4,20},{20... | collective-permute-start | bytes 1474568 | tf_op jit(solution)/shard_map/ppermute | solution.py:571
  34.0 24.1 %collective-permute-start.8 = (bf16[640,384]{1,0:T(8,128)(2,1)S(1)}, bf16[640,384]{1,0:T(8,128)(2,1)S(1)}, u32[]{:S(2)}, u32[]{:S(2)}) collective-permute-start(bf16[640,384]{1,0:T(8,128)(2,1)S(1)} %collective-permute-done.1.refs_1_), channel_id=1, source_target_pairs={{0,16},{16,0},{1,17},{17,1},{2,18},{18,2},{3,19},{19,3},{4,20},{20... | collective-permute-start | bytes 1474568 | tf_op jit(solution)/shard_map/ppermute | solution.py:571
  58.1 24.2 %collective-permute-start.12 = (bf16[1280,384]{1,0:T(8,128)(2,1)}, bf16[1280,384]{1,0:T(8,128)(2,1)S(1)}, u32[]{:S(2)}, u32[]{:S(2)}) collective-permute-start(bf16[1280,384]{1,0:T(8,128)(2,1)} %get-tuple-element.121), channel_id=1, source_target_pairs={{0,8},{4,12},{8,0},{12,4},{1,9},{5,13},{9,1},{13,5},{2,10},{6,14},... | collective-permute-start | bytes 2949128 | tf_op jit(solution)/shard_map/ppermute | solution.py:571
  58.7 25.2 %collective-permute-start.13 = (bf16[1280,384]{1,0:T(8,128)(2,1)}, bf16[1280,384]{1,0:T(8,128)(2,1)}, u32[]{:S(2)}, u32[]{:S(2)}) collective-permute-start(bf16[1280,384]{1,0:T(8,128)(2,1)} %collective-permute-done.6.refs_0_), channel_id=1, source_target_pairs={{0,16},{16,0},{1,17},{17,1},{2,18},{18,2},{3,19},{19,3},{4,20},{20... | collective-permute-start | bytes 2949128 | tf_op jit(solution)/shard_map/ppermute | solution.py:571
  60.6 24.7 %collective-permute-start.14 = (bf16[768,640]{1,0:T(8,128)(2,1)}, bf16[768,640]{1,0:T(8,128)(2,1)S(1)}, u32[]{:S(2)}, u32[]{:S(2)}) collective-permute-start(bf16[768,640]{1,0:T(8,128)(2,1)} %get-tuple-element.123), channel_id=1, source_target_pairs={{0,4},{17,20},{2,0},{19,16},{4,5},{21,21},{6,1},{23,17},{8,14},{25... | collective-permute-start | bytes 2949128 | tf_op jit(solution)/shard_map/ppermute | solution.py:598
  73.7 29.6 %collective-permute-start.16 = (bf16[2,768,128]{2,1,0:T(8,128)(2,1)}, bf16[2,768,128]{2,1,0:T(8,128)(2,1)}, u32[]{:S(2)}, u32[]{:S(2)}) collective-permute-start(bf16[2,768,128]{2,1,0:T(8,128)(2,1)} %attend.3.refs_0_), channel_id=1, source_target_pairs={{0,2},{1,3},{2,0},{3,1},{4,6},{5,7},{6,4},{7,5},{8,10},{9,11},{10,... | collective-permute-start | bytes 1179656 | tf_op jit(solution)/shard_map/ppermute | solution.py:571
  76.6 39.0 %collective-permute-start.17 = (bf16[2,768,128]{2,1,0:T(8,128)(2,1)}, bf16[2,768,128]{2,1,0:T(8,128)(2,1)S(1)}, u32[]{:S(2)}, u32[]{:S(2)}) collective-permute-start(bf16[2,768,128]{2,1,0:T(8,128)(2,1)} %attend.3.refs_0_), channel_id=1, source_target_pairs={{0,1},{1,0},{2,3},{3,2},{4,5},{5,4},{6,7},{7,6},{8,9},{9,8},{10,11... | collective-permute-start | bytes 1179656 | tf_op jit(solution)/shard_map/ppermute | solution.py:571
  82.4 37.6 %collective-permute-start.18 = (bf16[2,768,128]{2,1,0:T(8,128)(2,1)S(1)}, bf16[2,768,128]{2,1,0:T(8,128)(2,1)S(1)}, u32[]{:S(2)}, u32[]{:S(2)}) collective-permute-start(bf16[2,768,128]{2,1,0:T(8,128)(2,1)S(1)} %copy-done.27), channel_id=1, source_target_pairs={{0,3},{1,2},{2,1},{3,0},{4,7},{5,6},{6,5},{7,4},{8,11},{9,10},{10,... | collective-permute-start | bytes 1179656 | tf_op jit(solution)/shard_map/ppermute | solution.py:571
  83.9 36.0 %collective-permute-start.11 = (bf16[768,640]{1,0:T(8,128)(2,1)S(1)}, bf16[768,640]{1,0:T(8,128)(2,1)S(1)}, u32[]{:S(2)}, u32[]{:S(2)}) collective-permute-start(bf16[768,640]{1,0:T(8,128)(2,1)S(1)} %collective-permute-done.10), channel_id=1, source_target_pairs={{0,8},{1,9},{4,12},{5,13},{10,2},{11,3},{14,6},{15,7},{16,24},{17,... | collective-permute-start | bytes 2949128 | tf_op jit(solution)/shard_map/ppermute | solution.py:590
  85.2 34.7 %collective-permute-start.15 = (bf16[1280,384]{1,0:T(8,128)(2,1)}, bf16[1280,384]{1,0:T(8,128)(2,1)}, u32[]{:S(2)}, u32[]{:S(2)}) collective-permute-start(bf16[1280,384]{1,0:T(8,128)(2,1)} %copy-done.17), channel_id=1, source_target_pairs={{0,16},{16,0},{1,17},{17,1},{2,18},{18,2},{3,19},{19,3},{4,20},{20... | collective-permute-start | bytes 2949128 | tf_op jit(solution)/shard_map/ppermute | solution.py:571
  120.0 21.9 %collective-permute-start.22 = (bf16[2,768,128]{2,1,0:T(8,128)(2,1)}, bf16[2,768,128]{2,1,0:T(8,128)(2,1)S(1)}, u32[]{:S(2)}, u32[]{:S(2)}) collective-permute-start(bf16[2,768,128]{2,1,0:T(8,128)(2,1)} %attend.4.refs_0_), channel_id=1, source_target_pairs={{0,2},{1,3},{2,0},{3,1},{4,6},{5,7},{6,4},{7,5},{8,10},{9,11},{10,... | collective-permute-start | bytes 1179656 | tf_op jit(solution)/shard_map/ppermute | solution.py:571
  120.0 29.1 %collective-permute-start.23 = (bf16[2,768,128]{2,1,0:T(8,128)(2,1)}, bf16[2,768,128]{2,1,0:T(8,128)(2,1)}, u32[]{:S(2)}, u32[]{:S(2)}) collective-permute-start(bf16[2,768,128]{2,1,0:T(8,128)(2,1)} %attend.4.refs_0_), channel_id=1, source_target_pairs={{0,1},{1,0},{2,3},{3,2},{4,5},{5,4},{6,7},{7,6},{8,9},{9,8},{10,11... | collective-permute-start | bytes 1179656 | tf_op jit(solution)/shard_map/ppermute | solution.py:571
  124.0 33.5 %collective-permute-start.24 = (bf16[2,768,128]{2,1,0:T(8,128)(2,1)}, bf16[2,768,128]{2,1,0:T(8,128)(2,1)}, u32[]{:S(2)}, u32[]{:S(2)}) collective-permute-start(bf16[2,768,128]{2,1,0:T(8,128)(2,1)} %attend.4.refs_0_), channel_id=1, source_target_pairs={{0,3},{1,2},{2,1},{3,0},{4,7},{5,6},{6,5},{7,4},{8,11},{9,10},{10,... | collective-permute-start | bytes 1179656 | tf_op jit(solution)/shard_map/ppermute | solution.py:571
  124.1 33.3 %collective-permute-start.21 = (bf16[768,640]{1,0:T(8,128)(2,1)S(1)}, bf16[768,640]{1,0:T(8,128)(2,1)S(1)}, u32[]{:S(2)}, u32[]{:S(2)}) collective-permute-start(bf16[768,640]{1,0:T(8,128)(2,1)S(1)} %broadcast_select_fusion.3.refs_6_), channel_id=1, source_target_pairs={{0,16},{16,0},{1,17},{17,1},{2,18},{18,2},{3,19},{19,3},{4,20},{20... | collective-permute-start | bytes 2949128 | tf_op jit(solution)/shard_map/ppermute | solution.py:571
  128.1 30.4 %collective-permute-start.20 = (bf16[768,640]{1,0:T(8,128)(2,1)S(1)}, bf16[768,640]{1,0:T(8,128)(2,1)S(1)}, u32[]{:S(2)}, u32[]{:S(2)}) collective-permute-start(bf16[768,640]{1,0:T(8,128)(2,1)S(1)} %copy-done.6), channel_id=1, source_target_pairs={{0,8},{1,9},{4,12},{5,13},{10,2},{11,3},{14,6},{15,7},{16,24},{17,... | collective-permute-start | bytes 2949128 | tf_op jit(solution)/shard_map/ppermute | solution.py:590
  158.6 38.1 %collective-permute-start.29 = (bf16[768,640]{1,0:T(8,128)(2,1)S(1)}, bf16[768,640]{1,0:T(8,128)(2,1)S(1)}, u32[]{:S(2)}, u32[]{:S(2)}) collective-permute-start(bf16[768,640]{1,0:T(8,128)(2,1)S(1)} %broadcast_select_fusion.1), channel_id=1, source_target_pairs={{0,8},{4,12},{1,9},{5,13},{2,10},{6,14},{3,11},{7,15},{16,24},{20,... | collective-permute-start | bytes 2949128 | tf_op jit(solution)/shard_map/ppermute | solution.py:649
  160.2 36.6 %collective-permute-start.28 = (bf16[768,640]{1,0:T(8,128)(2,1)S(1)}, bf16[768,640]{1,0:T(8,128)(2,1)}, u32[]{:S(2)}, u32[]{:S(2)}) collective-permute-start(bf16[768,640]{1,0:T(8,128)(2,1)S(1)} %broadcast_select_fusion.2.refs_8_), channel_id=1, source_target_pairs={{0,16},{16,0},{1,17},{17,1},{2,18},{18,2},{3,19},{19,3},{4,20},{20... | collective-permute-start | bytes 2949128 | tf_op jit(solution)/shard_map/ppermute | solution.py:571
  160.3 18.0 %collective-permute-start.25 = (bf16[2,768,128]{2,1,0:T(8,128)(2,1)S(1)}, bf16[2,768,128]{2,1,0:T(8,128)(2,1)S(1)}, u32[]{:S(2)}, u32[]{:S(2)}) collective-permute-start(bf16[2,768,128]{2,1,0:T(8,128)(2,1)S(1)} %copy-done.30), channel_id=1, source_target_pairs={{0,2},{1,3},{2,0},{3,1},{4,6},{5,7},{6,4},{7,5},{8,10},{9,11},{10,... | collective-permute-start | bytes 1179656 | tf_op jit(solution)/shard_map/ppermute | solution.py:571
  160.4 21.9 %collective-permute-start.26 = (bf16[2,768,128]{2,1,0:T(8,128)(2,1)S(1)}, bf16[2,768,128]{2,1,0:T(8,128)(2,1)S(1)}, u32[]{:S(2)}, u32[]{:S(2)}) collective-permute-start(bf16[2,768,128]{2,1,0:T(8,128)(2,1)S(1)} %copy-done.30), channel_id=1, source_target_pairs={{0,1},{1,0},{2,3},{3,2},{4,5},{5,4},{6,7},{7,6},{8,9},{9,8},{10,11... | collective-permute-start | bytes 1179656 | tf_op jit(solution)/shard_map/ppermute | solution.py:571
  163.9 32.9 %collective-permute-start.27 = (bf16[2,768,128]{2,1,0:T(8,128)(2,1)S(1)}, bf16[2,768,128]{2,1,0:T(8,128)(2,1)S(1)}, u32[]{:S(2)}, u32[]{:S(2)}) collective-permute-start(bf16[2,768,128]{2,1,0:T(8,128)(2,1)S(1)} %copy-done.30), channel_id=1, source_target_pairs={{0,3},{1,2},{2,1},{3,0},{4,7},{5,6},{6,5},{7,4},{8,11},{9,10},{10,... | collective-permute-start | bytes 1179656 | tf_op jit(solution)/shard_map/ppermute | solution.py:571
  (52 other events, 526.2 us)

commit v4 on v3

--- a/solution.py
+++ b/solution.py
@@ -13,7 +13,7 @@
 COST = 1e6
 VMEM_LIMIT = 56 * 2**20
 ANY = pl.BlockSpec(memory_space=pltpu.HBM)
-SMEM = pl.BlockSpec(memory_space=pltpu.SMEM)
+FREE = pl.BlockSpec(memory_space=pl.ANY)
 VMEM = pl.BlockSpec(memory_space=pltpu.VMEM)
 
 
@@ -376,9 +376,17 @@
     )(hidden, beside, acc, qg.reshape(1, -1), kg.reshape(1, -1), *pieces)
 
 
-def bundle_kernel(*refs):
-    pieces, (out, buf, sems) = refs[:4], refs[4:]
-    copies = move(pieces, [buf.at[d] for d in range(4)], sems.at[pl.ds(0, 4)])
+def bundle_kernel(count, *refs):
+    pieces, (out, buf, sems) = refs[:count], refs[count:]
+    copies = move(pieces[:3], [buf.at[d] for d in range(3)], sems.at[pl.ds(0, 3)])
+    copies.append(pltpu.make_async_copy(pieces[3], buf.at[3], sems.at[3]))
+    if count == 4:
+        copies[3].start()
+    else:
+        _, _, z, _ = here()
+        inner = jnp.logical_or(z == 1, z == 2)
+        pl.when(inner)(copies[3].start)
+        pl.when(jnp.logical_not(inner))(pltpu.make_async_copy(pieces[4], buf.at[3], sems.at[3]).start)
     for d, copy in enumerate(copies):
         copy.wait()
         pltpu.make_async_copy(buf.at[d], out.at[d], sems.at[4 + d]).start()
@@ -389,8 +397,8 @@
 def bundle(*pieces):
     shape = (4, *pieces[0].shape)
     return pl.pallas_call(
-        bundle_kernel,
-        in_specs=[ANY] * 4,
+        functools.partial(bundle_kernel, len(pieces)),
+        in_specs=[ANY] * len(pieces),
         out_specs=ANY,
         out_shape=jax.ShapeDtypeStruct(shape, pieces[0].dtype),
         scratch_shapes=[pltpu.VMEM(shape, pieces[0].dtype), pltpu.SemaphoreType.DMA((8,))],
@@ -401,8 +409,9 @@
 
 
 def out_kernel(chunks, top, gate_own, gate_par, *refs):
-    mine, theirs, pieces = refs[:chunks], refs[chunks : 2 * chunks], refs[2 * chunks : 2 * chunks + 4]
-    terms, total, att, w, asems, wsems = refs[2 * chunks + 4 :]
+    mine, theirs, refs = refs[: chunks - 1], refs[chunks - 1 : 2 * chunks - 2], refs[2 * chunks - 2 :]
+    last_mine, last_theirs, pieces = refs[:4], refs[4:8], refs[8:12]
+    terms, total, att, w, asems, wsems = refs[12:]
     devices, _, rows, _ = att.shape
     group, _, plane, core = here()
     span = slice(top, top + rows)
@@ -410,11 +419,12 @@
     for d in range(devices):
         pairs = []
         for j in range(chunks):
+            got, given = (mine[j].at[d], theirs[j].at[d]) if j < chunks - 1 else (last_mine[d], last_theirs[d])
             at = pl.multiple_of(core * (chunks * HD) + j * HD, HD)
-            pairs.append((mine[j].at[d, :, span, :], att.at[d, :, :, pl.ds(at, HD)]))
+            pairs.append((got.at[:, span, :], att.at[d, :, :, pl.ds(at, HD)]))
             at = pl.multiple_of((1 - core) * (chunks * HD) + j * HD, HD)
             for i in range(2):
-                pairs.append((theirs[j].at[d, 1 - i, span, :], att.at[d, i, :, pl.ds(at, HD)]))
+                pairs.append((given.at[1 - i, span, :], att.at[d, i, :, pl.ds(at, HD)]))
         waits.append([pltpu.make_async_copy(a, b, asems.at[3 * chunks * d + n]) for n, (a, b) in enumerate(pairs)])
     wcopies = []
     for d in range(devices):
@@ -445,13 +455,13 @@
     total[...] = (terms[0] + terms[1]).astype(total.dtype)
 
 
-def out_projection(top, count, gate_own, gate_par, mine, theirs, pieces):
-    chunks = len(mine)
+def out_projection(top, count, gate_own, gate_par, mine, theirs, last_mine, last_theirs, pieces):
+    chunks = len(mine) + 1
     devices = mine[0].shape[0]
     deep, share = pieces[0].shape
     return pl.pallas_call(
         functools.partial(out_kernel, chunks, top),
-        in_specs=[VMEM, VMEM] + [ANY] * (2 * chunks + 4),
+        in_specs=[VMEM, VMEM] + [FREE] * (2 * chunks + 10),
         out_specs=[VMEM, VMEM],
         out_shape=[
             jax.ShapeDtypeStruct((2, count, share), jnp.float32),
@@ -466,15 +476,15 @@
         compiler_params=params(),
         cost_estimate=cost(12),
         name="out_projection",
-    )(gate_own, gate_par, *mine, *theirs, *pieces)
-
-
-def close_kernel(terms, carry, start, own, par, mine, send, squares):
-    _, _, _, core = here()
+    )(gate_own, gate_par, *mine, *theirs, *last_mine, *last_theirs, *pieces)
+
+
+def close_kernel(terms, carry, far, own, par, mine, send, squares):
+    _, t, _, core = here()
     first = core == 0
     low = jnp.where(first, own[...], par[...]).astype(jnp.float32)
     high = jnp.where(first, par[...], own[...]).astype(jnp.float32)
-    at_low = start[...].astype(jnp.float32) + carry[...].astype(jnp.float32)
+    at_low = jnp.where(t < 2, low, far[...].astype(jnp.float32)) + carry[...].astype(jnp.float32)
     at_high = at_low + terms[0]
     end = at_high + terms[1]
     mine[...] = jnp.where(first, at_high, end)
@@ -491,7 +501,7 @@
             squares[n : n + 1, :] += part
 
 
-def close(top, terms, carry, start, own, par):
+def close(top, terms, carry, far, own, par):
     _, count, share = terms.shape
     block = 192 if count % 192 == 0 and top % 192 == 0 else count
     skip = top // block
@@ -510,7 +520,7 @@
         compiler_params=params(),
         cost_estimate=cost(8),
         name="close",
-    )(terms, carry, start, own, par)
+    )(terms, carry, far, own, par)
 
 
 def join_kernel(parts, *refs):
@@ -582,6 +592,12 @@
     def along(array, flip):
         return over(array, "tensor", flip)
 
+    def middle(array):
+        return lax.ppermute(array, "tensor", [(1, 2), (2, 1)])
+
+    def outward(array):
+        return lax.ppermute(array, "tensor", [(1, 0), (2, 3)])
+
     def place(group, step, tensor):
         return (group * 4 + step) * devices + tensor
 
@@ -606,69 +622,69 @@
 
     y0 = far(p0)
     z0 = over(r0, "tm", 3)
-    hidden = fast_hidden(states, make_scale(stamp, mod_scale))
-    s1, s2, o0, o1 = packs(weights, others, w_out)
-    y0, z0, hidden, s1, s2, o0, o1, states, own_step, par_step = phase(
-        y0, z0, hidden, s1, s2, o0, o1, states, own_step, par_step
-    )
-
-    beside = partner(hidden)
-    y1, x0, xz0, sent0 = far(s1), swap(y0), swap(z0), to_plane(0, o0)
-    acc = near(hidden, beside, (*weights, *others))
-    y1, x0, xz0, acc, beside, s2, o1, sent0, states = phase(y1, x0, xz0, acc, beside, s2, o1, sent0, states)
-
-    x1, y2, sent1 = swap(y1), far(s2), to_plane(1, o1)
-    att0 = attend(0, hidden, beside, acc, 0, (y0, z0, x0, xz0), query_gain, key_gain)
-    att0, states = phase(att0, states)
-    two0, one0 = along(att0, 2), along(att0, 1)
     base = z * (2 * share)
     lat_own = lax.dynamic_slice_in_dim(states[0], base + core * share, share, 1)
     lat_give = lax.dynamic_slice_in_dim(states[0], base + (1 - core) * share, share, 1)
-    y2, x1, sent1, acc, lat_own, lat_give = phase(y2, x1, sent1, acc, lat_own, lat_give)
-
-    x2, u0, three0 = swap(y2), cross(sent0), along(att0, 3)
     lat_par = partner(lat_give)
-    att1 = attend(1, hidden, beside, acc, 1, (y1, x1), query_gain, key_gain)
-    u0, x2, sent1, att1, two0, one0, three0, lat_own, lat_par = phase(
-        u0, x2, sent1, att1, two0, one0, three0, lat_own, lat_par
+    hidden = fast_hidden(states, make_scale(stamp, mod_scale))
+    s1, s2, o0, o1 = packs(weights, others, w_out)
+    y0, z0, hidden, s1, s2, o0, o1, lat_own, lat_par, own_step, par_step = phase(
+        y0, z0, hidden, s1, s2, o0, o1, lat_own, lat_par, own_step, par_step
     )
 
-    home = chip == z // 2
-    v0 = jnp.where(home, sent0, u0)
-    xv0, u1 = swap(v0), cross(sent1)
-    two1, one1, three1 = along(att1, 2), along(att1, 1), along(att1, 3)
-    att2 = attend(2, hidden, beside, acc, 2, (y2, x2), query_gain, key_gain)
-    u1, xv0, v0, att2, two1, one1, three1, lat_own, lat_par = phase(
-        u1, xv0, v0, att2, two1, one1, three1, lat_own, lat_par
-    )
-
-    two2, one2, three2 = along(att2, 2), along(att2, 1), along(att2, 3)
-    v1 = jnp.where(home, sent1, u1)
-    xv1 = swap(v1)
-    start_near = jnp.where(core == 0, lat_own, lat_par)
-    start_far = lax.ppermute(start_near, "tm", [(0, 2), (1, 3)])
-    g0 = bundle(att0, one0, two0, three0)
-    g1 = bundle(att1, one1, two1, three1)
+    beside = partner(hidden)
+    y1, x0, xz0, sent0, sent1 = far(s1), swap(y0), swap(z0), to_plane(0, o0), to_plane(1, o1)
+    acc = near(hidden, beside, (*weights, *others))
+    y1, x0, xz0, acc, beside, s2, sent0 = phase(y1, x0, xz0, acc, beside, s2, sent0)
+
+    x1, y2 = swap(y1), far(s2)
+    att0 = attend(0, hidden, beside, acc, 0, (y0, z0, x0, xz0), query_gain, key_gain)
+    att0, own_step, par_step, sent1 = phase(att0, own_step, par_step, sent1)
+    two0, one0 = along(att0, 2), along(att0, 1)
     gates = []
     for pair in (own_step, par_step):
         gate = pair[1] * make_gate(pair[0], mod_gate, width)
         gates.append(lax.dynamic_slice_in_dim(gate, core * share, share, 0).reshape(1, share))
-    two2, one2, three2, v1, xv1, start_far, start_near, g0, g1, *gates = phase(
-        two2, one2, three2, v1, xv1, start_far, start_near, g0, g1, *gates
+    y2, x1, acc, *gates = phase(y2, x1, acc, *gates)
+
+    x2, u0, inner0 = swap(y2), cross(sent0), middle(att0)
+    att1 = attend(1, hidden, beside, acc, 1, (y1, x1), query_gain, key_gain)
+    att1, two0, v0 = phase(att1, two0, sent0)
+    outer0, two1 = outward(two0), along(att1, 2)
+    u0, x2, one0, inner0, outer0, v0 = phase(u0, x2, one0, inner0, outer0, v0)
+
+    home = chip == z // 2
+    v0 = jnp.where(home, v0, u0)
+    xv0, u1 = swap(v0), cross(sent1)
+    one1, inner1 = along(att1, 1), middle(att1)
+    att2 = attend(2, hidden, beside, acc, 2, (y2, x2), query_gain, key_gain)
+    two1, att2 = phase(two1, att2)
+    outer1, two2 = outward(two1), along(att2, 2)
+    g0 = bundle(att0, one0, two0, inner0, outer0)
+    u1, xv0, v0, one1, inner1, outer1, g0, lat_own, lat_par, *gates = phase(
+        u1, xv0, v0, one1, inner1, outer1, g0, lat_own, lat_par, *gates
     )
     gate_own, gate_par = gates
 
-    q0, q1 = partner(g0), partner(g1)
-    g2 = bundle(att2, one2, two2, three2)
-    start = jnp.where(chip == 0, start_near, start_far)
-    q0, q1, g2, start = phase(q0, q1, g2, start)
-    q2 = partner(g2)
+    one2, inner2 = along(att2, 1), middle(att2)
+    v1 = jnp.where(home, sent1, u1)
+    xv1 = swap(v1)
+    start_far = lax.ppermute(jnp.where(core == 0, lat_own, lat_par), "tm", [(0, 2), (1, 3)])
+    g1 = bundle(att1, one1, two1, inner1, outer1)
+    two2, one2, inner2, v1, xv1, g1, start_far = phase(two2, one2, inner2, v1, xv1, g1, start_far)
+    outer2 = outward(two2)
+    q0, q1, b0, b1, b2 = partner(g0), partner(g1), partner(att2), partner(one2), partner(two2)
+    outer2, inner2, q0, q1, b0, b1, b2 = phase(outer2, inner2, q0, q1, b0, b1, b2)
+
+    three2 = jnp.where(jnp.logical_or(z == 1, z == 2), inner2, outer2)
+    b3 = partner(three2)
     pieces = [v0, xv0, v1, xv1]
 
     count = rows // 2
 
     def project(top, gate_own):
-        return out_projection(top, count, gate_own, gate_par, [g0, g1, g2], [q0, q1, q2], pieces)
+        mine, theirs = [att2, one2, two2, three2], [b0, b1, b2, b3]
+        return out_projection(top, count, gate_own, gate_par, [g0, g1], [q0, q1], mine, theirs, pieces)
 
     def ahead(total):
         return lax.ppermute(total, "tm", [(0, 2), (1, 3)])
@@ -677,19 +693,18 @@
     terms0, total0, gate_own = phase(terms0, total0, gate_own)
     carry0 = ahead(total0)
     terms1, total1 = project(count, gate_own)
-    terms1, total1, carry0, start = phase(terms1, total1, carry0, start)
+    terms1, total1, carry0 = phase(terms1, total1, carry0)
     carry1 = ahead(total1)
-    own0, send0, squares0 = close(0, terms0, carry0, start, lat_own, lat_par)
-    carry1, own0, send0, squares0, start = phase(carry1, own0, send0, squares0, start)
+    own0, send0, squares0 = close(0, terms0, carry0, start_far, lat_own, lat_par)
+    carry1, own0, send0, squares0 = phase(carry1, own0, send0, squares0)
     given0 = partner(send0)
-    own1, send1, squares1 = close(count, terms1, carry1, start, lat_own, lat_par)
+    own1, send1, squares1 = close(count, terms1, carry1, start_far, lat_own, lat_par)
     given0, own1, send1, squares = phase(given0, own1, send1, squares0 + squares1)
     given1, squares_par = partner(send1), partner(squares)
     given1, squares = phase(given1, squares + squares_par)
     sums = jnp.sum(squares, axis=1)
+    sums = sums + along(sums, 1) + along(sums, 2) + along(sums, 3)
     next_share = join([own0, own1], [given0, given1])
-    sums, next_share = phase(sums, next_share)
-    sums = sums + along(sums, 1) + along(sums, 2) + along(sums, 3)
     errors = (lax.dynamic_slice_in_dim(sums, core, 1, 0) / (rows * width)).reshape(1, 1)
     return (next_share, errors)
 

time: 269 us -> 252 us (0.937)
  waiting for transfers between devices: 89.8 us -> 66.9 us
  starting transfers between devices: 49.4 us -> 58.4 us
  local copies, waits for them, and re-layouts: 12.7 us -> 8.89 us
    ppermute x34, waiting for transfers between devices: 75.1 us -> 26.7 us  [over(): lax.ppermute(array, axis, [(i, i ^ flip) for i in range(lax.axis_size(axi...]
    ppermute x1 -> x7, starting transfers between devices: 1.42 us -> 21.1 us  [the longest x3 13.3 us: middle(): return lax.ppermute(array, 'tensor', [(1, 2), (2, 1)])]
    ppermute x1 -> x7, waiting for transfers between devices: 0.01 us -> 19.3 us  [the longest x3 10.8 us: outward(): return lax.ppermute(array, 'tensor', [(1, 0), (2, 3)])]
    ppermute x34, starting transfers between devices: 40.8 us -> 30.4 us  [over(): lax.ppermute(array, axis, [(i, i ^ flip) for i in range(lax.axis_size(axi...]
    ppermute x2, waiting for transfers between devices: 0.01 us -> 4.23 us  [cross(): return lax.ppermute(array, ('tm', 'tensor'), pairs)]
    unnamed x70 -> x60, local copies, waits for them, and re-layouts: 7.43 us -> 3.58 us
    pallas_call x3 -> x2, Pallas kernels: 6.69 us -> 4.45 us  [bundle(): pl.pallas_call(functools.partial(bundle_kernel, len(pieces)), in_specs=[A...]
  transfers between devices with their start and end apart: 41 -> 47, of which waited for: 19 -> 15; matrix products, arithmetic and copies ran while one was open for 4% -> 5% of each run, Pallas kernels for 35% -> 37%
where the time goes in v4:
time: 252 us; the launch traced here: 248 us
  Pallas kernels  102 us (40%)
  waiting for transfers between devices  66.9 us (27%)
  starting transfers between devices  58.4 us (23%)
  local copies, waits for them, and re-layouts  8.89 us (4%)
  other arithmetic  8.04 us (3%)
  between operations  4.37 us (2%)
    pallas_call x3, Pallas kernels, attend(): pl.pallas_call(functools.partial(attend_kernel, chunk, row, parts), in_sp...  36.8 us
    ppermute x34, starting transfers between devices, over(): lax.ppermute(array, axis, [(i, i ^ flip) for i in range(lax.axis_size(axi...  30.4 us
    ppermute x34, waiting for transfers between devices, over(): lax.ppermute(array, axis, [(i, i ^ flip) for i in range(lax.axis_size(axi...  26.7 us
    pallas_call x2, Pallas kernels, out_projection(): pl.pallas_call(functools.partial(out_kernel, chunks, top), in_specs=[VMEM...  18.1 us
    pallas_call x1, Pallas kernels, near(): pl.pallas_call(near_kernel, in_specs=[ANY] * 8, out_specs=ANY, out_shape=...  17.9 us
    ppermute x2, waiting for transfers between devices, ahead(): return lax.ppermute(total, 'tm', [(0, 2), (1, 3)])  16.7 us
    ppermute x3, starting transfers between devices, middle(): return lax.ppermute(array, 'tensor', [(1, 2), (2, 1)])  13.3 us
    ppermute x3, waiting for transfers between devices, outward(): return lax.ppermute(array, 'tensor', [(1, 0), (2, 3)])  10.8 us
  transfers between devices with their start and end apart: 47, of which 15 were waited for; matrix products, arithmetic and copies ran while one was open for 5% of the time, Pallas kernels for 37%

profile of v4, /device:TPU:12, one launch (start us, length us, event | category | flops | bytes accessed | tf_op | source)
XLA Modules:
  0.0 248.4 jit_solution(11807445640551774493)
XLA Ops:
  9.4 8.9 %hidden.1.h_own = bf16[768,5120]{1,0:T(8,128)(2,1)} custom-call(bf16[1,768,5120]{2,1,0:T(8,128)(2,1)} %latent, f32[1,5120]{1,0:T(1,128)} %bitcast.11), custom_call_target="tpu_custom_call" | custom-call | flops 5000000000 | bytes 1024 | tf_op jit(solution)/shard_map/hidden/pallas_call | solution.py:121
  19.1 3.5 %packs.1 = (bf16[1280,384]{1,0:T(8,128)(2,1)}, bf16[1280,384]{1,0:T(8,128)(2,1)}, bf16[768,640]{1,0:T(8,128)(2,1)}, bf16[768,640]{1,0:T(8,128)(2,1)}) custom-call(bf16[1280,768]{1,0:T(8,128)(2,1)} %wq.5, bf16[1280,768]{1,0:T(8,128)(2,1)} %wk.5, bf16[1280,768]{1,0:T(8,128)(2,1)} %wv.5, bf16[1280,768]{1,0:T(8,128)(2,1)} %copy-done.1, ...), custom_call_target="tpu_custom_call" | custom-call | flops 1000000000 | bytes 1024 | tf_op jit(solution)/shard_map/packs/pallas_call | solution.py:225
  22.6 6.1 %collective-permute-done.1.refs_1_ = bf16[640,384]{1,0:T(8,128)(2,1)S(1)} collective-permute-done((bf16[640,384]{1,0:T(8,128)(2,1)S(1)}, bf16[640,384]{1,0:T(8,128)(2,1)S(1)}, u32[]{:S(2)}, u32[]{:S(2)}) %collective-permute-start.1) | collective-permute-done | bytes 491552 | tf_op jit(solution)/shard_map/ppermute | solution.py:581
  32.4 3.3 %collective-permute-start.8 = (bf16[640,384]{1,0:T(8,128)(2,1)S(1)}, bf16[640,384]{1,0:T(8,128)(2,1)S(1)}, u32[]{:S(2)}, u32[]{:S(2)}) collective-permute-start(bf16[640,384]{1,0:T(8,128)(2,1)S(1)} %collective-permute-done.refs_0_), channel_id=1, source_target_pairs={{0,16},{16,0},{1,17},{17,1},{2,18},{18,2},{3,19},{19,3},{4,20},{20... | collective-permute-start | bytes 1474568 | tf_op jit(solution)/shard_map/ppermute | solution.py:581
  35.7 6.0 %collective-permute-done.10.h_par = bf16[768,5120]{1,0:T(8,128)(2,1)} collective-permute-done((bf16[768,5120]{1,0:T(8,128)(2,1)}, bf16[768,5120]{1,0:T(8,128)(2,1)}, u32[]{:S(2)}, u32[]{:S(2)}) %collective-permute-start.10) | collective-permute-done | bytes 7864352 | tf_op jit(solution)/shard_map/ppermute | solution.py:581
  42.6 17.9 %near.1.acc = f32[3,2,768,384]{3,2,1,0:T(8,128)} custom-call(bf16[768,5120]{1,0:T(8,128)(2,1)} %hidden.1.h_own, bf16[768,5120]{1,0:T(8,128)(2,1)} %collective-permute-done.10.h_par, bf16[1280,768]{1,0:T(8,128)(2,1)} %wq.5, bf16[1280,768]{1,0:T(8,128)(2,1)} %wk.5, bf16[1280,768]{1,0:T(8,128)(2,1)} %wv.5, bf16[1280,768]{1,0:T(8,128)(2,1)} %copy-done.1, ...), custom_call_target="tpu_custom_call" | custom-call | flops 10000000000 | bytes 1024 | tf_op jit(solution)/shard_map/near/pallas_call | solution.py:282
  61.8 3.3 %collective-permute-start.16 = (bf16[1280,384]{1,0:T(8,128)(2,1)}, bf16[1280,384]{1,0:T(8,128)(2,1)S(1)}, u32[]{:S(2)}, u32[]{:S(2)}) collective-permute-start(bf16[1280,384]{1,0:T(8,128)(2,1)} %collective-permute-done.7.refs_0_), channel_id=1, source_target_pairs={{0,16},{16,0},{1,17},{17,1},{2,18},{18,2},{3,19},{19,3},{4,20},{20... | collective-permute-start | bytes 2949128 | tf_op jit(solution)/shard_map/ppermute | solution.py:581
  65.1 12.3 %attend.3.refs_0_ = bf16[2,768,128]{2,1,0:T(8,128)(2,1)} custom-call(bf16[768,5120]{1,0:T(8,128)(2,1)} %hidden.1.h_own, bf16[768,5120]{1,0:T(8,128)(2,1)} %collective-permute-done.10.h_par, f32[3,2,768,384]{3,2,1,0:T(8,128)} %near.1.acc, f32[1,768]{1,0:T(1,128)} %reshape.31.qg, f32[1,768]{1,0:T(1,128)} %reshape.32.kg, bf16[640,384]{1,0:T(8,128)(2,1)} %copy-done.17, ...), custom_call_target="tpu_custom_call" | custom-call | flops 12000000000 | bytes 1024 | tf_op jit(solution)/shard_map/attend/pallas_call | solution.py:360
  79.1 3.7 %collective-permute-start.19 = (bf16[2,768,128]{2,1,0:T(8,128)(2,1)}, bf16[2,768,128]{2,1,0:T(8,128)(2,1)}, u32[]{:S(2)}, u32[]{:S(2)}) collective-permute-start(bf16[2,768,128]{2,1,0:T(8,128)(2,1)} %attend.3.refs_0_), channel_id=1, source_target_pairs={{1,2},{2,1},{5,6},{6,5},{9,10},{10,9},{13,14},{14,13},{17,18},{18,... | collective-permute-start | bytes 1179656 | tf_op jit(solution)/shard_map/ppermute | solution.py:596
  91.1 12.2 %attend.4.refs_0_ = bf16[2,768,128]{2,1,0:T(8,128)(2,1)} custom-call(bf16[768,5120]{1,0:T(8,128)(2,1)} %hidden.1.h_own, bf16[768,5120]{1,0:T(8,128)(2,1)} %collective-permute-done.10.h_par, f32[3,2,768,384]{3,2,1,0:T(8,128)} %near.1.acc, f32[1,768]{1,0:T(1,128)} %reshape.31.qg, f32[1,768]{1,0:T(1,128)} %reshape.32.kg, ...), custom_call_target="tpu_custom_call" | custom-call | flops 12000000000 | bytes 1024 | tf_op jit(solution)/shard_map/attend/pallas_call | solution.py:360
  103.4 3.5 %collective-permute-start.21 = (bf16[2,768,128]{2,1,0:T(8,128)(2,1)S(1)}, bf16[2,768,128]{2,1,0:T(8,128)(2,1)}, u32[]{:S(2)}, u32[]{:S(2)}) collective-permute-start(bf16[2,768,128]{2,1,0:T(8,128)(2,1)S(1)} %collective-permute-done.20.refs_2_), channel_id=1, source_target_pairs={{1,0},{2,3},{5,4},{6,7},{9,8},{10,11},{13,12},{14,15},{17,16},{18,... | collective-permute-start | bytes 1179656 | tf_op jit(solution)/shard_map/ppermute | solution.py:599
  109.5 4.2 %collective-permute-done.14 = bf16[768,640]{1,0:T(8,128)(2,1)} collective-permute-done((bf16[768,640]{1,0:T(8,128)(2,1)S(1)}, bf16[768,640]{1,0:T(8,128)(2,1)}, u32[]{:S(2)}, u32[]{:S(2)}) %collective-permute-start.14) | collective-permute-done | bytes 983072 | tf_op jit(solution)/shard_map/ppermute | solution.py:606
  116.6 6.4 %collective-permute-start.24 = (bf16[2,768,128]{2,1,0:T(8,128)(2,1)}, bf16[2,768,128]{2,1,0:T(8,128)(2,1)}, u32[]{:S(2)}, u32[]{:S(2)}) collective-permute-start(bf16[2,768,128]{2,1,0:T(8,128)(2,1)} %attend.4.refs_0_), channel_id=1, source_target_pairs={{1,2},{2,1},{5,6},{6,5},{9,10},{10,9},{13,14},{14,13},{17,18},{18,... | collective-permute-start | bytes 1179656 | tf_op jit(solution)/shard_map/ppermute | solution.py:596
  126.1 12.4 %attend.5.refs_4_ = bf16[2,768,128]{2,1,0:T(8,128)(2,1)} custom-call(bf16[768,5120]{1,0:T(8,128)(2,1)} %hidden.1.h_own, bf16[768,5120]{1,0:T(8,128)(2,1)} %collective-permute-done.10.h_par, f32[3,2,768,384]{3,2,1,0:T(8,128)} %near.1.acc, f32[1,768]{1,0:T(1,128)} %reshape.31.qg, f32[1,768]{1,0:T(1,128)} %reshape.32.kg, ...), custom_call_target="tpu_custom_call" | custom-call | flops 12000000000 | bytes 1024 | tf_op jit(solution)/shard_map/attend/pallas_call | solution.py:360
  142.0 3.3 %collective-permute-done.26.refs_4_ = bf16[2,768,128]{2,1,0:T(8,128)(2,1)S(1)} collective-permute-done((bf16[2,768,128]{2,1,0:T(8,128)(2,1)}, bf16[2,768,128]{2,1,0:T(8,128)(2,1)S(1)}, u32[]{:S(2)}, u32[]{:S(2)}) %collective-permute-start.26) | collective-permute-done | bytes 393248 | tf_op jit(solution)/shard_map/ppermute | solution.py:599
  157.6 8.6 %collective-permute-done.27.refs_6_ = bf16[2,768,128]{2,1,0:T(8,128)(2,1)} collective-permute-done((bf16[2,768,128]{2,1,0:T(8,128)(2,1)S(1)}, bf16[2,768,128]{2,1,0:T(8,128)(2,1)}, u32[]{:S(2)}, u32[]{:S(2)}) %collective-permute-start.27) | collective-permute-done | bytes 393248 | tf_op jit(solution)/shard_map/ppermute | solution.py:581
  167.1 8.5 %collective-permute-done.29 = bf16[2,768,128]{2,1,0:T(8,128)(2,1)S(1)} collective-permute-done((bf16[2,768,128]{2,1,0:T(8,128)(2,1)S(1)}, bf16[2,768,128]{2,1,0:T(8,128)(2,1)S(1)}, u32[]{:S(2)}, u32[]{:S(2)}) %collective-permute-start.29) | collective-permute-done | bytes 393248 | tf_op jit(solution)/shard_map/ppermute | solution.py:596
  180.6 6.9 %collective-permute-done.32 = bf16[2,768,128]{2,1,0:T(8,128)(2,1)S(1)} collective-permute-done((bf16[2,768,128]{2,1,0:T(8,128)(2,1)}, bf16[2,768,128]{2,1,0:T(8,128)(2,1)S(1)}, u32[]{:S(2)}, u32[]{:S(2)}) %collective-permute-start.32) | collective-permute-done | bytes 393248 | tf_op jit(solution)/shard_map/ppermute | solution.py:599
  190.2 8.9 %out_projection.2 = (f32[2,384,640]{2,1,0:T(8,128)}, bf16[384,640]{1,0:T(8,128)(2,1)}) custom-call(f32[1,640]{1,0:T(1,128)} %reshape.33.gate_own, f32[1,640]{1,0:T(1,128)} %reshape.34.gate_par, bf16[4,2,768,128]{3,2,1,0:T(8,128)(2,1)} %bundle.2.refs_0_, bf16[4,2,768,128]{3,2,1,0:T(8,128)(2,1)} %bundle.3.refs_1_, ...), custom_call_target="tpu_custom_call" | custom-call | flops 12000000000 | bytes 1024 | tf_op jit(solution)/shard_map/out_projection/pallas_call | solution.py:462
  200.4 9.2 %out_projection.3 = (f32[2,384,640]{2,1,0:T(8,128)}, bf16[384,640]{1,0:T(8,128)(2,1)}) custom-call(f32[1,640]{1,0:T(1,128)} %reshape.33.gate_own, f32[1,640]{1,0:T(1,128)} %reshape.34.gate_par, bf16[4,2,768,128]{3,2,1,0:T(8,128)(2,1)} %bundle.2.refs_0_, bf16[4,2,768,128]{3,2,1,0:T(8,128)(2,1)} %bundle.3.refs_1_, ...), custom_call_target="tpu_custom_call" | custom-call | flops 12000000000 | bytes 1024 | tf_op jit(solution)/shard_map/out_projection/pallas_call | solution.py:462
  209.6 6.5 %collective-permute-done.39.carry = bf16[384,640]{1,0:T(8,128)(2,1)S(1)} collective-permute-done((bf16[384,640]{1,0:T(8,128)(2,1)}, bf16[384,640]{1,0:T(8,128)(2,1)S(1)}, u32[]{:S(2)}, u32[]{:S(2)}) %collective-permute-start.39) | collective-permute-done | bytes 491552 | tf_op jit(solution)/shard_map/ppermute | solution.py:690
  217.5 3.4 %close.2 = (f32[384,640]{1,0:T(8,128)}, f32[384,640]{1,0:T(8,128)}, f32[2,640]{1,0:T(2,128)}) custom-call(f32[2,384,640]{2,1,0:T(8,128)} %get-tuple-element.180.terms, bf16[384,640]{1,0:T(8,128)(2,1)} %copy-done.23, bf16[768,640]{1,0:T(8,128)(2,1)} %copy-done.10, bf16[768,640]{1,0:T(8,128)(2,1)} %copy-done, bf16[768,640]{1,0:T(8,128)(2,1)} %collective-permute-done.5.par), custom_call_target="tpu_custom_call" | custom-call | flops 8000000000 | bytes 1024 | tf_op jit(solution)/shard_map/close/pallas_call | solution.py:510
  220.8 10.2 %collective-permute-done.40.carry = bf16[384,640]{1,0:T(8,128)(2,1)S(1)} collective-permute-done((bf16[384,640]{1,0:T(8,128)(2,1)}, bf16[384,640]{1,0:T(8,128)(2,1)S(1)}, u32[]{:S(2)}, u32[]{:S(2)}) %collective-permute-start.40) | collective-permute-done | bytes 491552 | tf_op jit(solution)/shard_map/ppermute | solution.py:690
  231.8 3.3 %close.3 = (f32[384,640]{1,0:T(8,128)}, f32[384,640]{1,0:T(8,128)}, f32[2,640]{1,0:T(2,128)}) custom-call(f32[2,384,640]{2,1,0:T(8,128)} %get-tuple-element.188.terms, bf16[384,640]{1,0:T(8,128)(2,1)} %copy-done.24, bf16[768,640]{1,0:T(8,128)(2,1)} %copy-done.10, bf16[768,640]{1,0:T(8,128)(2,1)} %copy-done, bf16[768,640]{1,0:T(8,128)(2,1)} %collective-permute-done.5.par), custom_call_target="tpu_custom_call" | custom-call | flops 8000000000 | bytes 1024 | tf_op jit(solution)/shard_map/close/pallas_call | solution.py:510
  (163 shorter events, 71.6 us)
Async XLA Ops:
  1.2 17.9 %collective-permute-start.4 = (bf16[1280,768]{1,0:T(8,128)(2,1)}, bf16[1280,768]{1,0:T(8,128)(2,1)}, u32[]{:S(2)}, u32[]{:S(2)}) collective-permute-start(bf16[1280,768]{1,0:T(8,128)(2,1)} %wv.5), channel_id=1, source_target_pairs={{0,4},{4,0},{8,12},{12,8},{1,5},{5,1},{9,13},{13,9},{2,6},{6,2},{1... | collective-permute-start | bytes 5898248 | tf_op jit(solution)/shard_map/ppermute | solution.py:581
  5.3 23.4 %collective-permute-start.5 = (bf16[768,640]{1,0:T(8,128)(2,1)S(1)}, bf16[768,640]{1,0:T(8,128)(2,1)}, u32[]{:S(2)}, u32[]{:S(2)}) collective-permute-start(bf16[768,640]{1,0:T(8,128)(2,1)S(1)} %get-tuple-element.200), channel_id=1, source_target_pairs={{0,4},{4,0},{8,12},{12,8},{1,5},{5,1},{9,13},{13,9},{2,6},{6,2},{1... | collective-permute-start | bytes 2949128 | tf_op jit(solution)/shard_map/ppermute | solution.py:581
  8.4 20.3 %collective-permute-start.1 = (bf16[640,384]{1,0:T(8,128)(2,1)S(1)}, bf16[640,384]{1,0:T(8,128)(2,1)S(1)}, u32[]{:S(2)}, u32[]{:S(2)}) collective-permute-start(bf16[640,384]{1,0:T(8,128)(2,1)S(1)} %copy-done.19), channel_id=1, source_target_pairs={{0,12},{4,8},{8,4},{12,0},{1,13},{5,9},{9,5},{13,1},{2,14},{6,10},... | collective-permute-start | bytes 1474568 | tf_op jit(solution)/shard_map/ppermute | solution.py:581
  29.4 31.3 %collective-permute-start.11 = (bf16[768,640]{1,0:T(8,128)(2,1)}, bf16[768,640]{1,0:T(8,128)(2,1)S(1)}, u32[]{:S(2)}, u32[]{:S(2)}) collective-permute-start(bf16[768,640]{1,0:T(8,128)(2,1)} %get-tuple-element.116), channel_id=1, source_target_pairs={{0,0},{17,16},{2,4},{19,20},{4,1},{21,17},{6,5},{23,21},{8,10},{25... | collective-permute-start | bytes 2949128 | tf_op jit(solution)/shard_map/ppermute | solution.py:614
  30.1 30.5 %collective-permute-start.7 = (bf16[1280,384]{1,0:T(8,128)(2,1)}, bf16[1280,384]{1,0:T(8,128)(2,1)}, u32[]{:S(2)}, u32[]{:S(2)}) collective-permute-start(bf16[1280,384]{1,0:T(8,128)(2,1)} %get-tuple-element.112), channel_id=1, source_target_pairs={{0,8},{4,12},{8,0},{12,4},{1,9},{5,13},{9,1},{13,5},{2,10},{6,14},... | collective-permute-start | bytes 2949128 | tf_op jit(solution)/shard_map/ppermute | solution.py:581
  32.4 28.1 %collective-permute-start.8 = (bf16[640,384]{1,0:T(8,128)(2,1)S(1)}, bf16[640,384]{1,0:T(8,128)(2,1)S(1)}, u32[]{:S(2)}, u32[]{:S(2)}) collective-permute-start(bf16[640,384]{1,0:T(8,128)(2,1)S(1)} %collective-permute-done.refs_0_), channel_id=1, source_target_pairs={{0,16},{16,0},{1,17},{17,1},{2,18},{18,2},{3,19},{19,3},{4,20},{20... | collective-permute-start | bytes 1474568 | tf_op jit(solution)/shard_map/ppermute | solution.py:581
  35.7 24.9 %collective-permute-start.9 = (bf16[640,384]{1,0:T(8,128)(2,1)}, bf16[640,384]{1,0:T(8,128)(2,1)S(1)}, u32[]{:S(2)}, u32[]{:S(2)}) collective-permute-start(bf16[640,384]{1,0:T(8,128)(2,1)} %copy-done.18), channel_id=1, source_target_pairs={{0,16},{16,0},{1,17},{17,1},{2,18},{18,2},{3,19},{19,3},{4,20},{20... | collective-permute-start | bytes 1474568 | tf_op jit(solution)/shard_map/ppermute | solution.py:581
  41.7 35.6 %collective-permute-start.12 = (bf16[768,640]{1,0:T(8,128)(2,1)}, bf16[768,640]{1,0:T(8,128)(2,1)S(1)}, u32[]{:S(2)}, u32[]{:S(2)}) collective-permute-start(bf16[768,640]{1,0:T(8,128)(2,1)} %get-tuple-element.123), channel_id=1, source_target_pairs={{0,4},{17,20},{2,0},{19,16},{4,5},{21,21},{6,1},{23,17},{8,14},{25... | collective-permute-start | bytes 2949128 | tf_op jit(solution)/shard_map/ppermute | solution.py:614
  60.6 26.7 %collective-permute-start.15 = (bf16[1280,384]{1,0:T(8,128)(2,1)S(1)}, bf16[1280,384]{1,0:T(8,128)(2,1)}, u32[]{:S(2)}, u32[]{:S(2)}) collective-permute-start(bf16[1280,384]{1,0:T(8,128)(2,1)S(1)} %copy-done.12), channel_id=1, source_target_pairs={{0,8},{4,12},{8,0},{12,4},{1,9},{5,13},{9,1},{13,5},{2,10},{6,14},... | collective-permute-start | bytes 2949128 | tf_op jit(solution)/shard_map/ppermute | solution.py:581
  61.8 27.0 %collective-permute-start.16 = (bf16[1280,384]{1,0:T(8,128)(2,1)}, bf16[1280,384]{1,0:T(8,128)(2,1)S(1)}, u32[]{:S(2)}, u32[]{:S(2)}) collective-permute-start(bf16[1280,384]{1,0:T(8,128)(2,1)} %collective-permute-done.7.refs_0_), channel_id=1, source_target_pairs={{0,16},{16,0},{1,17},{17,1},{2,18},{18,2},{3,19},{19,3},{4,20},{20... | collective-permute-start | bytes 2949128 | tf_op jit(solution)/shard_map/ppermute | solution.py:581
  77.4 26.0 %collective-permute-start.20 = (bf16[2,768,128]{2,1,0:T(8,128)(2,1)}, bf16[2,768,128]{2,1,0:T(8,128)(2,1)S(1)}, u32[]{:S(2)}, u32[]{:S(2)}) collective-permute-start(bf16[2,768,128]{2,1,0:T(8,128)(2,1)} %attend.3.refs_0_), channel_id=1, source_target_pairs={{0,2},{1,3},{2,0},{3,1},{4,6},{5,7},{6,4},{7,5},{8,10},{9,11},{10,... | collective-permute-start | bytes 1179656 | tf_op jit(solution)/shard_map/ppermute | solution.py:581
  79.1 27.8 %collective-permute-start.18 = (bf16[2,768,128]{2,1,0:T(8,128)(2,1)}, bf16[2,768,128]{2,1,0:T(8,128)(2,1)}, u32[]{:S(2)}, u32[]{:S(2)}) collective-permute-start(bf16[2,768,128]{2,1,0:T(8,128)(2,1)} %attend.3.refs_0_), channel_id=1, source_target_pairs={{0,1},{1,0},{2,3},{3,2},{4,5},{5,4},{6,7},{7,6},{8,9},{9,8},{10,11... | collective-permute-start | bytes 1179656 | tf_op jit(solution)/shard_map/ppermute | solution.py:581
  79.1 29.1 %collective-permute-start.19 = (bf16[2,768,128]{2,1,0:T(8,128)(2,1)}, bf16[2,768,128]{2,1,0:T(8,128)(2,1)}, u32[]{:S(2)}, u32[]{:S(2)}) collective-permute-start(bf16[2,768,128]{2,1,0:T(8,128)(2,1)} %attend.3.refs_0_), channel_id=1, source_target_pairs={{1,2},{2,1},{5,6},{6,5},{9,10},{10,9},{13,14},{14,13},{17,18},{18,... | collective-permute-start | bytes 1179656 | tf_op jit(solution)/shard_map/ppermute | solution.py:596
  87.3 26.4 %collective-permute-start.14 = (bf16[768,640]{1,0:T(8,128)(2,1)S(1)}, bf16[768,640]{1,0:T(8,128)(2,1)}, u32[]{:S(2)}, u32[]{:S(2)}) collective-permute-start(bf16[768,640]{1,0:T(8,128)(2,1)S(1)} %collective-permute-done.11), channel_id=1, source_target_pairs={{0,8},{1,9},{4,12},{5,13},{10,2},{11,3},{14,6},{15,7},{16,24},{17,... | collective-permute-start | bytes 2949128 | tf_op jit(solution)/shard_map/ppermute | solution.py:606
  88.8 34.2 %collective-permute-start.17 = (bf16[1280,384]{1,0:T(8,128)(2,1)}, bf16[1280,384]{1,0:T(8,128)(2,1)}, u32[]{:S(2)}, u32[]{:S(2)}) collective-permute-start(bf16[1280,384]{1,0:T(8,128)(2,1)} %collective-permute-done.15.refs_0_), channel_id=1, source_target_pairs={{0,16},{16,0},{1,17},{17,1},{2,18},{18,2},{3,19},{19,3},{4,20},{20... | collective-permute-start | bytes 2949128 | tf_op jit(solution)/shard_map/ppermute | solution.py:581
  106.9 35.1 %collective-permute-start.13 = (bf16[768,640]{1,0:T(8,128)(2,1)S(1)}, bf16[768,640]{1,0:T(8,128)(2,1)}, u32[]{:S(2)}, u32[]{:S(2)}) collective-permute-start(bf16[768,640]{1,0:T(8,128)(2,1)S(1)} %collective-permute-done.12), channel_id=1, source_target_pairs={{0,8},{1,9},{4,12},{5,13},{10,2},{11,3},{14,6},{15,7},{16,24},{17,... | collective-permute-start | bytes 2949128 | tf_op jit(solution)/shard_map/ppermute | solution.py:606
  108.2 30.3 %collective-permute-start.25 = (bf16[2,768,128]{2,1,0:T(8,128)(2,1)}, bf16[2,768,128]{2,1,0:T(8,128)(2,1)}, u32[]{:S(2)}, u32[]{:S(2)}) collective-permute-start(bf16[2,768,128]{2,1,0:T(8,128)(2,1)} %attend.4.refs_0_), channel_id=1, source_target_pairs={{0,2},{1,3},{2,0},{3,1},{4,6},{5,7},{6,4},{7,5},{8,10},{9,11},{10,... | collective-permute-start | bytes 1179656 | tf_op jit(solution)/shard_map/ppermute | solution.py:581
  113.7 28.3 %collective-permute-start.23 = (bf16[2,768,128]{2,1,0:T(8,128)(2,1)}, bf16[2,768,128]{2,1,0:T(8,128)(2,1)}, u32[]{:S(2)}, u32[]{:S(2)}) collective-permute-start(bf16[2,768,128]{2,1,0:T(8,128)(2,1)} %attend.4.refs_0_), channel_id=1, source_target_pairs={{0,1},{1,0},{2,3},{3,2},{4,5},{5,4},{6,7},{7,6},{8,9},{9,8},{10,11... | collective-permute-start | bytes 1179656 | tf_op jit(solution)/shard_map/ppermute | solution.py:581
  116.6 25.4 %collective-permute-start.24 = (bf16[2,768,128]{2,1,0:T(8,128)(2,1)}, bf16[2,768,128]{2,1,0:T(8,128)(2,1)}, u32[]{:S(2)}, u32[]{:S(2)}) collective-permute-start(bf16[2,768,128]{2,1,0:T(8,128)(2,1)} %attend.4.refs_0_), channel_id=1, source_target_pairs={{1,2},{2,1},{5,6},{6,5},{9,10},{10,9},{13,14},{14,13},{17,18},{18,... | collective-permute-start | bytes 1179656 | tf_op jit(solution)/shard_map/ppermute | solution.py:596
  125.3 20.1 %collective-permute-start.22 = (bf16[768,640]{1,0:T(8,128)(2,1)}, bf16[768,640]{1,0:T(8,128)(2,1)S(1)}, u32[]{:S(2)}, u32[]{:S(2)}) collective-permute-start(bf16[768,640]{1,0:T(8,128)(2,1)} %broadcast_select_fusion.2.refs_12_), channel_id=1, source_target_pairs={{0,16},{16,0},{1,17},{17,1},{2,18},{18,2},{3,19},{19,3},{4,20},{20... | collective-permute-start | bytes 2949128 | tf_op jit(solution)/shard_map/ppermute | solution.py:581
  145.5 30.2 %collective-permute-start.31 = (bf16[768,640]{1,0:T(8,128)(2,1)S(1)}, bf16[768,640]{1,0:T(8,128)(2,1)S(1)}, u32[]{:S(2)}, u32[]{:S(2)}) collective-permute-start(bf16[768,640]{1,0:T(8,128)(2,1)S(1)} %broadcast_select_fusion), channel_id=1, source_target_pairs={{0,8},{4,12},{1,9},{5,13},{2,10},{6,14},{3,11},{7,15},{16,24},{20,... | collective-permute-start | bytes 2949128 | tf_op jit(solution)/shard_map/ppermute | solution.py:672
  148.3 27.4 %collective-permute-start.30 = (bf16[768,640]{1,0:T(8,128)(2,1)S(1)}, bf16[768,640]{1,0:T(8,128)(2,1)S(1)}, u32[]{:S(2)}, u32[]{:S(2)}) collective-permute-start(bf16[768,640]{1,0:T(8,128)(2,1)S(1)} %broadcast_select_fusion.1.refs_14_), channel_id=1, source_target_pairs={{0,16},{16,0},{1,17},{17,1},{2,18},{18,2},{3,19},{19,3},{4,20},{20... | collective-permute-start | bytes 2949128 | tf_op jit(solution)/shard_map/ppermute | solution.py:581
  152.1 23.6 %collective-permute-start.29 = (bf16[2,768,128]{2,1,0:T(8,128)(2,1)S(1)}, bf16[2,768,128]{2,1,0:T(8,128)(2,1)S(1)}, u32[]{:S(2)}, u32[]{:S(2)}) collective-permute-start(bf16[2,768,128]{2,1,0:T(8,128)(2,1)S(1)} %copy-done.26), channel_id=1, source_target_pairs={{1,2},{2,1},{5,6},{6,5},{9,10},{10,9},{13,14},{14,13},{17,18},{18,... | collective-permute-start | bytes 1179656 | tf_op jit(solution)/shard_map/ppermute | solution.py:596
  166.2 21.3 %collective-permute-start.33 = (bf16[4,2,768,128]{3,2,1,0:T(8,128)(2,1)S(1)}, bf16[4,2,768,128]{3,2,1,0:T(8,128)(2,1)}, u32[]{:S(2)}, u32[]{:S(2)}) collective-permute-start(bf16[4,2,768,128]{3,2,1,0:T(8,128)(2,1)S(1)} %copy-done.9), channel_id=1, source_target_pairs={{0,4},{4,0},{8,12},{12,8},{1,5},{5,1},{9,13},{13,9},{2,6},{6,2},{1... | collective-permute-start | bytes 4718600 | tf_op jit(solution)/shard_map/ppermute | solution.py:581
  (53 other events, 626.1 us)

commit v5 on v4

--- a/solution.py
+++ b/solution.py
@@ -359,7 +359,7 @@
     depth = sum(p.shape[0] for p in pieces)
     return pl.pallas_call(
         functools.partial(attend_kernel, chunk, row, parts),
-        in_specs=[ANY] * 3 + [VMEM] * 2 + [ANY] * parts,
+        in_specs=[FREE] * 3 + [VMEM] * 2 + [FREE] * parts,
         out_specs=VMEM,
         out_shape=jax.ShapeDtypeStruct((2, rows, HD), jnp.bfloat16),
         scratch_shapes=[
@@ -551,7 +551,7 @@
     count, share = mine[0].shape
     return pl.pallas_call(
         functools.partial(join_kernel, parts),
-        in_specs=[ANY] * (2 * parts),
+        in_specs=[FREE] * (2 * parts),
         out_specs=ANY,
         out_shape=jax.ShapeDtypeStruct((1, parts * count, 2 * share), jnp.float32),
         scratch_shapes=[
@@ -666,13 +666,13 @@
     )
     gate_own, gate_par = gates
 
-    one2, inner2 = along(att2, 1), middle(att2)
+    one2 = along(att2, 1)
     v1 = jnp.where(home, sent1, u1)
     xv1 = swap(v1)
     start_far = lax.ppermute(jnp.where(core == 0, lat_own, lat_par), "tm", [(0, 2), (1, 3)])
     g1 = bundle(att1, one1, two1, inner1, outer1)
-    two2, one2, inner2, v1, xv1, g1, start_far = phase(two2, one2, inner2, v1, xv1, g1, start_far)
-    outer2 = outward(two2)
+    two2, one2, v1, xv1, g1, start_far = phase(two2, one2, v1, xv1, g1, start_far)
+    outer2, inner2 = outward(two2), middle(att2)
     q0, q1, b0, b1, b2 = partner(g0), partner(g1), partner(att2), partner(one2), partner(two2)
     outer2, inner2, q0, q1, b0, b1, b2 = phase(outer2, inner2, q0, q1, b0, b1, b2)
 
@@ -693,7 +693,7 @@
     terms0, total0, gate_own = phase(terms0, total0, gate_own)
     carry0 = ahead(total0)
     terms1, total1 = project(count, gate_own)
-    terms1, total1, carry0 = phase(terms1, total1, carry0)
+    terms1, total1, terms0 = phase(terms1, total1, terms0)
     carry1 = ahead(total1)
     own0, send0, squares0 = close(0, terms0, carry0, start_far, lat_own, lat_par)
     carry1, own0, send0, squares0 = phase(carry1, own0, send0, squares0)

time: 252 us -> 246 us (0.976)
  waiting for transfers between devices: 66.9 us -> 58.8 us
    ppermute x3, waiting for transfers between devices: 10.8 us -> 3.86 us  [outward(): return lax.ppermute(array, 'tensor', [(1, 0), (2, 3)])]
    ppermute x2, waiting for transfers between devices: 16.7 us -> 10.8 us  [ahead(): return lax.ppermute(total, 'tm', [(0, 2), (1, 3)])]
    ppermute x34, waiting for transfers between devices: 26.7 us -> 29.8 us  [over(): lax.ppermute(array, axis, [(i, i ^ flip) for i in range(lax.axis_size(axi...]
    ppermute x1, waiting for transfers between devices: 0.01 us -> 2.57 us  [fast_body(): lax.ppermute(jnp.where(core == 0, lat_own, lat_par), 'tm', [(0, 2), (1, 3)])]
  transfers between devices with their start and end apart: 47 -> 47, of which waited for: 15 -> 16; matrix products, arithmetic and copies ran while one was open for 5% -> 5% of each run, Pallas kernels for 37% -> 38%
where the time goes in v5:
time: 246 us; the launch traced here: 244 us
  Pallas kernels  102 us (41%)
  starting transfers between devices  59.4 us (24%)
  waiting for transfers between devices  58.8 us (24%)
  local copies, waits for them, and re-layouts  11.3 us (5%)
  other arithmetic  8.03 us (3%)
  between operations  4.32 us (2%)
    pallas_call x3, Pallas kernels, attend(): pl.pallas_call(functools.partial(attend_kernel, chunk, row, parts), in_sp...  36.8 us
    ppermute x34, starting transfers between devices, over(): lax.ppermute(array, axis, [(i, i ^ flip) for i in range(lax.axis_size(axi...  30.6 us
    ppermute x34, waiting for transfers between devices, over(): lax.ppermute(array, axis, [(i, i ^ flip) for i in range(lax.axis_size(axi...  29.8 us
    pallas_call x2, Pallas kernels, out_projection(): pl.pallas_call(functools.partial(out_kernel, chunks, top), in_specs=[VMEM...  18.1 us
    pallas_call x1, Pallas kernels, near(): pl.pallas_call(near_kernel, in_specs=[ANY] * 8, out_specs=ANY, out_shape=...  17.9 us
    ppermute x3, starting transfers between devices, middle(): return lax.ppermute(array, 'tensor', [(1, 2), (2, 1)])  13.4 us
    ppermute x2, waiting for transfers between devices, ahead(): return lax.ppermute(total, 'tm', [(0, 2), (1, 3)])  10.8 us
    pallas_call x1, Pallas kernels, fast_hidden(): pl.pallas_call(hidden_kernel, grid=(rows // block,), in_specs=[pl.BlockSp...  8.92 us
  transfers between devices with their start and end apart: 47, of which 16 were waited for; matrix products, arithmetic and copies ran while one was open for 5% of the time, Pallas kernels for 38%

profile of v5, /device:TPU:12, one launch (start us, length us, event | category | flops | bytes accessed | tf_op | source)
XLA Modules:
  0.0 243.5 jit_solution(13474078400890350822)
XLA Ops:
  9.4 8.9 %hidden.1.h_own = bf16[768,5120]{1,0:T(8,128)(2,1)} custom-call(bf16[1,768,5120]{2,1,0:T(8,128)(2,1)} %latent, f32[1,5120]{1,0:T(1,128)} %bitcast.11), custom_call_target="tpu_custom_call" | custom-call | flops 5000000000 | bytes 1024 | tf_op jit(solution)/shard_map/hidden/pallas_call | solution.py:121
  19.1 3.5 %packs.1 = (bf16[1280,384]{1,0:T(8,128)(2,1)}, bf16[1280,384]{1,0:T(8,128)(2,1)}, bf16[768,640]{1,0:T(8,128)(2,1)}, bf16[768,640]{1,0:T(8,128)(2,1)}) custom-call(bf16[1280,768]{1,0:T(8,128)(2,1)} %wq.5, bf16[1280,768]{1,0:T(8,128)(2,1)} %wk.5, bf16[1280,768]{1,0:T(8,128)(2,1)} %wv.5, bf16[1280,768]{1,0:T(8,128)(2,1)} %copy-done.1, ...), custom_call_target="tpu_custom_call" | custom-call | flops 1000000000 | bytes 1024 | tf_op jit(solution)/shard_map/packs/pallas_call | solution.py:225
  22.6 6.1 %collective-permute-done.1.refs_1_ = bf16[640,384]{1,0:T(8,128)(2,1)S(1)} collective-permute-done((bf16[640,384]{1,0:T(8,128)(2,1)S(1)}, bf16[640,384]{1,0:T(8,128)(2,1)S(1)}, u32[]{:S(2)}, u32[]{:S(2)}) %collective-permute-start.1) | collective-permute-done | bytes 491552 | tf_op jit(solution)/shard_map/ppermute | solution.py:581
  32.4 3.3 %collective-permute-start.8 = (bf16[640,384]{1,0:T(8,128)(2,1)S(1)}, bf16[640,384]{1,0:T(8,128)(2,1)S(1)}, u32[]{:S(2)}, u32[]{:S(2)}) collective-permute-start(bf16[640,384]{1,0:T(8,128)(2,1)S(1)} %collective-permute-done.refs_0_), channel_id=1, source_target_pairs={{0,16},{16,0},{1,17},{17,1},{2,18},{18,2},{3,19},{19,3},{4,20},{20... | collective-permute-start | bytes 1474568 | tf_op jit(solution)/shard_map/ppermute | solution.py:581
  35.7 6.0 %collective-permute-done.10.h_par = bf16[768,5120]{1,0:T(8,128)(2,1)} collective-permute-done((bf16[768,5120]{1,0:T(8,128)(2,1)}, bf16[768,5120]{1,0:T(8,128)(2,1)}, u32[]{:S(2)}, u32[]{:S(2)}) %collective-permute-start.10) | collective-permute-done | bytes 7864352 | tf_op jit(solution)/shard_map/ppermute | solution.py:581
  42.6 17.9 %near.1.acc = f32[3,2,768,384]{3,2,1,0:T(8,128)} custom-call(bf16[768,5120]{1,0:T(8,128)(2,1)} %hidden.1.h_own, bf16[768,5120]{1,0:T(8,128)(2,1)} %collective-permute-done.10.h_par, bf16[1280,768]{1,0:T(8,128)(2,1)} %wq.5, bf16[1280,768]{1,0:T(8,128)(2,1)} %wk.5, bf16[1280,768]{1,0:T(8,128)(2,1)} %wv.5, bf16[1280,768]{1,0:T(8,128)(2,1)} %copy-done.1, ...), custom_call_target="tpu_custom_call" | custom-call | flops 10000000000 | bytes 1024 | tf_op jit(solution)/shard_map/near/pallas_call | solution.py:282
  61.8 3.3 %collective-permute-start.16 = (bf16[1280,384]{1,0:T(8,128)(2,1)}, bf16[1280,384]{1,0:T(8,128)(2,1)S(1)}, u32[]{:S(2)}, u32[]{:S(2)}) collective-permute-start(bf16[1280,384]{1,0:T(8,128)(2,1)} %collective-permute-done.7.refs_0_), channel_id=1, source_target_pairs={{0,16},{16,0},{1,17},{17,1},{2,18},{18,2},{3,19},{19,3},{4,20},{20... | collective-permute-start | bytes 2949128 | tf_op jit(solution)/shard_map/ppermute | solution.py:581
  65.1 12.3 %attend.3.refs_0_ = bf16[2,768,128]{2,1,0:T(8,128)(2,1)} custom-call(bf16[768,5120]{1,0:T(8,128)(2,1)} %hidden.1.h_own, bf16[768,5120]{1,0:T(8,128)(2,1)} %collective-permute-done.10.h_par, f32[3,2,768,384]{3,2,1,0:T(8,128)} %near.1.acc, f32[1,768]{1,0:T(1,128)} %reshape.31.qg, f32[1,768]{1,0:T(1,128)} %reshape.32.kg, bf16[640,384]{1,0:T(8,128)(2,1)} %copy-done.17, ...), custom_call_target="tpu_custom_call" | custom-call | flops 12000000000 | bytes 1024 | tf_op jit(solution)/shard_map/attend/pallas_call | solution.py:360
  79.1 3.7 %collective-permute-start.19 = (bf16[2,768,128]{2,1,0:T(8,128)(2,1)}, bf16[2,768,128]{2,1,0:T(8,128)(2,1)}, u32[]{:S(2)}, u32[]{:S(2)}) collective-permute-start(bf16[2,768,128]{2,1,0:T(8,128)(2,1)} %attend.3.refs_0_), channel_id=1, source_target_pairs={{1,2},{2,1},{5,6},{6,5},{9,10},{10,9},{13,14},{14,13},{17,18},{18,... | collective-permute-start | bytes 1179656 | tf_op jit(solution)/shard_map/ppermute | solution.py:596
  91.1 12.2 %attend.4.refs_0_ = bf16[2,768,128]{2,1,0:T(8,128)(2,1)} custom-call(bf16[768,5120]{1,0:T(8,128)(2,1)} %hidden.1.h_own, bf16[768,5120]{1,0:T(8,128)(2,1)} %collective-permute-done.10.h_par, f32[3,2,768,384]{3,2,1,0:T(8,128)} %near.1.acc, f32[1,768]{1,0:T(1,128)} %reshape.31.qg, f32[1,768]{1,0:T(1,128)} %reshape.32.kg, ...), custom_call_target="tpu_custom_call" | custom-call | flops 12000000000 | bytes 1024 | tf_op jit(solution)/shard_map/attend/pallas_call | solution.py:360
  103.4 3.5 %collective-permute-start.21 = (bf16[2,768,128]{2,1,0:T(8,128)(2,1)S(1)}, bf16[2,768,128]{2,1,0:T(8,128)(2,1)}, u32[]{:S(2)}, u32[]{:S(2)}) collective-permute-start(bf16[2,768,128]{2,1,0:T(8,128)(2,1)S(1)} %collective-permute-done.20.refs_2_), channel_id=1, source_target_pairs={{1,0},{2,3},{5,4},{6,7},{9,8},{10,11},{13,12},{14,15},{17,16},{18,... | collective-permute-start | bytes 1179656 | tf_op jit(solution)/shard_map/ppermute | solution.py:599
  109.5 4.2 %collective-permute-done.14 = bf16[768,640]{1,0:T(8,128)(2,1)} collective-permute-done((bf16[768,640]{1,0:T(8,128)(2,1)S(1)}, bf16[768,640]{1,0:T(8,128)(2,1)}, u32[]{:S(2)}, u32[]{:S(2)}) %collective-permute-start.14) | collective-permute-done | bytes 983072 | tf_op jit(solution)/shard_map/ppermute | solution.py:606
  116.6 6.4 %collective-permute-start.24 = (bf16[2,768,128]{2,1,0:T(8,128)(2,1)}, bf16[2,768,128]{2,1,0:T(8,128)(2,1)}, u32[]{:S(2)}, u32[]{:S(2)}) collective-permute-start(bf16[2,768,128]{2,1,0:T(8,128)(2,1)} %attend.4.refs_0_), channel_id=1, source_target_pairs={{1,2},{2,1},{5,6},{6,5},{9,10},{10,9},{13,14},{14,13},{17,18},{18,... | collective-permute-start | bytes 1179656 | tf_op jit(solution)/shard_map/ppermute | solution.py:596
  126.1 12.3 %attend.5.refs_4_ = bf16[2,768,128]{2,1,0:T(8,128)(2,1)} custom-call(bf16[768,5120]{1,0:T(8,128)(2,1)} %hidden.1.h_own, bf16[768,5120]{1,0:T(8,128)(2,1)} %collective-permute-done.10.h_par, f32[3,2,768,384]{3,2,1,0:T(8,128)} %near.1.acc, f32[1,768]{1,0:T(1,128)} %reshape.31.qg, f32[1,768]{1,0:T(1,128)} %reshape.32.kg, ...), custom_call_target="tpu_custom_call" | custom-call | flops 12000000000 | bytes 1024 | tf_op jit(solution)/shard_map/attend/pallas_call | solution.py:360
  142.0 3.3 %collective-permute-done.26.refs_4_ = bf16[2,768,128]{2,1,0:T(8,128)(2,1)S(1)} collective-permute-done((bf16[2,768,128]{2,1,0:T(8,128)(2,1)}, bf16[2,768,128]{2,1,0:T(8,128)(2,1)S(1)}, u32[]{:S(2)}, u32[]{:S(2)}) %collective-permute-start.26) | collective-permute-done | bytes 393248 | tf_op jit(solution)/shard_map/ppermute | solution.py:599
  156.0 9.4 %collective-permute-done.27.refs_6_ = bf16[2,768,128]{2,1,0:T(8,128)(2,1)} collective-permute-done((bf16[2,768,128]{2,1,0:T(8,128)(2,1)S(1)}, bf16[2,768,128]{2,1,0:T(8,128)(2,1)}, u32[]{:S(2)}, u32[]{:S(2)}) %collective-permute-start.27) | collective-permute-done | bytes 393248 | tf_op jit(solution)/shard_map/ppermute | solution.py:581
  171.9 3.3 %collective-permute-start.32 = (bf16[2,768,128]{2,1,0:T(8,128)(2,1)S(1)}, bf16[2,768,128]{2,1,0:T(8,128)(2,1)S(1)}, u32[]{:S(2)}, u32[]{:S(2)}) collective-permute-start(bf16[2,768,128]{2,1,0:T(8,128)(2,1)S(1)} %copy-done.26), channel_id=1, source_target_pairs={{1,2},{2,1},{5,6},{6,5},{9,10},{10,9},{13,14},{14,13},{17,18},{18,... | collective-permute-start | bytes 1179656 | tf_op jit(solution)/shard_map/ppermute | solution.py:596
  177.7 7.6 %collective-permute-done.32 = bf16[2,768,128]{2,1,0:T(8,128)(2,1)S(1)} collective-permute-done((bf16[2,768,128]{2,1,0:T(8,128)(2,1)S(1)}, bf16[2,768,128]{2,1,0:T(8,128)(2,1)S(1)}, u32[]{:S(2)}, u32[]{:S(2)}) %collective-permute-start.32) | collective-permute-done | bytes 393248 | tf_op jit(solution)/shard_map/ppermute | solution.py:596
  190.9 8.9 %out_projection.2 = (f32[2,384,640]{2,1,0:T(8,128)}, bf16[384,640]{1,0:T(8,128)(2,1)}) custom-call(f32[1,640]{1,0:T(1,128)} %reshape.33.gate_own, f32[1,640]{1,0:T(1,128)} %reshape.34.gate_par, bf16[4,2,768,128]{3,2,1,0:T(8,128)(2,1)} %bundle.2.refs_0_, bf16[4,2,768,128]{3,2,1,0:T(8,128)(2,1)} %bundle.3.refs_1_, ...), custom_call_target="tpu_custom_call" | custom-call | flops 12000000000 | bytes 1024 | tf_op jit(solution)/shard_map/out_projection/pallas_call | solution.py:462
  201.1 9.2 %out_projection.3 = (f32[2,384,640]{2,1,0:T(8,128)}, bf16[384,640]{1,0:T(8,128)(2,1)}) custom-call(f32[1,640]{1,0:T(1,128)} %reshape.33.gate_own, f32[1,640]{1,0:T(1,128)} %reshape.34.gate_par, bf16[4,2,768,128]{3,2,1,0:T(8,128)(2,1)} %bundle.2.refs_0_, bf16[4,2,768,128]{3,2,1,0:T(8,128)(2,1)} %bundle.3.refs_1_, ...), custom_call_target="tpu_custom_call" | custom-call | flops 12000000000 | bytes 1024 | tf_op jit(solution)/shard_map/out_projection/pallas_call | solution.py:462
  211.6 4.4 %collective-permute-done.40.carry = bf16[384,640]{1,0:T(8,128)(2,1)S(1)} collective-permute-done((bf16[384,640]{1,0:T(8,128)(2,1)}, bf16[384,640]{1,0:T(8,128)(2,1)S(1)}, u32[]{:S(2)}, u32[]{:S(2)}) %collective-permute-start.40) | collective-permute-done | bytes 491552 | tf_op jit(solution)/shard_map/ppermute | solution.py:690
  216.8 3.4 %close.2 = (f32[384,640]{1,0:T(8,128)}, f32[384,640]{1,0:T(8,128)}, f32[2,640]{1,0:T(2,128)}) custom-call(f32[2,384,640]{2,1,0:T(8,128)} %get-tuple-element.178.terms, bf16[384,640]{1,0:T(8,128)(2,1)} %copy-done.23, bf16[768,640]{1,0:T(8,128)(2,1)} %copy-done.10, bf16[768,640]{1,0:T(8,128)(2,1)} %copy-done, bf16[768,640]{1,0:T(8,128)(2,1)} %collective-permute-done.5.par), custom_call_target="tpu_custom_call" | custom-call | flops 8000000000 | bytes 1024 | tf_op jit(solution)/shard_map/close/pallas_call | solution.py:510
  220.1 6.4 %collective-permute-done.39.carry = bf16[384,640]{1,0:T(8,128)(2,1)S(1)} collective-permute-done((bf16[384,640]{1,0:T(8,128)(2,1)}, bf16[384,640]{1,0:T(8,128)(2,1)S(1)}, u32[]{:S(2)}, u32[]{:S(2)}) %collective-permute-start.39) | collective-permute-done | bytes 491552 | tf_op jit(solution)/shard_map/ppermute | solution.py:690
  227.3 3.3 %close.3 = (f32[384,640]{1,0:T(8,128)}, f32[384,640]{1,0:T(8,128)}, f32[2,640]{1,0:T(2,128)}) custom-call(f32[2,384,640]{2,1,0:T(8,128)} %get-tuple-element.186.terms, bf16[384,640]{1,0:T(8,128)(2,1)} %copy-done.24, bf16[768,640]{1,0:T(8,128)(2,1)} %copy-done.10, bf16[768,640]{1,0:T(8,128)(2,1)} %copy-done, bf16[768,640]{1,0:T(8,128)(2,1)} %collective-permute-done.5.par), custom_call_target="tpu_custom_call" | custom-call | flops 8000000000 | bytes 1024 | tf_op jit(solution)/shard_map/close/pallas_call | solution.py:510
  (163 shorter events, 76.5 us)
Async XLA Ops:
  0.7 17.6 %collective-permute-start.3 = (bf16[1280,768]{1,0:T(8,128)(2,1)}, bf16[1280,768]{1,0:T(8,128)(2,1)}, u32[]{:S(2)}, u32[]{:S(2)}) collective-permute-start(bf16[1280,768]{1,0:T(8,128)(2,1)} %wk.5), channel_id=1, source_target_pairs={{0,4},{4,0},{8,12},{12,8},{1,5},{5,1},{9,13},{13,9},{2,6},{6,2},{1... | collective-permute-start | bytes 5898248 | tf_op jit(solution)/shard_map/ppermute | solution.py:581
  1.2 17.9 %collective-permute-start.4 = (bf16[1280,768]{1,0:T(8,128)(2,1)}, bf16[1280,768]{1,0:T(8,128)(2,1)}, u32[]{:S(2)}, u32[]{:S(2)}) collective-permute-start(bf16[1280,768]{1,0:T(8,128)(2,1)} %wv.5), channel_id=1, source_target_pairs={{0,4},{4,0},{8,12},{12,8},{1,5},{5,1},{9,13},{13,9},{2,6},{6,2},{1... | collective-permute-start | bytes 5898248 | tf_op jit(solution)/shard_map/ppermute | solution.py:581
  5.3 23.4 %collective-permute-start.5 = (bf16[768,640]{1,0:T(8,128)(2,1)S(1)}, bf16[768,640]{1,0:T(8,128)(2,1)}, u32[]{:S(2)}, u32[]{:S(2)}) collective-permute-start(bf16[768,640]{1,0:T(8,128)(2,1)S(1)} %get-tuple-element.198), channel_id=1, source_target_pairs={{0,4},{4,0},{8,12},{12,8},{1,5},{5,1},{9,13},{13,9},{2,6},{6,2},{1... | collective-permute-start | bytes 2949128 | tf_op jit(solution)/shard_map/ppermute | solution.py:581
  8.4 20.3 %collective-permute-start.1 = (bf16[640,384]{1,0:T(8,128)(2,1)S(1)}, bf16[640,384]{1,0:T(8,128)(2,1)S(1)}, u32[]{:S(2)}, u32[]{:S(2)}) collective-permute-start(bf16[640,384]{1,0:T(8,128)(2,1)S(1)} %copy-done.19), channel_id=1, source_target_pairs={{0,12},{4,8},{8,4},{12,0},{1,13},{5,9},{9,5},{13,1},{2,14},{6,10},... | collective-permute-start | bytes 1474568 | tf_op jit(solution)/shard_map/ppermute | solution.py:581
  29.4 31.3 %collective-permute-start.11 = (bf16[768,640]{1,0:T(8,128)(2,1)}, bf16[768,640]{1,0:T(8,128)(2,1)S(1)}, u32[]{:S(2)}, u32[]{:S(2)}) collective-permute-start(bf16[768,640]{1,0:T(8,128)(2,1)} %get-tuple-element.115), channel_id=1, source_target_pairs={{0,0},{17,16},{2,4},{19,20},{4,1},{21,17},{6,5},{23,21},{8,10},{25... | collective-permute-start | bytes 2949128 | tf_op jit(solution)/shard_map/ppermute | solution.py:614
  30.1 30.5 %collective-permute-start.7 = (bf16[1280,384]{1,0:T(8,128)(2,1)}, bf16[1280,384]{1,0:T(8,128)(2,1)}, u32[]{:S(2)}, u32[]{:S(2)}) collective-permute-start(bf16[1280,384]{1,0:T(8,128)(2,1)} %get-tuple-element.111), channel_id=1, source_target_pairs={{0,8},{4,12},{8,0},{12,4},{1,9},{5,13},{9,1},{13,5},{2,10},{6,14},... | collective-permute-start | bytes 2949128 | tf_op jit(solution)/shard_map/ppermute | solution.py:581
  32.4 28.1 %collective-permute-start.8 = (bf16[640,384]{1,0:T(8,128)(2,1)S(1)}, bf16[640,384]{1,0:T(8,128)(2,1)S(1)}, u32[]{:S(2)}, u32[]{:S(2)}) collective-permute-start(bf16[640,384]{1,0:T(8,128)(2,1)S(1)} %collective-permute-done.refs_0_), channel_id=1, source_target_pairs={{0,16},{16,0},{1,17},{17,1},{2,18},{18,2},{3,19},{19,3},{4,20},{20... | collective-permute-start | bytes 1474568 | tf_op jit(solution)/shard_map/ppermute | solution.py:581
  35.7 24.9 %collective-permute-start.9 = (bf16[640,384]{1,0:T(8,128)(2,1)}, bf16[640,384]{1,0:T(8,128)(2,1)S(1)}, u32[]{:S(2)}, u32[]{:S(2)}) collective-permute-start(bf16[640,384]{1,0:T(8,128)(2,1)} %copy-done.18), channel_id=1, source_target_pairs={{0,16},{16,0},{1,17},{17,1},{2,18},{18,2},{3,19},{19,3},{4,20},{20... | collective-permute-start | bytes 1474568 | tf_op jit(solution)/shard_map/ppermute | solution.py:581
  41.7 35.6 %collective-permute-start.12 = (bf16[768,640]{1,0:T(8,128)(2,1)}, bf16[768,640]{1,0:T(8,128)(2,1)S(1)}, u32[]{:S(2)}, u32[]{:S(2)}) collective-permute-start(bf16[768,640]{1,0:T(8,128)(2,1)} %get-tuple-element.122), channel_id=1, source_target_pairs={{0,4},{17,20},{2,0},{19,16},{4,5},{21,21},{6,1},{23,17},{8,14},{25... | collective-permute-start | bytes 2949128 | tf_op jit(solution)/shard_map/ppermute | solution.py:614
  60.6 26.7 %collective-permute-start.15 = (bf16[1280,384]{1,0:T(8,128)(2,1)S(1)}, bf16[1280,384]{1,0:T(8,128)(2,1)}, u32[]{:S(2)}, u32[]{:S(2)}) collective-permute-start(bf16[1280,384]{1,0:T(8,128)(2,1)S(1)} %copy-done.12), channel_id=1, source_target_pairs={{0,8},{4,12},{8,0},{12,4},{1,9},{5,13},{9,1},{13,5},{2,10},{6,14},... | collective-permute-start | bytes 2949128 | tf_op jit(solution)/shard_map/ppermute | solution.py:581
  61.8 27.0 %collective-permute-start.16 = (bf16[1280,384]{1,0:T(8,128)(2,1)}, bf16[1280,384]{1,0:T(8,128)(2,1)S(1)}, u32[]{:S(2)}, u32[]{:S(2)}) collective-permute-start(bf16[1280,384]{1,0:T(8,128)(2,1)} %collective-permute-done.7.refs_0_), channel_id=1, source_target_pairs={{0,16},{16,0},{1,17},{17,1},{2,18},{18,2},{3,19},{19,3},{4,20},{20... | collective-permute-start | bytes 2949128 | tf_op jit(solution)/shard_map/ppermute | solution.py:581
  77.4 26.0 %collective-permute-start.20 = (bf16[2,768,128]{2,1,0:T(8,128)(2,1)}, bf16[2,768,128]{2,1,0:T(8,128)(2,1)S(1)}, u32[]{:S(2)}, u32[]{:S(2)}) collective-permute-start(bf16[2,768,128]{2,1,0:T(8,128)(2,1)} %attend.3.refs_0_), channel_id=1, source_target_pairs={{0,2},{1,3},{2,0},{3,1},{4,6},{5,7},{6,4},{7,5},{8,10},{9,11},{10,... | collective-permute-start | bytes 1179656 | tf_op jit(solution)/shard_map/ppermute | solution.py:581
  79.1 27.8 %collective-permute-start.18 = (bf16[2,768,128]{2,1,0:T(8,128)(2,1)}, bf16[2,768,128]{2,1,0:T(8,128)(2,1)}, u32[]{:S(2)}, u32[]{:S(2)}) collective-permute-start(bf16[2,768,128]{2,1,0:T(8,128)(2,1)} %attend.3.refs_0_), channel_id=1, source_target_pairs={{0,1},{1,0},{2,3},{3,2},{4,5},{5,4},{6,7},{7,6},{8,9},{9,8},{10,11... | collective-permute-start | bytes 1179656 | tf_op jit(solution)/shard_map/ppermute | solution.py:581
  79.1 29.1 %collective-permute-start.19 = (bf16[2,768,128]{2,1,0:T(8,128)(2,1)}, bf16[2,768,128]{2,1,0:T(8,128)(2,1)}, u32[]{:S(2)}, u32[]{:S(2)}) collective-permute-start(bf16[2,768,128]{2,1,0:T(8,128)(2,1)} %attend.3.refs_0_), channel_id=1, source_target_pairs={{1,2},{2,1},{5,6},{6,5},{9,10},{10,9},{13,14},{14,13},{17,18},{18,... | collective-permute-start | bytes 1179656 | tf_op jit(solution)/shard_map/ppermute | solution.py:596
  87.3 26.4 %collective-permute-start.14 = (bf16[768,640]{1,0:T(8,128)(2,1)S(1)}, bf16[768,640]{1,0:T(8,128)(2,1)}, u32[]{:S(2)}, u32[]{:S(2)}) collective-permute-start(bf16[768,640]{1,0:T(8,128)(2,1)S(1)} %collective-permute-done.11), channel_id=1, source_target_pairs={{0,8},{1,9},{4,12},{5,13},{10,2},{11,3},{14,6},{15,7},{16,24},{17,... | collective-permute-start | bytes 2949128 | tf_op jit(solution)/shard_map/ppermute | solution.py:606
  88.8 34.2 %collective-permute-start.17 = (bf16[1280,384]{1,0:T(8,128)(2,1)}, bf16[1280,384]{1,0:T(8,128)(2,1)}, u32[]{:S(2)}, u32[]{:S(2)}) collective-permute-start(bf16[1280,384]{1,0:T(8,128)(2,1)} %collective-permute-done.15.refs_0_), channel_id=1, source_target_pairs={{0,16},{16,0},{1,17},{17,1},{2,18},{18,2},{3,19},{19,3},{4,20},{20... | collective-permute-start | bytes 2949128 | tf_op jit(solution)/shard_map/ppermute | solution.py:581
  106.9 35.1 %collective-permute-start.13 = (bf16[768,640]{1,0:T(8,128)(2,1)S(1)}, bf16[768,640]{1,0:T(8,128)(2,1)}, u32[]{:S(2)}, u32[]{:S(2)}) collective-permute-start(bf16[768,640]{1,0:T(8,128)(2,1)S(1)} %collective-permute-done.12), channel_id=1, source_target_pairs={{0,8},{1,9},{4,12},{5,13},{10,2},{11,3},{14,6},{15,7},{16,24},{17,... | collective-permute-start | bytes 2949128 | tf_op jit(solution)/shard_map/ppermute | solution.py:606
  108.2 30.2 %collective-permute-start.25 = (bf16[2,768,128]{2,1,0:T(8,128)(2,1)}, bf16[2,768,128]{2,1,0:T(8,128)(2,1)}, u32[]{:S(2)}, u32[]{:S(2)}) collective-permute-start(bf16[2,768,128]{2,1,0:T(8,128)(2,1)} %attend.4.refs_0_), channel_id=1, source_target_pairs={{0,2},{1,3},{2,0},{3,1},{4,6},{5,7},{6,4},{7,5},{8,10},{9,11},{10,... | collective-permute-start | bytes 1179656 | tf_op jit(solution)/shard_map/ppermute | solution.py:581
  113.7 28.4 %collective-permute-start.23 = (bf16[2,768,128]{2,1,0:T(8,128)(2,1)}, bf16[2,768,128]{2,1,0:T(8,128)(2,1)}, u32[]{:S(2)}, u32[]{:S(2)}) collective-permute-start(bf16[2,768,128]{2,1,0:T(8,128)(2,1)} %attend.4.refs_0_), channel_id=1, source_target_pairs={{0,1},{1,0},{2,3},{3,2},{4,5},{5,4},{6,7},{7,6},{8,9},{9,8},{10,11... | collective-permute-start | bytes 1179656 | tf_op jit(solution)/shard_map/ppermute | solution.py:581
  116.6 25.4 %collective-permute-start.24 = (bf16[2,768,128]{2,1,0:T(8,128)(2,1)}, bf16[2,768,128]{2,1,0:T(8,128)(2,1)}, u32[]{:S(2)}, u32[]{:S(2)}) collective-permute-start(bf16[2,768,128]{2,1,0:T(8,128)(2,1)} %attend.4.refs_0_), channel_id=1, source_target_pairs={{1,2},{2,1},{5,6},{6,5},{9,10},{10,9},{13,14},{14,13},{17,18},{18,... | collective-permute-start | bytes 1179656 | tf_op jit(solution)/shard_map/ppermute | solution.py:596
  125.3 20.1 %collective-permute-start.22 = (bf16[768,640]{1,0:T(8,128)(2,1)}, bf16[768,640]{1,0:T(8,128)(2,1)S(1)}, u32[]{:S(2)}, u32[]{:S(2)}) collective-permute-start(bf16[768,640]{1,0:T(8,128)(2,1)} %broadcast_select_fusion.2.refs_12_), channel_id=1, source_target_pairs={{0,16},{16,0},{1,17},{17,1},{2,18},{18,2},{3,19},{19,3},{4,20},{20... | collective-permute-start | bytes 2949128 | tf_op jit(solution)/shard_map/ppermute | solution.py:581
  147.3 23.7 %collective-permute-start.30 = (bf16[768,640]{1,0:T(8,128)(2,1)S(1)}, bf16[768,640]{1,0:T(8,128)(2,1)S(1)}, u32[]{:S(2)}, u32[]{:S(2)}) collective-permute-start(bf16[768,640]{1,0:T(8,128)(2,1)S(1)} %broadcast_select_fusion), channel_id=1, source_target_pairs={{0,8},{4,12},{1,9},{5,13},{2,10},{6,14},{3,11},{7,15},{16,24},{20,... | collective-permute-start | bytes 2949128 | tf_op jit(solution)/shard_map/ppermute | solution.py:672
  150.0 20.9 %collective-permute-start.29 = (bf16[768,640]{1,0:T(8,128)(2,1)S(1)}, bf16[768,640]{1,0:T(8,128)(2,1)S(1)}, u32[]{:S(2)}, u32[]{:S(2)}) collective-permute-start(bf16[768,640]{1,0:T(8,128)(2,1)S(1)} %broadcast_select_fusion.1.refs_14_), channel_id=1, source_target_pairs={{0,16},{16,0},{1,17},{17,1},{2,18},{18,2},{3,19},{19,3},{4,20},{20... | collective-permute-start | bytes 2949128 | tf_op jit(solution)/shard_map/ppermute | solution.py:581
  153.8 34.5 %collective-permute-start.33 = (bf16[4,2,768,128]{3,2,1,0:T(8,128)(2,1)S(1)}, bf16[4,2,768,128]{3,2,1,0:T(8,128)(2,1)}, u32[]{:S(2)}, u32[]{:S(2)}) collective-permute-start(bf16[4,2,768,128]{3,2,1,0:T(8,128)(2,1)S(1)} %copy-done.9), channel_id=1, source_target_pairs={{0,4},{4,0},{8,12},{12,8},{1,5},{5,1},{9,13},{13,9},{2,6},{6,2},{1... | collective-permute-start | bytes 4718600 | tf_op jit(solution)/shard_map/ppermute | solution.py:581
  (53 other events, 616.5 us)

commit v6 on v5

--- a/solution.py
+++ b/solution.py
@@ -10,7 +10,7 @@
 
 HD = 128
 CARRY = jnp.bfloat16
-COST = 1e6
+COST = 3e6
 VMEM_LIMIT = 56 * 2**20
 ANY = pl.BlockSpec(memory_space=pltpu.HBM)
 FREE = pl.BlockSpec(memory_space=pl.ANY)

time: 246 us -> 246 us (level)
    unnamed x60 -> x64, local copies, waits for them, and re-layouts: 5.94 us -> 5.77 us
  transfers between devices with their start and end apart: 47 -> 47, of which waited for: 16 -> 16; matrix products, arithmetic and copies ran while one was open for 5% -> 6% of each run, Pallas kernels for 38% -> 38%
where the time goes in v6:
time: 246 us; the launch traced here: 243 us
  Pallas kernels  102 us (41%)
  starting transfers between devices  59.5 us (24%)
  waiting for transfers between devices  57.3 us (23%)
  local copies, waits for them, and re-layouts  12 us (5%)
  other arithmetic  8.07 us (3%)
  between operations  4.36 us (2%)
    pallas_call x3, Pallas kernels, attend(): pl.pallas_call(functools.partial(attend_kernel, chunk, row, parts), in_sp...  36.7 us
    ppermute x34, starting transfers between devices, over(): lax.ppermute(array, axis, [(i, i ^ flip) for i in range(lax.axis_size(axi...  30.6 us
    ppermute x34, waiting for transfers between devices, over(): lax.ppermute(array, axis, [(i, i ^ flip) for i in range(lax.axis_size(axi...  28.2 us
    pallas_call x2, Pallas kernels, out_projection(): pl.pallas_call(functools.partial(out_kernel, chunks, top), in_specs=[VMEM...  18.1 us
    pallas_call x1, Pallas kernels, near(): pl.pallas_call(near_kernel, in_specs=[ANY] * 8, out_specs=ANY, out_shape=...  17.9 us
    ppermute x3, starting transfers between devices, middle(): return lax.ppermute(array, 'tensor', [(1, 2), (2, 1)])  13.3 us
    ppermute x2, waiting for transfers between devices, ahead(): return lax.ppermute(total, 'tm', [(0, 2), (1, 3)])  10.6 us
    pallas_call x1, Pallas kernels, fast_hidden(): pl.pallas_call(hidden_kernel, grid=(rows // block,), in_specs=[pl.BlockSp...  8.93 us
  transfers between devices with their start and end apart: 47, of which 16 were waited for; matrix products, arithmetic and copies ran while one was open for 6% of the time, Pallas kernels for 38%

profile of v6, /device:TPU:12, one launch (start us, length us, event | category | flops | bytes accessed | tf_op | source)
XLA Modules:
  0.0 242.9 jit_solution(17750892427624773346)
XLA Ops:
  9.5 8.9 %hidden.1.h_own = bf16[768,5120]{1,0:T(8,128)(2,1)} custom-call(bf16[1,768,5120]{2,1,0:T(8,128)(2,1)} %latent, f32[1,5120]{1,0:T(1,128)} %bitcast.11), custom_call_target="tpu_custom_call" | custom-call | flops 15000000512 | bytes 1024 | tf_op jit(solution)/shard_map/hidden/pallas_call | solution.py:121
  20.0 3.5 %packs.1 = (bf16[1280,384]{1,0:T(8,128)(2,1)}, bf16[1280,384]{1,0:T(8,128)(2,1)}, bf16[768,640]{1,0:T(8,128)(2,1)}, bf16[768,640]{1,0:T(8,128)(2,1)}) custom-call(bf16[1280,768]{1,0:T(8,128)(2,1)} %wq.5, bf16[1280,768]{1,0:T(8,128)(2,1)} %wk.5, bf16[1280,768]{1,0:T(8,128)(2,1)} %wv.5, bf16[1280,768]{1,0:T(8,128)(2,1)} %copy-done.1, ...), custom_call_target="tpu_custom_call" | custom-call | flops 3000000000 | bytes 1024 | tf_op jit(solution)/shard_map/packs/pallas_call | solution.py:225
  23.5 6.1 %collective-permute-done.1.refs_1_ = bf16[640,384]{1,0:T(8,128)(2,1)S(1)} collective-permute-done((bf16[640,384]{1,0:T(8,128)(2,1)S(1)}, bf16[640,384]{1,0:T(8,128)(2,1)S(1)}, u32[]{:S(2)}, u32[]{:S(2)}) %collective-permute-start.1) | collective-permute-done | bytes 491552 | tf_op jit(solution)/shard_map/ppermute | solution.py:581
  34.2 3.3 %collective-permute-start.8 = (bf16[640,384]{1,0:T(8,128)(2,1)S(1)}, bf16[640,384]{1,0:T(8,128)(2,1)S(1)}, u32[]{:S(2)}, u32[]{:S(2)}) collective-permute-start(bf16[640,384]{1,0:T(8,128)(2,1)S(1)} %collective-permute-done.refs_0_), channel_id=1, source_target_pairs={{0,16},{16,0},{1,17},{17,1},{2,18},{18,2},{3,19},{19,3},{4,20},{20... | collective-permute-start | bytes 1474568 | tf_op jit(solution)/shard_map/ppermute | solution.py:581
  37.6 5.8 %collective-permute-done.10.h_par = bf16[768,5120]{1,0:T(8,128)(2,1)} collective-permute-done((bf16[768,5120]{1,0:T(8,128)(2,1)}, bf16[768,5120]{1,0:T(8,128)(2,1)}, u32[]{:S(2)}, u32[]{:S(2)}) %collective-permute-start.10) | collective-permute-done | bytes 7864352 | tf_op jit(solution)/shard_map/ppermute | solution.py:581
  44.3 17.9 %near.1.acc = f32[3,2,768,384]{3,2,1,0:T(8,128)} custom-call(bf16[768,5120]{1,0:T(8,128)(2,1)} %hidden.1.h_own, bf16[768,5120]{1,0:T(8,128)(2,1)} %collective-permute-done.10.h_par, bf16[1280,768]{1,0:T(8,128)(2,1)} %wq.5, bf16[1280,768]{1,0:T(8,128)(2,1)} %wk.5, bf16[1280,768]{1,0:T(8,128)(2,1)} %wv.5, bf16[1280,768]{1,0:T(8,128)(2,1)} %copy-done.1, ...), custom_call_target="tpu_custom_call" | custom-call | flops 30000001024 | bytes 1024 | tf_op jit(solution)/shard_map/near/pallas_call | solution.py:282
  63.5 3.3 %collective-permute-start.16 = (bf16[1280,384]{1,0:T(8,128)(2,1)S(1)}, bf16[1280,384]{1,0:T(8,128)(2,1)S(1)}, u32[]{:S(2)}, u32[]{:S(2)}) collective-permute-start(bf16[1280,384]{1,0:T(8,128)(2,1)S(1)} %collective-permute-done.7.refs_0_), channel_id=1, source_target_pairs={{0,16},{16,0},{1,17},{17,1},{2,18},{18,2},{3,19},{19,3},{4,20},{20... | collective-permute-start | bytes 2949128 | tf_op jit(solution)/shard_map/ppermute | solution.py:581
  66.8 12.2 %attend.3.refs_0_ = bf16[2,768,128]{2,1,0:T(8,128)(2,1)} custom-call(bf16[768,5120]{1,0:T(8,128)(2,1)} %hidden.1.h_own, bf16[768,5120]{1,0:T(8,128)(2,1)} %collective-permute-done.10.h_par, f32[3,2,768,384]{3,2,1,0:T(8,128)} %near.1.acc, f32[1,768]{1,0:T(1,128)} %reshape.31.qg, f32[1,768]{1,0:T(1,128)} %reshape.32.kg, bf16[640,384]{1,0:T(8,128)(2,1)} %copy-done.19, ...), custom_call_target="tpu_custom_call" | custom-call | flops 35999997952 | bytes 1024 | tf_op jit(solution)/shard_map/attend/pallas_call | solution.py:360
  80.8 3.7 %collective-permute-start.19 = (bf16[2,768,128]{2,1,0:T(8,128)(2,1)}, bf16[2,768,128]{2,1,0:T(8,128)(2,1)}, u32[]{:S(2)}, u32[]{:S(2)}) collective-permute-start(bf16[2,768,128]{2,1,0:T(8,128)(2,1)} %attend.3.refs_0_), channel_id=1, source_target_pairs={{1,2},{2,1},{5,6},{6,5},{9,10},{10,9},{13,14},{14,13},{17,18},{18,... | collective-permute-start | bytes 1179656 | tf_op jit(solution)/shard_map/ppermute | solution.py:596
  92.8 12.2 %attend.4.refs_0_ = bf16[2,768,128]{2,1,0:T(8,128)(2,1)} custom-call(bf16[768,5120]{1,0:T(8,128)(2,1)} %hidden.1.h_own, bf16[768,5120]{1,0:T(8,128)(2,1)} %collective-permute-done.10.h_par, f32[3,2,768,384]{3,2,1,0:T(8,128)} %near.1.acc, f32[1,768]{1,0:T(1,128)} %reshape.31.qg, f32[1,768]{1,0:T(1,128)} %reshape.32.kg, bf16[1280,384]{1,0:T(8,128)(2,1)} %copy-done.15, ...), custom_call_target="tpu_custom_call" | custom-call | flops 35999997952 | bytes 1024 | tf_op jit(solution)/shard_map/attend/pallas_call | solution.py:360
  105.1 3.5 %collective-permute-start.21 = (bf16[2,768,128]{2,1,0:T(8,128)(2,1)S(1)}, bf16[2,768,128]{2,1,0:T(8,128)(2,1)}, u32[]{:S(2)}, u32[]{:S(2)}) collective-permute-start(bf16[2,768,128]{2,1,0:T(8,128)(2,1)S(1)} %collective-permute-done.20.refs_2_), channel_id=1, source_target_pairs={{1,0},{2,3},{5,4},{6,7},{9,8},{10,11},{13,12},{14,15},{17,16},{18,... | collective-permute-start | bytes 1179656 | tf_op jit(solution)/shard_map/ppermute | solution.py:599
  111.1 4.5 %collective-permute-done.14 = bf16[768,640]{1,0:T(8,128)(2,1)} collective-permute-done((bf16[768,640]{1,0:T(8,128)(2,1)S(1)}, bf16[768,640]{1,0:T(8,128)(2,1)}, u32[]{:S(2)}, u32[]{:S(2)}) %collective-permute-start.14) | collective-permute-done | bytes 983072 | tf_op jit(solution)/shard_map/ppermute | solution.py:606
  118.4 6.3 %collective-permute-start.24 = (bf16[2,768,128]{2,1,0:T(8,128)(2,1)}, bf16[2,768,128]{2,1,0:T(8,128)(2,1)}, u32[]{:S(2)}, u32[]{:S(2)}) collective-permute-start(bf16[2,768,128]{2,1,0:T(8,128)(2,1)} %attend.4.refs_0_), channel_id=1, source_target_pairs={{1,2},{2,1},{5,6},{6,5},{9,10},{10,9},{13,14},{14,13},{17,18},{18,... | collective-permute-start | bytes 1179656 | tf_op jit(solution)/shard_map/ppermute | solution.py:596
  127.9 12.2 %attend.5.refs_4_ = bf16[2,768,128]{2,1,0:T(8,128)(2,1)} custom-call(bf16[768,5120]{1,0:T(8,128)(2,1)} %hidden.1.h_own, bf16[768,5120]{1,0:T(8,128)(2,1)} %collective-permute-done.10.h_par, f32[3,2,768,384]{3,2,1,0:T(8,128)} %near.1.acc, f32[1,768]{1,0:T(1,128)} %reshape.31.qg, f32[1,768]{1,0:T(1,128)} %reshape.32.kg, ...), custom_call_target="tpu_custom_call" | custom-call | flops 35999997952 | bytes 1024 | tf_op jit(solution)/shard_map/attend/pallas_call | solution.py:360
  143.8 3.2 %collective-permute-done.26.refs_4_ = bf16[2,768,128]{2,1,0:T(8,128)(2,1)S(1)} collective-permute-done((bf16[2,768,128]{2,1,0:T(8,128)(2,1)}, bf16[2,768,128]{2,1,0:T(8,128)(2,1)S(1)}, u32[]{:S(2)}, u32[]{:S(2)}) %collective-permute-start.26) | collective-permute-done | bytes 393248 | tf_op jit(solution)/shard_map/ppermute | solution.py:599
  157.8 8.1 %collective-permute-done.27.refs_6_ = bf16[2,768,128]{2,1,0:T(8,128)(2,1)} collective-permute-done((bf16[2,768,128]{2,1,0:T(8,128)(2,1)S(1)}, bf16[2,768,128]{2,1,0:T(8,128)(2,1)}, u32[]{:S(2)}, u32[]{:S(2)}) %collective-permute-start.27) | collective-permute-done | bytes 393248 | tf_op jit(solution)/shard_map/ppermute | solution.py:581
  171.4 3.3 %collective-permute-start.32 = (bf16[2,768,128]{2,1,0:T(8,128)(2,1)S(1)}, bf16[2,768,128]{2,1,0:T(8,128)(2,1)S(1)}, u32[]{:S(2)}, u32[]{:S(2)}) collective-permute-start(bf16[2,768,128]{2,1,0:T(8,128)(2,1)S(1)} %copy-done.28), channel_id=1, source_target_pairs={{1,2},{2,1},{5,6},{6,5},{9,10},{10,9},{13,14},{14,13},{17,18},{18,... | collective-permute-start | bytes 1179656 | tf_op jit(solution)/shard_map/ppermute | solution.py:596
  177.2 7.6 %collective-permute-done.32 = bf16[2,768,128]{2,1,0:T(8,128)(2,1)S(1)} collective-permute-done((bf16[2,768,128]{2,1,0:T(8,128)(2,1)S(1)}, bf16[2,768,128]{2,1,0:T(8,128)(2,1)S(1)}, u32[]{:S(2)}, u32[]{:S(2)}) %collective-permute-start.32) | collective-permute-done | bytes 393248 | tf_op jit(solution)/shard_map/ppermute | solution.py:596
  190.4 8.9 %out_projection.2 = (f32[2,384,640]{2,1,0:T(8,128)}, bf16[384,640]{1,0:T(8,128)(2,1)}) custom-call(f32[1,640]{1,0:T(1,128)} %reshape.33.gate_own, f32[1,640]{1,0:T(1,128)} %reshape.34.gate_par, bf16[4,2,768,128]{3,2,1,0:T(8,128)(2,1)} %bundle.2.refs_0_, bf16[4,2,768,128]{3,2,1,0:T(8,128)(2,1)} %bundle.3.refs_1_, ...), custom_call_target="tpu_custom_call" | custom-call | flops 35999997952 | bytes 1024 | tf_op jit(solution)/shard_map/out_projection/pallas_call | solution.py:462
  200.6 9.2 %out_projection.3 = (f32[2,384,640]{2,1,0:T(8,128)}, bf16[384,640]{1,0:T(8,128)(2,1)}) custom-call(f32[1,640]{1,0:T(1,128)} %reshape.33.gate_own, f32[1,640]{1,0:T(1,128)} %reshape.34.gate_par, bf16[4,2,768,128]{3,2,1,0:T(8,128)(2,1)} %bundle.2.refs_0_, bf16[4,2,768,128]{3,2,1,0:T(8,128)(2,1)} %bundle.3.refs_1_, ...), custom_call_target="tpu_custom_call" | custom-call | flops 35999997952 | bytes 1024 | tf_op jit(solution)/shard_map/out_projection/pallas_call | solution.py:462
  211.2 4.2 %collective-permute-done.40.carry = bf16[384,640]{1,0:T(8,128)(2,1)S(1)} collective-permute-done((bf16[384,640]{1,0:T(8,128)(2,1)}, bf16[384,640]{1,0:T(8,128)(2,1)S(1)}, u32[]{:S(2)}, u32[]{:S(2)}) %collective-permute-start.40) | collective-permute-done | bytes 491552 | tf_op jit(solution)/shard_map/ppermute | solution.py:690
  216.2 3.4 %close.2 = (f32[384,640]{1,0:T(8,128)}, f32[384,640]{1,0:T(8,128)}, f32[2,640]{1,0:T(2,128)}) custom-call(f32[2,384,640]{2,1,0:T(8,128)} %get-tuple-element.178.terms, bf16[384,640]{1,0:T(8,128)(2,1)} %copy-done.25, bf16[768,640]{1,0:T(8,128)(2,1)} %copy-done.11, bf16[768,640]{1,0:T(8,128)(2,1)} %get-tuple-element.155.own, bf16[768,640]{1,0:T(8,128)(2,1)} %copy-done.2), custom_call_target="tpu_custom_call" | custom-call | flops 24000000000 | bytes 1024 | tf_op jit(solution)/shard_map/close/pallas_call | solution.py:510
  219.5 6.4 %collective-permute-done.39.carry = bf16[384,640]{1,0:T(8,128)(2,1)S(1)} collective-permute-done((bf16[384,640]{1,0:T(8,128)(2,1)}, bf16[384,640]{1,0:T(8,128)(2,1)S(1)}, u32[]{:S(2)}, u32[]{:S(2)}) %collective-permute-start.39) | collective-permute-done | bytes 491552 | tf_op jit(solution)/shard_map/ppermute | solution.py:690
  226.7 3.3 %close.3 = (f32[384,640]{1,0:T(8,128)}, f32[384,640]{1,0:T(8,128)}, f32[2,640]{1,0:T(2,128)}) custom-call(f32[2,384,640]{2,1,0:T(8,128)} %get-tuple-element.186.terms, bf16[384,640]{1,0:T(8,128)(2,1)} %copy-done.26, bf16[768,640]{1,0:T(8,128)(2,1)} %copy-done.11, bf16[768,640]{1,0:T(8,128)(2,1)} %get-tuple-element.155.own, bf16[768,640]{1,0:T(8,128)(2,1)} %copy-done.2), custom_call_target="tpu_custom_call" | custom-call | flops 24000000000 | bytes 1024 | tf_op jit(solution)/shard_map/close/pallas_call | solution.py:510
  (167 shorter events, 77.6 us)
Async XLA Ops:
  0.7 18.5 %collective-permute-start.3 = (bf16[1280,768]{1,0:T(8,128)(2,1)}, bf16[1280,768]{1,0:T(8,128)(2,1)}, u32[]{:S(2)}, u32[]{:S(2)}) collective-permute-start(bf16[1280,768]{1,0:T(8,128)(2,1)} %wk.5), channel_id=1, source_target_pairs={{0,4},{4,0},{8,12},{12,8},{1,5},{5,1},{9,13},{13,9},{2,6},{6,2},{1... | collective-permute-start | bytes 5898248 | tf_op jit(solution)/shard_map/ppermute | solution.py:581
  1.2 18.8 %collective-permute-start.4 = (bf16[1280,768]{1,0:T(8,128)(2,1)}, bf16[1280,768]{1,0:T(8,128)(2,1)}, u32[]{:S(2)}, u32[]{:S(2)}) collective-permute-start(bf16[1280,768]{1,0:T(8,128)(2,1)} %wv.5), channel_id=1, source_target_pairs={{0,4},{4,0},{8,12},{12,8},{1,5},{5,1},{9,13},{13,9},{2,6},{6,2},{1... | collective-permute-start | bytes 5898248 | tf_op jit(solution)/shard_map/ppermute | solution.py:581
  6.2 23.3 %collective-permute-start.5 = (bf16[768,640]{1,0:T(8,128)(2,1)S(1)}, bf16[768,640]{1,0:T(8,128)(2,1)S(1)}, u32[]{:S(2)}, u32[]{:S(2)}) collective-permute-start(bf16[768,640]{1,0:T(8,128)(2,1)S(1)} %get-tuple-element.198), channel_id=1, source_target_pairs={{0,4},{4,0},{8,12},{12,8},{1,5},{5,1},{9,13},{13,9},{2,6},{6,2},{1... | collective-permute-start | bytes 2949128 | tf_op jit(solution)/shard_map/ppermute | solution.py:581
  8.5 21.0 %collective-permute-start.1 = (bf16[640,384]{1,0:T(8,128)(2,1)S(1)}, bf16[640,384]{1,0:T(8,128)(2,1)S(1)}, u32[]{:S(2)}, u32[]{:S(2)}) collective-permute-start(bf16[640,384]{1,0:T(8,128)(2,1)S(1)} %copy-done.20), channel_id=1, source_target_pairs={{0,12},{4,8},{8,4},{12,0},{1,13},{5,9},{9,5},{13,1},{2,14},{6,10},... | collective-permute-start | bytes 1474568 | tf_op jit(solution)/shard_map/ppermute | solution.py:581
  32.2 30.1 %collective-permute-start.11 = (bf16[768,640]{1,0:T(8,128)(2,1)}, bf16[768,640]{1,0:T(8,128)(2,1)S(1)}, u32[]{:S(2)}, u32[]{:S(2)}) collective-permute-start(bf16[768,640]{1,0:T(8,128)(2,1)} %get-tuple-element.115), channel_id=1, source_target_pairs={{0,0},{17,16},{2,4},{19,20},{4,1},{21,17},{6,5},{23,21},{8,10},{25... | collective-permute-start | bytes 2949128 | tf_op jit(solution)/shard_map/ppermute | solution.py:614
  33.1 29.2 %collective-permute-start.7 = (bf16[1280,384]{1,0:T(8,128)(2,1)}, bf16[1280,384]{1,0:T(8,128)(2,1)S(1)}, u32[]{:S(2)}, u32[]{:S(2)}) collective-permute-start(bf16[1280,384]{1,0:T(8,128)(2,1)} %get-tuple-element.111), channel_id=1, source_target_pairs={{0,8},{4,12},{8,0},{12,4},{1,9},{5,13},{9,1},{13,5},{2,10},{6,14},... | collective-permute-start | bytes 2949128 | tf_op jit(solution)/shard_map/ppermute | solution.py:581
  34.2 28.0 %collective-permute-start.8 = (bf16[640,384]{1,0:T(8,128)(2,1)S(1)}, bf16[640,384]{1,0:T(8,128)(2,1)S(1)}, u32[]{:S(2)}, u32[]{:S(2)}) collective-permute-start(bf16[640,384]{1,0:T(8,128)(2,1)S(1)} %collective-permute-done.refs_0_), channel_id=1, source_target_pairs={{0,16},{16,0},{1,17},{17,1},{2,18},{18,2},{3,19},{19,3},{4,20},{20... | collective-permute-start | bytes 1474568 | tf_op jit(solution)/shard_map/ppermute | solution.py:581
  37.5 24.7 %collective-permute-start.9 = (bf16[640,384]{1,0:T(8,128)(2,1)}, bf16[640,384]{1,0:T(8,128)(2,1)S(1)}, u32[]{:S(2)}, u32[]{:S(2)}) collective-permute-start(bf16[640,384]{1,0:T(8,128)(2,1)} %copy-done.21), channel_id=1, source_target_pairs={{0,16},{16,0},{1,17},{17,1},{2,18},{18,2},{3,19},{19,3},{4,20},{20... | collective-permute-start | bytes 1474568 | tf_op jit(solution)/shard_map/ppermute | solution.py:581
  43.4 35.6 %collective-permute-start.12 = (bf16[768,640]{1,0:T(8,128)(2,1)}, bf16[768,640]{1,0:T(8,128)(2,1)S(1)}, u32[]{:S(2)}, u32[]{:S(2)}) collective-permute-start(bf16[768,640]{1,0:T(8,128)(2,1)} %get-tuple-element.122), channel_id=1, source_target_pairs={{0,4},{17,20},{2,0},{19,16},{4,5},{21,21},{6,1},{23,17},{8,14},{25... | collective-permute-start | bytes 2949128 | tf_op jit(solution)/shard_map/ppermute | solution.py:614
  62.3 26.7 %collective-permute-start.15 = (bf16[1280,384]{1,0:T(8,128)(2,1)S(1)}, bf16[1280,384]{1,0:T(8,128)(2,1)}, u32[]{:S(2)}, u32[]{:S(2)}) collective-permute-start(bf16[1280,384]{1,0:T(8,128)(2,1)S(1)} %copy-done.13), channel_id=1, source_target_pairs={{0,8},{4,12},{8,0},{12,4},{1,9},{5,13},{9,1},{13,5},{2,10},{6,14},... | collective-permute-start | bytes 2949128 | tf_op jit(solution)/shard_map/ppermute | solution.py:581
  63.5 27.0 %collective-permute-start.16 = (bf16[1280,384]{1,0:T(8,128)(2,1)S(1)}, bf16[1280,384]{1,0:T(8,128)(2,1)S(1)}, u32[]{:S(2)}, u32[]{:S(2)}) collective-permute-start(bf16[1280,384]{1,0:T(8,128)(2,1)S(1)} %collective-permute-done.7.refs_0_), channel_id=1, source_target_pairs={{0,16},{16,0},{1,17},{17,1},{2,18},{18,2},{3,19},{19,3},{4,20},{20... | collective-permute-start | bytes 2949128 | tf_op jit(solution)/shard_map/ppermute | solution.py:581
  79.0 26.1 %collective-permute-start.20 = (bf16[2,768,128]{2,1,0:T(8,128)(2,1)}, bf16[2,768,128]{2,1,0:T(8,128)(2,1)S(1)}, u32[]{:S(2)}, u32[]{:S(2)}) collective-permute-start(bf16[2,768,128]{2,1,0:T(8,128)(2,1)} %attend.3.refs_0_), channel_id=1, source_target_pairs={{0,2},{1,3},{2,0},{3,1},{4,6},{5,7},{6,4},{7,5},{8,10},{9,11},{10,... | collective-permute-start | bytes 1179656 | tf_op jit(solution)/shard_map/ppermute | solution.py:581
  80.8 27.8 %collective-permute-start.18 = (bf16[2,768,128]{2,1,0:T(8,128)(2,1)}, bf16[2,768,128]{2,1,0:T(8,128)(2,1)}, u32[]{:S(2)}, u32[]{:S(2)}) collective-permute-start(bf16[2,768,128]{2,1,0:T(8,128)(2,1)} %attend.3.refs_0_), channel_id=1, source_target_pairs={{0,1},{1,0},{2,3},{3,2},{4,5},{5,4},{6,7},{7,6},{8,9},{9,8},{10,11... | collective-permute-start | bytes 1179656 | tf_op jit(solution)/shard_map/ppermute | solution.py:581
  80.8 29.1 %collective-permute-start.19 = (bf16[2,768,128]{2,1,0:T(8,128)(2,1)}, bf16[2,768,128]{2,1,0:T(8,128)(2,1)}, u32[]{:S(2)}, u32[]{:S(2)}) collective-permute-start(bf16[2,768,128]{2,1,0:T(8,128)(2,1)} %attend.3.refs_0_), channel_id=1, source_target_pairs={{1,2},{2,1},{5,6},{6,5},{9,10},{10,9},{13,14},{14,13},{17,18},{18,... | collective-permute-start | bytes 1179656 | tf_op jit(solution)/shard_map/ppermute | solution.py:596
  89.0 26.6 %collective-permute-start.14 = (bf16[768,640]{1,0:T(8,128)(2,1)S(1)}, bf16[768,640]{1,0:T(8,128)(2,1)}, u32[]{:S(2)}, u32[]{:S(2)}) collective-permute-start(bf16[768,640]{1,0:T(8,128)(2,1)S(1)} %collective-permute-done.11), channel_id=1, source_target_pairs={{0,8},{1,9},{4,12},{5,13},{10,2},{11,3},{14,6},{15,7},{16,24},{17,... | collective-permute-start | bytes 2949128 | tf_op jit(solution)/shard_map/ppermute | solution.py:606
  90.5 34.2 %collective-permute-start.17 = (bf16[1280,384]{1,0:T(8,128)(2,1)}, bf16[1280,384]{1,0:T(8,128)(2,1)}, u32[]{:S(2)}, u32[]{:S(2)}) collective-permute-start(bf16[1280,384]{1,0:T(8,128)(2,1)} %collective-permute-done.15.refs_0_), channel_id=1, source_target_pairs={{0,16},{16,0},{1,17},{17,1},{2,18},{18,2},{3,19},{19,3},{4,20},{20... | collective-permute-start | bytes 2949128 | tf_op jit(solution)/shard_map/ppermute | solution.py:581
  108.6 35.2 %collective-permute-start.13 = (bf16[768,640]{1,0:T(8,128)(2,1)S(1)}, bf16[768,640]{1,0:T(8,128)(2,1)}, u32[]{:S(2)}, u32[]{:S(2)}) collective-permute-start(bf16[768,640]{1,0:T(8,128)(2,1)S(1)} %collective-permute-done.12), channel_id=1, source_target_pairs={{0,8},{1,9},{4,12},{5,13},{10,2},{11,3},{14,6},{15,7},{16,24},{17,... | collective-permute-start | bytes 2949128 | tf_op jit(solution)/shard_map/ppermute | solution.py:606
  109.9 30.2 %collective-permute-start.25 = (bf16[2,768,128]{2,1,0:T(8,128)(2,1)}, bf16[2,768,128]{2,1,0:T(8,128)(2,1)}, u32[]{:S(2)}, u32[]{:S(2)}) collective-permute-start(bf16[2,768,128]{2,1,0:T(8,128)(2,1)} %attend.4.refs_0_), channel_id=1, source_target_pairs={{0,2},{1,3},{2,0},{3,1},{4,6},{5,7},{6,4},{7,5},{8,10},{9,11},{10,... | collective-permute-start | bytes 1179656 | tf_op jit(solution)/shard_map/ppermute | solution.py:581
  115.6 28.2 %collective-permute-start.23 = (bf16[2,768,128]{2,1,0:T(8,128)(2,1)}, bf16[2,768,128]{2,1,0:T(8,128)(2,1)}, u32[]{:S(2)}, u32[]{:S(2)}) collective-permute-start(bf16[2,768,128]{2,1,0:T(8,128)(2,1)} %attend.4.refs_0_), channel_id=1, source_target_pairs={{0,1},{1,0},{2,3},{3,2},{4,5},{5,4},{6,7},{7,6},{8,9},{9,8},{10,11... | collective-permute-start | bytes 1179656 | tf_op jit(solution)/shard_map/ppermute | solution.py:581
  118.4 25.4 %collective-permute-start.24 = (bf16[2,768,128]{2,1,0:T(8,128)(2,1)}, bf16[2,768,128]{2,1,0:T(8,128)(2,1)}, u32[]{:S(2)}, u32[]{:S(2)}) collective-permute-start(bf16[2,768,128]{2,1,0:T(8,128)(2,1)} %attend.4.refs_0_), channel_id=1, source_target_pairs={{1,2},{2,1},{5,6},{6,5},{9,10},{10,9},{13,14},{14,13},{17,18},{18,... | collective-permute-start | bytes 1179656 | tf_op jit(solution)/shard_map/ppermute | solution.py:596
  127.0 20.0 %collective-permute-start.22 = (bf16[768,640]{1,0:T(8,128)(2,1)}, bf16[768,640]{1,0:T(8,128)(2,1)S(1)}, u32[]{:S(2)}, u32[]{:S(2)}) collective-permute-start(bf16[768,640]{1,0:T(8,128)(2,1)} %broadcast_select_fusion.2.refs_12_), channel_id=1, source_target_pairs={{0,16},{16,0},{1,17},{17,1},{2,18},{18,2},{3,19},{19,3},{4,20},{20... | collective-permute-start | bytes 2949128 | tf_op jit(solution)/shard_map/ppermute | solution.py:581
  148.9 22.4 %collective-permute-start.30 = (bf16[768,640]{1,0:T(8,128)(2,1)S(1)}, bf16[768,640]{1,0:T(8,128)(2,1)S(1)}, u32[]{:S(2)}, u32[]{:S(2)}) collective-permute-start(bf16[768,640]{1,0:T(8,128)(2,1)S(1)} %broadcast_select_fusion), channel_id=1, source_target_pairs={{0,8},{4,12},{1,9},{5,13},{2,10},{6,14},{3,11},{7,15},{16,24},{20,... | collective-permute-start | bytes 2949128 | tf_op jit(solution)/shard_map/ppermute | solution.py:672
  151.7 19.7 %collective-permute-start.29 = (bf16[768,640]{1,0:T(8,128)(2,1)S(1)}, bf16[768,640]{1,0:T(8,128)(2,1)S(1)}, u32[]{:S(2)}, u32[]{:S(2)}) collective-permute-start(bf16[768,640]{1,0:T(8,128)(2,1)S(1)} %broadcast_select_fusion.1.refs_14_), channel_id=1, source_target_pairs={{0,16},{16,0},{1,17},{17,1},{2,18},{18,2},{3,19},{19,3},{4,20},{20... | collective-permute-start | bytes 2949128 | tf_op jit(solution)/shard_map/ppermute | solution.py:581
  155.5 32.3 %collective-permute-start.33 = (bf16[4,2,768,128]{3,2,1,0:T(8,128)(2,1)S(1)}, bf16[4,2,768,128]{3,2,1,0:T(8,128)(2,1)}, u32[]{:S(2)}, u32[]{:S(2)}) collective-permute-start(bf16[4,2,768,128]{3,2,1,0:T(8,128)(2,1)S(1)} %copy-done.10), channel_id=1, source_target_pairs={{0,4},{4,0},{8,12},{12,8},{1,5},{5,1},{9,13},{13,9},{2,6},{6,2},{1... | collective-permute-start | bytes 4718600 | tf_op jit(solution)/shard_map/ppermute | solution.py:581
  (55 other events, 600.0 us)
